TPU v7x, 128 devices: a whole 4x4x4 slice. The times are simulated.
128 devices in a mesh: brick: 32 (over y, x, core), pool: 4 (over z).
Axes of the slice: x: 4, y: 4, z: 4, core: 2. Of those that a mesh axis runs over, the one named last changes fastest.
Arguments:
- displacement: float32 [3, 1179648], P(None, ('brick', 'pool')), may hold values from -6 to 6
- node_map: int32 [8, 1048576], P(None, ('brick', 'pool')), may hold values from 0 to 9215
- shape_grads: float32 [3, 8, 1048576], P(None, None, ('brick', 'pool')), may hold values from -2 to 2
- volumes: float32 [1048576], P(('brick', 'pool')), may hold values from 0.5 to 2
- elastic_moduli: float32 [2, 1048576], P(None, ('brick', 'pool')), may hold values from 1 to 10
- external_force: float32 [3, 1179648], P(None, ('brick', 'pool')), may hold values from -64 to 64
- nodal_mass: float32 [1179648], P(('brick', 'pool')), may hold values from 10 to 40
- shared_nodes: int32 [128, 4, 1024], P(('brick', 'pool')), may hold values from 0 to 9215, as said below
- band_count: int32 [128], P(('brick', 'pool')), may hold values from 1 to 4, as said below
- band_owner: int32 [128, 4], P(('brick', 'pool')), may hold values from -1 to 127, as said below
- band_element: int32 [128, 4], P(('brick', 'pool')), may hold values from 0 to 8191, as said below
- micro_fields: float32 [512, 8, 4096], P(('brick', 'pool')), may hold values from -5 to 10, as said below
Outputs:
- acceleration: float32 [3, 1179648], P(None, ('brick', 'pool'))
- band_stress: float32 [6, 512], P(None, ('brick', 'pool'))
- owned_fields: float32 [256, 8, 4096], P(('brick', 'pool'))
Inputs may be any that keep to these rules, and one draw needn't show every extreme that they name: `band_count`: they sum to 256. `band_owner`: -1 exactly on slots k >= band_count[d]. The live slots of all blocks, block by block in order, take consecutive ordinals m = t, t + 1, ... for some start t; the slot with ordinal m is owned by device pi((m // 4) % 32) * 4 + m % 4 for a permutation pi of the brick indices. So every device owns exactly 2 live slots and no two live slots of one block share an owner. `band_element`: the entries of one block's row are different. `shared_nodes`: the 4096 entries of one block are different. `micro_fields`: channels 6 and 7 lie between 1 and 10, channels 0 to 5 between -5 and 5.
All inputs are finite; a program needn't handle non-finite values.
Results may differ from a plain program's by a relative error of at most 0.0001.
Values sent between devices are 32-bit elements; how exact they have to be, the bound alone decides.
No kernel may reach another device: no remote copies, remote signals or barrier semaphores. Data moves between devices by JAX's collectives and lax.ppermute only.
A program may use at most 192 MiB of HBM per device.

v0:
```python
import math

import jax
import jax.numpy as jnp
from jax import lax
from jax.sharding import PartitionSpec as P

P_DEV = 2
G = 16
NV = 4096
ITERS = 2


ref_lambda = 5.5
ref_shear = 5.5
highest = lax.Precision.HIGHEST


def with_halo(cells, sides, width):
    for axis, dim in sides:
        count = lax.axis_size(axis)
        ends = count - 1
        head = lax.slice_in_dim(cells, 0, width, axis=dim)
        tail = lax.slice_in_dim(cells, cells.shape[dim] - width, cells.shape[dim], axis=dim)
        cells = jnp.concatenate(
            [
                lax.ppermute(tail, axis, [(i, (i + 1) % count) for i in range(ends)]),
                cells,
                lax.ppermute(head, axis, [((i + 1) % count, i) for i in range(ends)]),
            ],
            axis=dim,
        )
    return cells


def wave_of(positions, length_cells):
    return jnp.where(positions * 2 < length_cells, positions, positions - length_cells).astype(
        jnp.float32
    )


def green_apply(tensor_parts, wave_x, wave_y, wave_z):
    tau_xx, tau_yy, tau_zz, tau_yz, tau_xz, tau_xy = tensor_parts
    along_x = tau_xx * wave_x + tau_xy * wave_y + tau_xz * wave_z
    along_y = tau_xy * wave_x + tau_yy * wave_y + tau_yz * wave_z
    along_z = tau_xz * wave_x + tau_yz * wave_y + tau_zz * wave_z
    squared = wave_x * wave_x + wave_y * wave_y + wave_z * wave_z
    nonzero = squared > 0.0
    safe_square = jnp.where(nonzero, squared, 1.0)
    first_term = jnp.where(nonzero, 1.0 / (2.0 * ref_shear * safe_square), 0.0)
    coupling = (ref_lambda + ref_shear) / (ref_shear * (ref_lambda + 2.0 * ref_shear))
    second = jnp.where(nonzero, coupling / (safe_square * safe_square), 0.0)
    normal_part = (along_x * wave_x + along_y * wave_y + along_z * wave_z) * second
    return [
        first_term * (2.0 * wave_x * along_x) - normal_part * wave_x * wave_x,
        first_term * (2.0 * wave_y * along_y) - normal_part * wave_y * wave_y,
        first_term * (2.0 * wave_z * along_z) - normal_part * wave_z * wave_z,
        first_term * (wave_y * along_z + wave_z * along_y) - normal_part * wave_y * wave_z,
        first_term * (wave_x * along_z + wave_z * along_x) - normal_part * wave_x * wave_z,
        first_term * (wave_x * along_y + wave_y * along_x) - normal_part * wave_x * wave_y,
    ]


def cell_stress(strain, lame_first, shear_mod):
    trace_sum = strain[:, 0] + strain[:, 1] + strain[:, 2]
    normal = [lame_first * trace_sum + 2.0 * shear_mod * strain[:, channel] for channel in range(3)]
    shears = [2.0 * shear_mod * strain[:, channel] for channel in range(3, 6)]
    return jnp.stack(normal + shears, axis=1)


def element_strain(displacement, node_map, shape_grads):
    corners = displacement[:, node_map]
    tensor = jnp.einsum("iae,jae->ije", corners, shape_grads, precision=highest)
    return jnp.stack(
        [
            tensor[0, 0],
            tensor[1, 1],
            tensor[2, 2],
            0.5 * (tensor[1, 2] + tensor[2, 1]),
            0.5 * (tensor[0, 2] + tensor[2, 0]),
            0.5 * (tensor[0, 1] + tensor[1, 0]),
        ],
        axis=0,
    )


def macro_stress(strain, moduli):
    trace_sum = strain[0] + strain[1] + strain[2]
    normal = [moduli[0] * trace_sum + 2.0 * moduli[1] * strain[channel] for channel in range(3)]
    shears = [2.0 * moduli[1] * strain[channel] for channel in range(3, 6)]
    return jnp.stack(normal + shears, axis=0)


def element_forces(stress, shape_grads, volumes):
    full = jnp.stack(
        [
            jnp.stack([stress[0], stress[5], stress[4]]),
            jnp.stack([stress[5], stress[1], stress[3]]),
            jnp.stack([stress[4], stress[3], stress[2]]),
        ]
    )
    return jnp.einsum("ije,jae->iae", full, shape_grads, precision=highest) * volumes[None, None, :]


def dft_tables():
    edge = jnp.arange(G, dtype=jnp.int32)
    edge_phase = jnp.mod(edge[:, None] * edge[None, :], G).astype(jnp.float32) * (2.0 * math.pi / G)
    plane = jnp.arange(G * G, dtype=jnp.int32)
    plane_rows = plane // G
    plane_cols = plane % G
    plane_phase = jnp.mod(
        plane_rows[:, None] * plane_rows[None, :] + plane_cols[:, None] * plane_cols[None, :], G
    )
    plane_phase = plane_phase.astype(jnp.float32) * (2.0 * math.pi / G)
    wave_x = wave_of(edge, G)[:, None]
    wave_y = wave_of(plane_rows, G)[None, :]
    wave_z = wave_of(plane_cols, G)[None, :]
    return (
        jnp.cos(edge_phase),
        jnp.sin(edge_phase),
        jnp.cos(plane_phase),
        jnp.sin(plane_phase),
        wave_x,
        wave_y,
        wave_z,
    )


def forward_dft(values, tables):
    cos_edge, sin_edge, cos_plane, sin_plane = (tables[0], tables[1], tables[2], tables[3])
    plane_cos = jnp.einsum("bcxl,lk->bcxk", values, cos_plane, precision=highest)
    plane_sin = -jnp.einsum("bcxl,lk->bcxk", values, sin_plane, precision=highest)
    real_part = jnp.einsum("jx,bcxk->bcjk", cos_edge, plane_cos, precision=highest) + jnp.einsum(
        "jx,bcxk->bcjk", sin_edge, plane_sin, precision=highest
    )
    imag_part = jnp.einsum("jx,bcxk->bcjk", cos_edge, plane_sin, precision=highest) - jnp.einsum(
        "jx,bcxk->bcjk", sin_edge, plane_cos, precision=highest
    )
    return (real_part, imag_part)


def inverse_dft(real_part, imag_part, tables):
    cos_edge, sin_edge, cos_plane, sin_plane = (tables[0], tables[1], tables[2], tables[3])
    edge_real = jnp.einsum("jx,bcxk->bcjk", cos_edge, real_part, precision=highest) - jnp.einsum(
        "jx,bcxk->bcjk", sin_edge, imag_part, precision=highest
    )
    edge_imag = jnp.einsum("jx,bcxk->bcjk", cos_edge, imag_part, precision=highest) + jnp.einsum(
        "jx,bcxk->bcjk", sin_edge, real_part, precision=highest
    )
    result = jnp.einsum("bcxl,lk->bcxk", edge_real, cos_plane, precision=highest) - jnp.einsum(
        "bcxl,lk->bcxk", edge_imag, sin_plane, precision=highest
    )
    return result / NV


def cell_iterate(fields, macro, tables):
    members = fields.shape[0]
    wave_x, wave_y, wave_z = (tables[4], tables[5], tables[6])
    strain = fields[:, :6].reshape(members, 6, G, G * G)
    lame_first = fields[:, 6].reshape(members, G, G * G)
    shear_mod = fields[:, 7].reshape(members, G, G * G)
    target = macro[:, :, None, None]
    for iteration in range(ITERS):
        real_part, imag_part = forward_dft(cell_stress(strain, lame_first, shear_mod), tables)
        real_out = jnp.stack(
            green_apply([real_part[:, channel] for channel in range(6)], wave_x, wave_y, wave_z),
            axis=1,
        )
        imag_out = jnp.stack(
            green_apply([imag_part[:, channel] for channel in range(6)], wave_x, wave_y, wave_z),
            axis=1,
        )
        update = inverse_dft(real_out, imag_out, tables)
        average = jnp.mean(strain, axis=(2, 3), keepdims=True)
        strain = strain - update + (target - average)
    final = cell_stress(strain, lame_first, shear_mod)
    homogenized = jnp.mean(final, axis=(2, 3))
    return (jnp.concatenate([strain.reshape(members, 6, NV), fields[:, 6:]], axis=1), homogenized)


def solve_cells(fields, macro):
    members = fields.shape[0]
    tables = dft_tables()

    def one_block(block_pair):
        return cell_iterate(block_pair[0], block_pair[1], tables)

    grouped = (
        fields.reshape(members // members, members, 8, NV),
        macro.reshape(members // members, members, 6),
    )
    new_fields, homogenized = lax.map(one_block, grouped)
    return (new_fields.reshape(members, 8, NV), homogenized.reshape(members, 6))


def arrival_order(flag_column):
    present = flag_column > 0.5
    present_int = present.astype(jnp.int32)
    ranks = jnp.cumsum(present_int) - present_int
    owned_slots = jnp.arange(P_DEV, dtype=jnp.int32)
    hits = (ranks[None, :] == owned_slots[:, None]) & present[None, :]
    sources = jnp.arange(flag_column.shape[0], dtype=jnp.int32)
    return jnp.sum(jnp.where(hits, sources[None, :], 0), axis=1)


def deliver(cells, extras, owners, live):
    pools = lax.axis_size("pool")
    bricks = lax.axis_size("brick")
    devices = bricks * pools
    slot_count = owners.shape[0]
    width = extras.shape[1]
    slot_index = jnp.arange(slot_count, dtype=jnp.int32)
    targets = jnp.arange(devices, dtype=jnp.int32)
    matches = (owners[:, None] == targets[None, :]) & live[:, None]
    sending = jnp.any(matches, axis=0)
    source_slot = jnp.sum(jnp.where(matches, slot_index[:, None], 0), axis=0)
    outbound = jnp.where(sending[:, None, None], cells[source_slot], 0.0)
    tags = jnp.concatenate(
        [
            jnp.where(sending[:, None], extras[source_slot], 0.0),
            sending.astype(jnp.float32)[:, None],
        ],
        axis=1,
    )
    arrived, arrived_tags = (
        lax.all_to_all(outbound, ("brick", "pool"), split_axis=0, concat_axis=0, tiled=True),
        lax.all_to_all(tags, ("brick", "pool"), split_axis=0, concat_axis=0, tiled=True),
    )
    picks = arrival_order(arrived_tags[:, width])
    return (arrived[picks], arrived_tags[picks, :width], picks)


def shards(
    displacement,
    node_map,
    shape_grads,
    volumes,
    elastic_moduli,
    external_force,
    nodal_mass,
    shared_nodes,
    band_count,
    band_owner,
    band_element,
    micro_fields,
):
    slot_count = band_owner.shape[1]
    elements = node_map.shape[1]
    strain = element_strain(displacement, node_map, shape_grads)
    owners = band_owner[0]
    chosen = band_element[0]
    slot_index = jnp.arange(slot_count, dtype=jnp.int32)
    live = slot_index < band_count[0]
    band_strain = strain[:, chosen].T
    updated, homogenized = solve_cells(micro_fields, band_strain)
    owned_fields, unused_tags, unused_blocks = deliver(
        updated, jnp.zeros((slot_count, 0), jnp.float32), owners, live
    )
    band_stress = jnp.where(live[:, None], homogenized, 0.0).T
    stress = macro_stress(strain, elastic_moduli)
    stress = stress.at[:, jnp.where(live, chosen, elements)].set(band_stress, mode="drop")
    forces = element_forces(stress, shape_grads, volumes)
    own_force = jnp.zeros((3, displacement.shape[1]), jnp.float32).at[:, node_map].add(forces)
    face_lists = shared_nodes[0]
    brick_send = jnp.stack([own_force[:, face_lists[0]], own_force[:, face_lists[1]]], axis=1)
    brick_rim = with_halo(brick_send, (("brick", 1),), 1)
    pool_send = jnp.stack([own_force[:, face_lists[2]], own_force[:, face_lists[3]]], axis=1)
    pool_rim = with_halo(pool_send, (("pool", 1),), 1)
    assembled = own_force.at[:, face_lists[0]].add(brick_rim[:, 0])
    assembled = assembled.at[:, face_lists[1]].add(brick_rim[:, 3])
    assembled = assembled.at[:, face_lists[2]].add(pool_rim[:, 0])
    assembled = assembled.at[:, face_lists[3]].add(pool_rim[:, 3])
    acceleration = (external_force - assembled) / nodal_mass[None, :]
    return (acceleration, band_stress, owned_fields)


def solution(mesh):
    placed = (
        P(None, ("brick", "pool")),
        P(None, ("brick", "pool")),
        P(None, None, ("brick", "pool")),
        P(("brick", "pool")),
        P(None, ("brick", "pool")),
        P(None, ("brick", "pool")),
        P(("brick", "pool")),
        P(("brick", "pool"), None, None),
        P(("brick", "pool")),
        P(("brick", "pool"), None),
        P(("brick", "pool"), None),
        P(("brick", "pool"), None, None),
    )
    return jax.shard_map(
        shards,
        mesh=mesh,
        in_specs=placed,
        out_specs=(
            P(None, ("brick", "pool")),
            P(None, ("brick", "pool")),
            P(("brick", "pool"), None, None),
        ),
        check_vma=False,
    )
```

profile of v0, /device:TPU:40, one launch (start us, length us, event | category | flops | bytes accessed | tf_op | source)
XLA Modules:
  0.0 1224.9 jit_solution(4420801537783433653)
XLA Ops:
  2.8 10.2 all-to-all-start.1
  13.0 1.6 multiply_reduce_fusion
  16.2 1.5 convolution_negate_fusion.1
  26.0 3.0 copy.188
  28.9 217.8 %gather_fusion = f32[65536,3]{1,0:T(8,128)} fusion(f32[3,9216]{0,1:T(8,128)} %copy.188, s32[65536]{0:T(1024)S(1)} %broadcast_clamp_fusion), kind=kCustom, calls=%fused_computation | custom fusion | bytes 1835008 | tf_op jit(solution)/shard_map/gather | solution.py:72
  246.8 52.4 %copy.189 = f32[8,8192,3]{0,2,1:T(4,128)} copy(f32[8,8192,3]{2,1,0:T(8,128)} %bitcast.434) | data formatting | bytes 1572864 | tf_op jit(solution)/shard_map/gather | solution.py:72
  299.1 10.6 copy.190
  309.7 60.5 %fusion.2 = f32[3,3,8192]{1,0,2:T(4,128)} fusion(f32[3,8,8192]{1,0,2:T(4,128)} %copy.190, f32[8,8192,3]{0,2,1:T(4,128)} %copy.189), kind=kOutput, calls=%fused_computation.18 | convolution fusion | flops 7077888 | bytes 1867776 | tf_op jit(solution)/shard_map/iae,jae->ije/dot_general | solution.py:73
  370.2 171.9 %fusion.10 = (f32[8192]{0:T(1024)S(1)}, f32[8192]{0:T(1024)S(1)}, f32[8192]{0:T(1024)S(1)}, f32[8192]{0:T(1024)S(1)}, f32[8192]{0:T(1024)S(1)}, /*index=5*/f32[8192]{0:T(1024)S(1)}) fusion(f32[3,3,8192]{1,0,2:T(4,128)} %fusion.2), kind=kLoop, calls=%fused_computation.31 | loop fusion | flops 49152 | bytes 491520 | tf_op jit(solution)/shard_map/mul | solution.py:81
  542.4 2.6 copy.198
  545.0 2.7 gather_fusion.1
  547.8 1.7 fusion.296
  549.7 1.5 fusion.41
  551.2 1.5 convolution_negate_fusion
  560.1 1.7 fusion.26
  562.0 7.4 gather_fusion.6
  569.4 11.9 broadcast_select_fusion
  581.3 10.2 all-to-all-start
  592.1 2.6 copy.213
  595.1 4.7 scatter_custom_fusion
  599.8 20.4 %fusion.295 = (f32[1,8192]{0,1:T(8,128)}, f32[1,8192]{0,1:T(8,128)}, f32[1,8192]{0,1:T(8,128)}, f32[1,8192]{0,1:T(8,128)}, f32[1,8192]{0,1:T(8,128)}, /*index=5*/f32[1,8192]{0,1:T(8,128)}) fusion(f32[6,8192]{0,1:T(8,128)} %scatter_custom_fusion), kind=kLoop, calls=%fused_computation.413 | loop fusion | bytes 393216 | tf_op jit(solution)/shard_map/slice | solution.py:97
  620.2 2.8 copy.214
  623.0 2.8 copy.215
  625.8 2.8 copy.216
  628.7 2.8 copy.218
  631.5 2.8 copy.219
  634.4 2.8 copy.222
  637.6 10.8 copy.223
  648.4 71.9 %multiply_bitcast_fusion = f32[8,8192,3]{0,2,1:T(4,128)} fusion(f32[8192]{0:T(1024)S(1)} %copy-done.5, f32[3,3,8192]{1,0,2:T(4,128)} %copy.223, f32[3,8,8192]{1,0,2:T(4,128)} %copy.190), kind=kOutput, calls=%fused_computation.16 | convolution fusion | flops 7274496 | bytes 1900544 | tf_op jit(solution)/shard_map/ije,jae->iae/dot_general | solution.py:102
  720.3 52.0 %copy.237 = f32[8,8192,3]{2,1,0:T(8,128)} copy(f32[8,8192,3]{0,2,1:T(4,128)} %multiply_bitcast_fusion) | data formatting | bytes 1572864 | tf_op jit(solution)/shard_map/mul | solution.py:102
  772.3 349.9 %scatter_custom_fusion.1 = f32[3,9216]{0,1:T(8,128)} fusion(s32[65536]{0:T(1024)S(1)} %bitcast.458, f32[65536,3]{1,0:T(8,128)} %bitcast.435, f32[]{:T(128)} %constant.123.clone.1), kind=kCustom, calls=%fused_computation.32 | custom fusion | flops 196608 | bytes 111104 | tf_op jit(solution)/shard_map/scatter-add | solution.py:263
  1122.3 6.3 gather_fusion.2
  1128.6 2.0 collective-permute-start
  1130.6 5.1 gather_fusion.3
  1135.8 5.6 collective-permute-start.1
  1141.4 6.3 gather_fusion.4
  1147.8 3.6 collective-permute-start.2
  1151.4 6.3 gather_fusion.5
  1157.7 2.2 collective-permute-start.3
  1159.9 3.0 copy.227
  1163.6 2.4 compare_convert_fusion
  1166.4 9.9 scatter_custom_fusion.2
  1176.3 9.9 scatter_custom_fusion.3
  1186.3 10.1 scatter_custom_fusion.4
  1196.4 9.9 scatter_custom_fusion.5
  1206.3 7.6 subtract_divide_fusion
  1213.9 3.7 copy.232
  1217.7 7.0 gather_fusion.7
  (119 shorter events, 21.2 us)
Async XLA Ops:
  0.6 18.8 %copy-start.9 = (s32[1,4]{1,0:T(1,128)S(1)}, s32[1,4]{1,0:T(1,128)}, u32[]{:S(2)}) copy-start(s32[1,4]{1,0:T(1,128)} %param.21) | copy-start | bytes 52
  2.8 578.5 %all-to-all-start.1 = ((f32[128,1,1]{2,1,0:T(1,128)}), f32[128,1,1]{2,1,0:T(1,128)S(1)}, u32[]{:S(2)}, u32[]{:S(2)}) async-start(f32[128,1,1]{2,1,0:T(1,128)} %copy.230), calls=%async_computation.1 | async-start | bytes 131072 | tf_op jit(solution)/shard_map/all_to_all | solution.py:227
  21.6 4.2 copy-start.1
  21.8 4.1 copy-start.2
  246.8 52.4 %copy-start = (f32[3,8,8192]{2,1,0:T(8,128)S(1)}, f32[3,8,8192]{2,1,0:T(8,128)}, u32[]{:S(2)}) copy-start(f32[3,8,8192]{2,1,0:T(8,128)} %param.14) | copy-start | bytes 2359300
  542.1 2.9 copy-start.8
  581.3 10.2 copy-start.4
  581.3 636.3 %all-to-all-start = ((f32[128,8,4096]{2,1,0:T(8,128)}), f32[128,8,4096]{2,1,0:T(8,128)}, u32[]{:S(2)}, u32[]{:S(2)}) async-start(f32[128,8,4096]{2,1,0:T(8,128)} %broadcast_select_fusion), calls=%async_computation | async-start | bytes 33554432 | tf_op jit(solution)/shard_map/all_to_all | solution.py:226
  637.6 10.8 copy-start.5
  772.3 349.9 %copy-start.7 = (s32[1,4,1024]{2,1,0:T(4,128)S(1)}, s32[1,4,1024]{2,1,0:T(4,128)}, u32[]{:S(2)}) copy-start(s32[1,4,1024]{2,1,0:T(4,128)} %param.19) | copy-start | bytes 49156
  772.3 387.6 %copy-start.3 = (f32[3,9216]{1,0:T(4,128)S(1)}, f32[3,9216]{1,0:T(4,128)}, u32[]{:S(2)}) copy-start(f32[3,9216]{1,0:T(4,128)} %param.17) | copy-start | bytes 331780
  1128.6 37.8 %collective-permute-start = (f32[3,1,1024]{0,2,1:T(8,128)}, f32[3,1,1024]{0,2,1:T(8,128)S(1)}, u32[]{:S(2)}, u32[]{:S(2)}) collective-permute-start(f32[3,1,1024]{0,2,1:T(8,128)} %bitcast.58), channel_id=1, source_target_pairs={{0,4},{4,8},{8,12},{12,16},{16,20},{20,24},{24,28},{28,32},{32,36}... | collective-permute-start | bytes 36872 | tf_op jit(solution)/shard_map/ppermute | solution.py:27
  1135.8 40.5 %collective-permute-start.1 = (f32[3,1,1024]{0,2,1:T(8,128)S(1)}, f32[3,1,1024]{0,2,1:T(8,128)S(1)}, u32[]{:S(2)}, u32[]{:S(2)}) collective-permute-start(f32[3,1,1024]{0,2,1:T(8,128)S(1)} %bitcast.482), channel_id=1, source_target_pairs={{4,0},{8,4},{12,8},{16,12},{20,16},{24,20},{28,24},{32,28},{36,32}... | collective-permute-start | bytes 36872 | tf_op jit(solution)/shard_map/ppermute | solution.py:29
  1147.8 38.5 %collective-permute-start.2 = (f32[3,1,1024]{0,2,1:T(8,128)}, f32[3,1,1024]{0,2,1:T(8,128)S(1)}, u32[]{:S(2)}, u32[]{:S(2)}) collective-permute-start(f32[3,1,1024]{0,2,1:T(8,128)} %bitcast.484), channel_id=1, source_target_pairs={{0,1},{1,2},{2,3},{4,5},{5,6},{6,7},{8,9},{9,10},{10,11},{12,13},{... | collective-permute-start | bytes 36872 | tf_op jit(solution)/shard_map/ppermute | solution.py:27
  1157.7 38.7 %collective-permute-start.3 = (f32[3,1,1024]{0,2,1:T(8,128)}, f32[3,1,1024]{0,2,1:T(8,128)S(1)}, u32[]{:S(2)}, u32[]{:S(2)}) collective-permute-start(f32[3,1,1024]{0,2,1:T(8,128)} %bitcast.483), channel_id=1, source_target_pairs={{1,0},{2,1},{3,2},{5,4},{6,5},{7,6},{9,8},{10,9},{11,10},{13,12},{... | collective-permute-start | bytes 36872 | tf_op jit(solution)/shard_map/ppermute | solution.py:29
  1186.3 20.0 %copy-start.6 = (f32[9216]{0:T(1024)S(1)}, f32[9216]{0:T(1024)}, u32[]{:S(2)}) copy-start(f32[9216]{0:T(1024)} %param.18) | copy-start | bytes 110596
where the time goes:
time: 1230 us; the launch traced here: 1220 us
  other arithmetic  596 us (48%)
  local copies, waits for them, and re-layouts  440 us (36%)
  matrix products  153 us (12%)
  starting transfers between devices  33.9 us (3%)
    scatter-add x1, other arithmetic, shards(): jnp.zeros((3, displacement.shape[1]), jnp.float32).at[:, node_map]  350 us
    gather x2, local copies, waits for them, and re-layouts, element_strain(): corners = displacement[:, node_map]  270 us
    mul x1, other arithmetic, element_strain(): 0.5 * (tensor[0, 1] + tensor[1, 0])  172 us
    dot_general x1, matrix products, element_forces(): jnp.einsum('ije,jae->iae', full, shape_grads, precision=highest)  71.9 us
    dot_general x1, matrix products, element_strain(): tensor = jnp.einsum('iae,jae->ije', corners, shape_grads, precision=highest)  60.5 us
    mul x1, local copies, waits for them, and re-layouts, element_forces(): jnp.einsum('ije,jae->iae', full, shape_grads, precision=highest)  52 us
  transfers between devices with their start and end apart: 6, of which 0 were waited for; matrix products, arithmetic and copies ran while one was open for 96% of the time, Pallas kernels for 0%

commit v1 on v0

v1 whole, which is shorter than its diff:
```python
import math

import jax
import jax.numpy as jnp
import numpy as np
from jax import lax
from jax.experimental import pallas as pl
from jax.experimental.pallas import tpu as pltpu
from jax.sharding import PartitionSpec as P

G = 16
NV = 4096
ITERS = 2
LANES = 128
TILES = 32
HI = 40
LO = 256
VMEM = pltpu.VMEM
SMEM = pltpu.SMEM
f32 = jnp.float32
bf16 = jnp.bfloat16

ref_lambda = 5.5
ref_shear = 5.5


def green_table():
    index = np.arange(G)

    def operator(ix, iy, iz):
        wave = [np.where(2 * m < G, m, m - G).astype(np.float64) for m in (ix, iy, iz)]
        kx, ky, kz = np.broadcast_arrays(wave[0], wave[1], wave[2])
        square = kx * kx + ky * ky + kz * kz
        safe = np.where(square > 0, square, 1.0)
        first = np.where(square > 0, 1.0 / (2.0 * ref_shear * safe), 0.0)
        factor = (ref_lambda + ref_shear) / (ref_shear * (ref_lambda + 2.0 * ref_shear))
        second = np.where(square > 0, factor / (safe * safe), 0.0)
        zero, one = np.zeros_like(kx), np.ones_like(kx)
        columns = []
        for j in range(6):
            xx, yy, zz, yz, xz, xy = [one if j == c else zero for c in range(6)]
            wx = xx * kx + xy * ky + xz * kz
            wy = xy * kx + yy * ky + yz * kz
            wz = xz * kx + yz * ky + zz * kz
            s = (wx * kx + wy * ky + wz * kz) * second
            columns.append(
                np.stack(
                    [
                        first * 2 * kx * wx - s * kx * kx,
                        first * 2 * ky * wy - s * ky * ky,
                        first * 2 * kz * wz - s * kz * kz,
                        first * (ky * wz + kz * wy) - s * ky * kz,
                        first * (kx * wz + kz * wx) - s * kx * kz,
                        first * (kx * wy + ky * wx) - s * kx * ky,
                        zero,
                        zero,
                    ]
                )
            )
        return np.stack(columns)

    ix, iy, iz = index[:, None, None], index[None, :, None], index[None, None, :]
    table = 0.5 * (operator(ix, iy, iz) + operator((-ix) % G, (-iy) % G, (-iz) % G)) / NV
    return table.reshape(6, 8, G, G * G).transpose(2, 0, 1, 3).astype(np.float32)


def plane_tables():
    plane = np.arange(G * G)
    phase = (plane[:, None] // G * (plane[None, :] // G) + plane[:, None] % G * (plane[None, :] % G)) % G
    parts = []
    for table in (np.cos(phase * (2 * np.pi / G)), np.sin(phase * (2 * np.pi / G))):
        table = table.astype(np.float32)
        high = table.astype(bf16)
        parts += [high, (table - high.astype(np.float32)).astype(bf16)]
    return np.stack(parts)


def twiddle(value, power, sign):
    re, im = value
    power %= 16
    if power == 0:
        return re, im
    if power == 4:
        return (-im, re) if sign > 0 else (im, -re)
    if power == 8:
        return -re, -im
    if power == 12:
        return (im, -re) if sign > 0 else (-im, re)
    angle = sign * 2 * math.pi * power / 16
    c, s = math.cos(angle), math.sin(angle)
    if power % 4 == 2:
        h = abs(c)
        a = re if c > 0 else -re
        b = im if c > 0 else -im
        if c * s > 0:
            return (a - b) * h, (a + b) * h
        return (a + b) * h, (b - a) * h
    return re * c - im * s, re * s + im * c


def dft4(v, sign):
    (ar, ai), (br, bi), (cr, ci), (dr, di) = v
    pr, pi_ = ar + cr, ai + ci
    mr, mi = ar - cr, ai - ci
    qr, qi = br + dr, bi + di
    nr, ni = br - dr, bi - di
    if sign < 0:
        jr, ji = ni, -nr
    else:
        jr, ji = -ni, nr
    return [(pr + qr, pi_ + qi), (mr + jr, mi + ji), (pr - qr, pi_ - qi), (mr - jr, mi - ji)]


def dft16(values, sign):
    inner = []
    for n2 in range(4):
        inner.append(dft4([values[n2 + 4 * n1] for n1 in range(4)], sign))
    out = [None] * 16
    for k1 in range(4):
        column = dft4([twiddle(inner[n2][k1], n2 * k1, sign) for n2 in range(4)], sign)
        for k2 in range(4):
            out[k1 + 4 * k2] = column[k2]
    return out


def slab_stress(d, first_rows):
    wide = d.shape
    trace = d[0:1] + d[1:2] + d[2:3]
    lam_trace = jnp.broadcast_to(d[6:7] * trace, wide)
    twice = jnp.broadcast_to(2.0 * d[7:8], wide)
    return twice * d + jnp.where(first_rows, lam_trace, 0.0)


def plane_products(sr, si, cmat):
    x = jnp.concatenate([sr[...], si[...]], axis=0)
    high = x.astype(bf16)
    low = (x - high.astype(f32)).astype(bf16)

    def times(at):
        a, b = cmat[at], cmat[at + 1]
        return (
            jnp.dot(high, a, preferred_element_type=f32)
            + jnp.dot(low, a, preferred_element_type=f32)
            + jnp.dot(high, b, preferred_element_type=f32)
        )

    return times(0), times(2)


def cells_kernel(
    count, owner, element, disp, nm, grads, micro, green, cmat, send, band_stress, st, sr, si
):
    half_rows = 8 * G
    lane = lax.broadcasted_iota(jnp.int32, (8, LANES), 1)
    row = lax.broadcasted_iota(jnp.int32, (8, LANES), 0)
    row_wide = lax.broadcasted_iota(jnp.int32, (8, 2 * LANES), 0)
    first_rows = row_wide < 3

    targets = []
    for k in range(4):
        e = element[0, k]
        base = pl.multiple_of(e // LANES * LANES, LANES)
        at = lane == e % LANES

        def pick(tile):
            return jnp.sum(jnp.where(at, tile, 0.0), axis=1, keepdims=True)

        node = pick(nm[:, pl.ds(base, LANES)].astype(f32)).astype(jnp.int32)
        shape = [jnp.broadcast_to(pick(grads[j, :, pl.ds(base, LANES)]), (8, LANES)) for j in range(3)]
        node = jnp.broadcast_to(node, (8, LANES)) - lane
        found = [jnp.zeros((8, LANES), f32) for _ in range(3)]
        for r in range(72):
            hit = node == r * LANES
            for c in range(3):
                values = jnp.broadcast_to(disp[c : c + 1, r * LANES : (r + 1) * LANES], (8, LANES))
                found[c] = jnp.where(hit, values, found[c])
        u = [jnp.sum(found[c], axis=1, keepdims=True) for c in range(3)]

        def total(value):
            return jnp.sum(value, axis=0, keepdims=True)

        parts = [
            total(u[0] * shape[0]),
            total(u[1] * shape[1]),
            total(u[2] * shape[2]),
            0.5 * total(u[1] * shape[2] + u[2] * shape[1]),
            0.5 * total(u[0] * shape[2] + u[2] * shape[0]),
            0.5 * total(u[0] * shape[1] + u[1] * shape[0]),
        ]
        target = jnp.zeros((8, LANES), f32)
        for c in range(6):
            target = jnp.where(row == c, jnp.broadcast_to(parts[c], (8, LANES)), target)
        targets.append(target)

    def slab(k, x, iteration):
        if iteration == 0:
            return micro[k, :, 2 * LANES * x : 2 * LANES * (x + 1)]
        return st[k, 8 * x : 8 * x + 8, :]

    shifts = []
    for k in range(4):
        total = jnp.zeros((8, 2 * LANES), f32)
        for x in range(G):
            total = total + slab(k, x, 0)
        mean = jnp.sum(total, axis=1, keepdims=True) * (1.0 / NV)
        shift = jnp.where(row < 6, targets[k] - mean, 0.0)
        shifts.append(jnp.concatenate([shift, shift], axis=1))

    for iteration in range(ITERS):
        for pair in range(2):
            for x in range(G):
                at = pair * half_rows + 8 * x
                sr[at : at + 8, :] = slab_stress(slab(2 * pair, x, iteration), first_rows)
                si[at : at + 8, :] = slab_stress(slab(2 * pair + 1, x, iteration), first_rows)
        by_cos, by_sin = plane_products(sr, si, cmat)
        rows = 2 * half_rows
        sr[...] = by_cos[:rows] + by_sin[rows:]
        si[...] = by_cos[rows:] - by_sin[:rows]
        for pair in range(2):
            for part in range(2):
                cols = slice(part * LANES, (part + 1) * LANES)
                at = [pair * half_rows + 8 * x for x in range(G)]
                values = dft16([(sr[a : a + 8, cols], si[a : a + 8, cols]) for a in at], -1)
                for x in range(G):
                    sr[at[x] : at[x] + 8, cols] = values[x][0]
                    si[at[x] : at[x] + 8, cols] = values[x][1]
                updates = []
                for x in range(G):
                    re = im = None
                    for j in range(6):
                        weight = green[x, j, :, cols]
                        tr = weight * jnp.broadcast_to(sr[at[x] + j : at[x] + j + 1, cols], (8, LANES))
                        ti = weight * jnp.broadcast_to(si[at[x] + j : at[x] + j + 1, cols], (8, LANES))
                        re = tr if re is None else re + tr
                        im = ti if im is None else im + ti
                    updates.append((re, im))
                values = dft16(updates, 1)
                for x in range(G):
                    sr[at[x] : at[x] + 8, cols] = values[x][0]
                    si[at[x] : at[x] + 8, cols] = values[x][1]
        by_cos, by_sin = plane_products(sr, si, cmat)
        sr[...] = by_cos[:rows] - by_sin[rows:]
        si[...] = by_cos[rows:] + by_sin[:rows]
        for k in range(4):
            source = (sr, si)[k % 2]
            for x in range(G):
                at = k // 2 * half_rows + 8 * x
                value = slab(k, x, iteration) - source[at : at + 8, :]
                if iteration == 0:
                    value = value + shifts[k]
                st[k, 8 * x : 8 * x + 8, :] = value

    result = jnp.zeros((8, LANES), f32)
    for k in range(4):
        live = k < count[0]
        total = jnp.zeros((8, 2 * LANES), f32)
        for x in range(G):
            total = total + slab_stress(st[k, 8 * x : 8 * x + 8, :], first_rows)
        mean = jnp.sum(total, axis=1, keepdims=True) * (1.0 / NV)
        result = jnp.where((lane == k) & live, jnp.broadcast_to(mean, (8, LANES)), result)
        pool = owner[0, k] & 3

        @pl.when(live)
        def _():
            for i in range(TILES):
                x, part = i // 2, i % 2
                send[i * 4 + pool] = st[k, 8 * x : 8 * x + 8, part * LANES : (part + 1) * LANES]

    band_stress[...] = result[0:6, 0:4]


def solve_cells(count, owner, element, disp, nm, grads, micro, green, cmat):
    rows = 16 * G
    return pl.pallas_call(
        cells_kernel,
        out_shape=(
            jax.ShapeDtypeStruct((4 * TILES, 8, LANES), f32),
            jax.ShapeDtypeStruct((6, 4), f32),
        ),
        in_specs=[pl.BlockSpec(memory_space=SMEM)] * 3 + [pl.BlockSpec(memory_space=VMEM)] * 6,
        out_specs=(pl.BlockSpec(memory_space=VMEM), pl.BlockSpec(memory_space=VMEM)),
        scratch_shapes=[
            VMEM((4, 8 * G, 2 * LANES), f32),
            VMEM((rows, 2 * LANES), f32),
            VMEM((rows, 2 * LANES), f32),
        ],
        compiler_params=pltpu.CompilerParams(vmem_limit_bytes=32 << 20),
        name="cells",
    )(count, owner, element, disp, nm, grads, micro, green, cmat)


def one_hot_sum(node, values, width):
    hi = jnp.broadcast_to(node >> 8, (HI, width))
    lo = jnp.broadcast_to(node & 255, (LO, width))
    coarse = lax.broadcasted_iota(jnp.int32, (HI, width), 0) == hi
    fine = lax.broadcasted_iota(jnp.int32, (LO, width), 0) == lo
    left = jnp.concatenate(
        [jnp.where(coarse, jnp.broadcast_to(v, (HI, width)), 0.0) for v in values], axis=0
    ).astype(bf16)
    right = jnp.where(fine, 1.0, 0.0).astype(bf16)
    return left, right


def halves(value):
    high = value.astype(bf16).astype(f32)
    return high, value - high


def macro_kernel(count, element, replace, disp, nm, grads, volumes, moduli, shared, own, f0, f1, f2, f3, sums):
    sums[...] = jnp.zeros_like(sums)
    lane = lax.broadcasted_iota(jnp.int32, (1, LANES), 1)
    live = [k < count[0] for k in range(4)]

    def scatter(node, forces):
        values = []
        for force in forces:
            values += list(halves(force))
        total = None
        for s in range(0, 8, 2):
            lefts, rights = [], []
            for q in (s, s + 1):
                left, right = one_hot_sum(node[q : q + 1], [v[q : q + 1] for v in values], LANES)
                lefts.append(left)
                rights.append(right)
            product = lax.dot_general(
                jnp.concatenate(lefts, axis=1),
                jnp.concatenate(rights, axis=1),
                (((1,), (1,)), ((), ())),
                preferred_element_type=f32,
            )
            total = product if total is None else total + product
        sums[...] += total

    def body(step, carry):
        scatter(carry[0], carry[1:])
        t = jnp.minimum(step, 63)
        cols = pl.ds(pl.multiple_of(t * LANES, LANES), LANES)
        node = nm[:, cols]
        hi, lo = node >> 7, node & 127
        u = [jnp.zeros((8, LANES), f32) for _ in range(3)]
        for r in range(72):
            hit = hi == r
            for c in range(3):
                values = jnp.broadcast_to(disp[c : c + 1, r * LANES : (r + 1) * LANES], (8, LANES))
                found = jnp.take_along_axis(values, lo, axis=1, mode="promise_in_bounds")
                u[c] = jnp.where(hit, found, u[c])
        g = [grads[j, :, cols] for j in range(3)]

        def total(value):
            return jnp.sum(value, axis=0, keepdims=True)

        strain = [
            total(u[0] * g[0]),
            total(u[1] * g[1]),
            total(u[2] * g[2]),
            0.5 * total(u[1] * g[2] + u[2] * g[1]),
            0.5 * total(u[0] * g[2] + u[2] * g[0]),
            0.5 * total(u[0] * g[1] + u[1] * g[0]),
        ]
        lam = moduli[0:1, cols]
        mu = moduli[1:2, cols]
        volume = volumes[pl.ds(t, 1), :]
        spherical = lam * (strain[0] + strain[1] + strain[2])
        stress = [spherical + 2.0 * mu * strain[c] for c in range(3)]
        stress += [2.0 * mu * strain[c] for c in range(3, 6)]
        for k in range(4):
            hit = (lane + t * LANES == element[0, k]) & live[k]
            stress = [jnp.where(hit, replace[c, k], stress[c]) for c in range(6)]
        xx, yy, zz, yz, xz, xy = [
            jnp.broadcast_to(component * volume, (8, LANES)) for component in stress
        ]
        fx = xx * g[0] + xy * g[1] + xz * g[2]
        fy = xy * g[0] + yy * g[1] + yz * g[2]
        fz = xz * g[0] + yz * g[1] + zz * g[2]
        return node, fx, fy, fz

    zero = jnp.zeros((8, LANES), f32)
    lax.fori_loop(0, 65, body, (jnp.zeros((8, LANES), jnp.int32), zero, zero, zero))

    for c in range(3):
        at = 2 * c * HI
        own[c * HI : (c + 1) * HI, :] = sums[at : at + HI, :] + sums[at + HI : at + 2 * HI, :]

    faces = (f0, f1, f2, f3)
    for pair in range(4):
        first, second = 2 * pair, 2 * pair + 1
        node = jnp.concatenate(
            [
                shared[0, :, first * LANES : (first + 1) * LANES],
                shared[0, :, second * LANES : (second + 1) * LANES],
            ],
            axis=0,
        )
        hi, lo = node >> 7, node & 127
        picked = [jnp.zeros((8, LANES), f32) for _ in range(3)]
        for r in range(72):
            hit = hi == r
            for c in range(3):
                at = c * HI + r // 2
                cols = slice(r % 2 * LANES, (r % 2 + 1) * LANES)
                values = jnp.broadcast_to(own[at : at + 1, cols], (8, LANES))
                found = jnp.take_along_axis(values, lo, axis=1, mode="promise_in_bounds")
                picked[c] = jnp.where(hit, found, picked[c])
        for c in range(3):
            for face in range(4):
                faces[face][c : c + 1, first * LANES : (first + 1) * LANES] = picked[c][face : face + 1]
                faces[face][c : c + 1, second * LANES : (second + 1) * LANES] = picked[c][
                    4 + face : 5 + face
                ]


def macro_forces(count, element, replace, disp, nm, grads, volumes, moduli, shared):
    vmem = pl.BlockSpec(memory_space=VMEM)
    return pl.pallas_call(
        macro_kernel,
        out_shape=(jax.ShapeDtypeStruct((3 * HI, LO), f32),)
        + (jax.ShapeDtypeStruct((3, 1024), f32),) * 4,
        in_specs=[pl.BlockSpec(memory_space=SMEM)] * 3 + [vmem] * 6,
        out_specs=(vmem,) * 5,
        scratch_shapes=[VMEM((6 * HI, LO), f32)],
        compiler_params=pltpu.CompilerParams(vmem_limit_bytes=32 << 20),
        name="macro",
    )(count, element, replace, disp, nm, grads, volumes, moduli, shared)


def assemble_kernel(own, shared, r0, r1, r2, r3, external, mass, out):
    total = None
    for face, arrived in enumerate((r0, r1, r2, r3)):
        for part in range(4):
            cols = slice(part * LO, (part + 1) * LO)
            values = []
            for c in range(3):
                values += list(halves(arrived[c : c + 1, cols]))
            left, right = one_hot_sum(shared[0, face : face + 1, cols], values, LO)
            product = lax.dot_general(
                left, right, (((1,), (1,)), ((), ())), preferred_element_type=f32
            )
            total = product if total is None else total + product
    for c in range(3):
        at = 2 * c * HI
        whole = own[c * HI : (c + 1) * HI, :] + total[at : at + HI] + total[at + HI : at + 2 * HI]
        for r in range(36):
            out[c : c + 1, r * LO : (r + 1) * LO] = whole[r : r + 1]
    out[...] = (external[...] - out[...]) / mass[...]


def assemble(own, shared, arrived, external, mass):
    vmem = pl.BlockSpec(memory_space=VMEM)
    return pl.pallas_call(
        assemble_kernel,
        out_shape=jax.ShapeDtypeStruct(external.shape, f32),
        in_specs=[vmem] * 8,
        out_specs=vmem,
        compiler_params=pltpu.CompilerParams(vmem_limit_bytes=32 << 20),
        name="assemble",
    )(own, shared, *arrived, external, mass)


def sort_kernel(pool, owners, pieces, out, order, places, sem):
    blocks = owners.shape[0]
    lane = lax.broadcasted_iota(jnp.int32, (blocks, LANES), 1)
    block = lax.broadcasted_iota(jnp.int32, (blocks, LANES), 0)
    wanted = lane * 4 + pool[0]
    hit = jnp.zeros((blocks, LANES), jnp.bool_)
    for k in range(4):
        hit = hit | (jnp.broadcast_to(owners[:, k : k + 1], (blocks, LANES)) == wanted)
    first = jnp.min(jnp.where(hit, block, blocks - 1), axis=0, keepdims=True)
    last = jnp.max(jnp.where(hit, block, 0), axis=0, keepdims=True)
    order[0:1, :] = first
    order[1:2, :] = last
    copy = pltpu.make_async_copy(order, places, sem)
    copy.start()
    copy.wait()
    for b in range(out.shape[0]):
        for s in range(2):
            out[b, s] = pieces[places[s, b]]


def sort_pieces(pool, owners, pieces, bricks):
    vmem = pl.BlockSpec(memory_space=VMEM)
    return pl.pallas_call(
        sort_kernel,
        out_shape=jax.ShapeDtypeStruct((bricks, 2, 8, LANES), f32),
        in_specs=[pl.BlockSpec(memory_space=SMEM), vmem, vmem],
        out_specs=vmem,
        scratch_shapes=[VMEM((8, LANES), jnp.int32), SMEM((8, LANES), jnp.int32), pltpu.SemaphoreType.DMA],
        compiler_params=pltpu.CompilerParams(vmem_limit_bytes=32 << 20),
        name="sort_pieces",
    )(pool, owners, pieces)


def join_kernel(pieces, out):
    for i in range(TILES):
        for s in range(2):
            out[s, :, i * LANES : (i + 1) * LANES] = pieces[i, s]


def join_pieces(pieces):
    vmem = pl.BlockSpec(memory_space=VMEM)
    return pl.pallas_call(
        join_kernel,
        out_shape=jax.ShapeDtypeStruct((2, 8, NV), f32),
        in_specs=[vmem],
        out_specs=vmem,
        name="join_pieces",
    )(pieces)


def shards(
    displacement,
    node_map,
    shape_grads,
    volumes,
    elastic_moduli,
    external_force,
    nodal_mass,
    shared_nodes,
    band_count,
    band_owner,
    band_element,
    micro_fields,
):
    both = ("brick", "pool")
    bricks, pools = lax.axis_size("brick"), lax.axis_size("pool")
    owners = lax.all_gather(band_owner, both, axis=0, tiled=True)
    send, band_stress = solve_cells(
        band_count,
        band_owner,
        band_element,
        displacement,
        node_map,
        shape_grads,
        micro_fields,
        jnp.asarray(green_table()),
        jnp.asarray(plane_tables()),
    )
    pieces = lax.all_to_all(send, both, split_axis=0, concat_axis=0, tiled=True)
    own, f0, f1, f2, f3 = macro_forces(
        band_count,
        band_element,
        band_stress,
        displacement,
        node_map,
        shape_grads,
        volumes.reshape(64, LANES),
        elastic_moduli,
        shared_nodes,
    )
    up_b = [(i, i + 1) for i in range(bricks - 1)]
    down_b = [(i + 1, i) for i in range(bricks - 1)]
    up_p = [(i, i + 1) for i in range(pools - 1)]
    down_p = [(i + 1, i) for i in range(pools - 1)]
    arrived = (
        lax.ppermute(f1, "brick", up_b),
        lax.ppermute(f0, "brick", down_b),
        lax.ppermute(f3, "pool", up_p),
        lax.ppermute(f2, "pool", down_p),
    )
    pool = lax.axis_index("pool").astype(jnp.int32).reshape(1)
    sorted_pieces = sort_pieces(pool, owners, pieces, bricks)
    mine = lax.all_to_all(sorted_pieces, "brick", split_axis=0, concat_axis=0, tiled=True)
    acceleration = assemble(own, shared_nodes, arrived, external_force, nodal_mass.reshape(1, -1))
    owned_fields = join_pieces(mine)
    return (acceleration, band_stress, owned_fields)


def solution(mesh):
    both = ("brick", "pool")
    placed = (
        P(None, both),
        P(None, both),
        P(None, None, both),
        P(both),
        P(None, both),
        P(None, both),
        P(both),
        P(both, None, None),
        P(both),
        P(both, None),
        P(both, None),
        P(both, None, None),
    )
    return jax.shard_map(
        shards,
        mesh=mesh,
        in_specs=placed,
        out_specs=(P(None, both), P(None, both), P(both, None, None)),
        check_vma=False,
    )
```

time: 1230 us -> 126 us (0.10)
  other arithmetic: 596 us -> 0 us
  local copies, waits for them, and re-layouts: 440 us -> 7.63 us
  matrix products: 153 us -> 0 us
  blocking collectives: 0 us -> 44.9 us
  Pallas kernels: 0 us -> 38.6 us
    scatter-add x5 -> x0, other arithmetic: 390 us -> none  [the longest x1 350 us: shards(): jnp.zeros((3, displacement.shape[1]), jnp.float32).at[:, node_map]]
    gather x9 -> x0, local copies, waits for them, and re-layouts: 311 us -> none  [the longest x2 270 us: element_strain(): corners = displacement[:, node_map]]
    mul x7 -> x0, other arithmetic: 174 us -> none  [the longest x1 172 us: element_strain(): 0.5 * (tensor[0, 1] + tensor[1, 0])]
    dot_general x26 -> x0, matrix products: 153 us -> none  [the longest x1 71.9 us: element_forces(): jnp.einsum('ije,jae->iae', full, shape_grads, precision=highest)]
    mul x1 -> x0, local copies, waits for them, and re-layouts: 52 us -> none  [element_forces(): jnp.einsum('ije,jae->iae', full, shape_grads, precision=highest)]
    all_gather x0 -> x1, blocking collectives: none -> 44.9 us  [shards(): owners = lax.all_gather(band_owner, both, axis=0, tiled=True)]
    pallas_call x0 -> x5, Pallas kernels: none -> 38.6 us  [the longest x1 27.1 us: macro_forces(): pl.pallas_call(macro_kernel, out_shape=(jax.ShapeDtypeStruct((3 * HI, LO)...]
    slice x8 -> x0, local copies, waits for them, and re-layouts: 38.5 us -> none  [the longest x2 23.2 us: element_forces(): stress[0]]
  transfers between devices with their start and end apart: 6 -> 6, of which waited for: 0 -> 1; matrix products, arithmetic and copies ran while one was open for 96% -> 1% of each run, Pallas kernels for 0% -> 23%
where the time goes in v1:
time: 126 us; the launch traced here: 125 us
  blocking collectives  44.9 us (36%)
  Pallas kernels  38.6 us (31%)
  starting transfers between devices  30.3 us (24%)
  local copies, waits for them, and re-layouts  7.63 us (6%)
  waiting for transfers between devices  1.88 us (1%)
  between operations  1.53 us (1%)
    all_gather x1, blocking collectives, shards(): owners = lax.all_gather(band_owner, both, axis=0, tiled=True)  44.9 us
    pallas_call x1, Pallas kernels, macro_forces(): pl.pallas_call(macro_kernel, out_shape=(jax.ShapeDtypeStruct((3 * HI, LO)...  27.1 us
    all_to_all x1, starting transfers between devices, shards(): pieces = lax.all_to_all(send, both, split_axis=0, concat_axis=0, tiled=True)  10.2 us
    unnamed x35, local copies, waits for them, and re-layouts  7.63 us
    pallas_call x1, Pallas kernels, solve_cells(): pl.pallas_call(cells_kernel, out_shape=(jax.ShapeDtypeStruct((4 * TILES,...  6.87 us
    all_to_all x1, starting transfers between devices, shards(): lax.all_to_all(sorted_pieces, 'brick', split_axis=0, concat_axis=0, tiled...  6.59 us
    ppermute x1, starting transfers between devices, shards(): lax.ppermute(f0, 'brick', down_b)  5.61 us
    ppermute x1, starting transfers between devices, shards(): lax.ppermute(f2, 'pool', down_p)  3.09 us
  transfers between devices with their start and end apart: 6, of which 1 were waited for; matrix products, arithmetic and copies ran while one was open for 1% of the time, Pallas kernels for 23%

profile of v1, /device:TPU:40, one launch (start us, length us, event | category | flops | bytes accessed | tf_op | source)
XLA Modules:
  0.0 124.8 jit_solution(9007990761517832040)
XLA Ops:
  0.6 0.0 copy-start.15
  0.6 0.0 copy-start.14
  1.3 0.0 copy-done.15
  1.3 0.0 copy-done.14
  1.3 0.0 copy-start
  1.3 1.1 copy-done
  2.5 0.0 copy-start.2
  2.5 0.9 copy-done.2
  3.4 1.1 copy-done.4
  4.6 0.9 copy-done.5
  5.5 1.0 copy-done.7
  6.5 1.0 copy-done.8
  7.6 6.9 %cells.1 = (f32[128,8,128]{2,1,0:T(8,128)}, f32[6,4]{1,0:T(8,128)S(1)}) custom-call(s32[1]{0:T(128)S(6)} %copy.20.count, s32[1,4]{1,0:T(1,128)S(1)} %copy-done.14, s32[1,4]{1,0:T(1,128)S(1)} %copy-done.15, f32[3,9216]{1,0:T(4,128)S(1)} %copy-done.5, s32[8,8192]{1,0:T(8,128)S(1)} %copy-done.2, f32[3,8,8192]{2,1,0:T(8,128)S(1)} %copy-done, ...), custom_call_target="tpu_custom_call" | custom-call | tf_op jit(solution)/shard_map/cells/pallas_call | solution.py:274
  14.4 10.2 %all-to-all-start = ((f32[128,8,128]{2,1,0:T(8,128)}), f32[128,8,128]{2,1,0:T(8,128)S(1)}, u32[]{:S(2)}, u32[]{:S(2)}) async-start(f32[128,8,128]{2,1,0:T(8,128)} %get-tuple-element.16), calls=%async_computation | async-start | bytes 1048576 | tf_op jit(solution)/shard_map/all_to_all | solution.py:537
  24.6 0.0 copy-start.1
  24.6 44.9 %all-gather = s32[128,1,4]{2,1,0:T(1,128)S(1)} all-gather(s32[1,1,4]{2,1,0:T(1,128)S(1)} %bitcast.8), channel_id=1, replica_groups=mesh['brick'=32,'pool'=4] {'brick','pool'}, dimensions={0}, use_global_device_ids=true | all-gather | bytes 2064 | tf_op jit(solution)/shard_map/all_gather | solution.py:525
  69.5 0.0 all-to-all-done.pieces
  69.5 1.5 %sort_pieces.1 = f32[32,2,8,128]{3,2,1,0:T(8,128)} custom-call(s32[1]{0:T(128)} %bitcast.2.pool, s32[128,4]{1,0:T(8,128)S(1)} %bitcast.5, f32[128,8,128]{2,1,0:T(8,128)S(1)} %all-to-all-done.pieces), custom_call_target="tpu_custom_call" | custom-call | tf_op jit(solution)/shard_map/sort_pieces/pallas_call | solution.py:481
  71.0 0.0 copy-start.3
  71.0 0.0 copy-start.6
  71.0 0.0 copy-start.10
  71.0 0.0 copy-start.11
  71.0 0.0 copy-start.13
  71.1 6.6 %all-to-all-start.1 = ((f32[32,2,8,128]{3,2,1,0:T(8,128)}), f32[32,2,8,128]{3,2,1,0:T(8,128)S(1)}, u32[]{:S(2)}, u32[]{:S(2)}) async-start(f32[32,2,8,128]{3,2,1,0:T(8,128)} %sort_pieces.1), calls=%async_computation.1 | async-start | bytes 524288 | tf_op jit(solution)/shard_map/all_to_all | solution.py:561
  77.6 0.0 copy-done.1
  77.7 0.0 copy-done.3
  77.7 0.0 copy-done.6
  77.7 0.0 copy-done.10
  77.7 0.0 copy-done.11
  77.7 0.0 copy-done.13
  77.7 0.0 copy-start.9
  77.7 0.0 copy-start.12
  77.7 27.1 %macro.1 = (f32[120,256]{1,0:T(8,128)S(1)}, f32[3,1024]{1,0:T(4,128)S(1)}, f32[3,1024]{1,0:T(4,128)S(1)}, f32[3,1024]{1,0:T(4,128)S(1)}, f32[3,1024]{1,0:T(4,128)S(1)}) custom-call(s32[1]{0:T(128)S(6)} %copy.20.count, s32[1,4]{1,0:T(1,128)S(1)} %copy-done.15, f32[6,4]{1,0:T(8,128)S(1)} %get-tuple-element.21.replace, f32[3,9216]{1,0:T(4,128)S(1)} %copy-done.6, ...), custom_call_target="tpu_custom_call" | custom-call | tf_op jit(solution)/shard_map/macro/pallas_call | solution.py:414
  104.8 2.1 %collective-permute-start = (f32[3,1024]{1,0:T(4,128)S(1)}, f32[3,1024]{1,0:T(4,128)S(1)}, u32[]{:S(2)}, u32[]{:S(2)}) collective-permute-start(f32[3,1024]{1,0:T(4,128)S(1)} %get-tuple-element.12), channel_id=1, source_target_pairs={{0,4},{4,8},{8,12},{12,16},{16,20},{20,24},{24,28},{28,32},{32,36}... | collective-permute-start | bytes 36872 | tf_op jit(solution)/shard_map/ppermute | solution.py:554
  106.9 5.6 %collective-permute-start.1 = (f32[3,1024]{1,0:T(4,128)S(1)}, f32[3,1024]{1,0:T(4,128)S(1)}, u32[]{:S(2)}, u32[]{:S(2)}) collective-permute-start(f32[3,1024]{1,0:T(4,128)S(1)} %get-tuple-element.13), channel_id=1, source_target_pairs={{4,0},{8,4},{12,8},{16,12},{20,16},{24,20},{28,24},{32,28},{36,32}... | collective-permute-start | bytes 36872 | tf_op jit(solution)/shard_map/ppermute | solution.py:555
  112.5 2.8 %collective-permute-start.2 = (f32[3,1024]{1,0:T(4,128)S(1)}, f32[3,1024]{1,0:T(4,128)S(1)}, u32[]{:S(2)}, u32[]{:S(2)}) collective-permute-start(f32[3,1024]{1,0:T(4,128)S(1)} %get-tuple-element.14), channel_id=1, source_target_pairs={{0,1},{1,2},{2,3},{4,5},{5,6},{6,7},{8,9},{9,10},{10,11},{12,13},{... | collective-permute-start | bytes 36872 | tf_op jit(solution)/shard_map/ppermute | solution.py:556
  115.3 3.1 %collective-permute-start.3 = (f32[3,1024]{1,0:T(4,128)S(1)}, f32[3,1024]{1,0:T(4,128)S(1)}, u32[]{:S(2)}, u32[]{:S(2)}) collective-permute-start(f32[3,1024]{1,0:T(4,128)S(1)} %get-tuple-element.15), channel_id=1, source_target_pairs={{1,0},{2,1},{3,2},{5,4},{6,5},{7,6},{9,8},{10,9},{11,10},{13,12},{... | collective-permute-start | bytes 36872 | tf_op jit(solution)/shard_map/ppermute | solution.py:557
  118.4 0.7 copy.19
  119.0 0.0 collective-permute-done.r0
  119.0 0.0 collective-permute-done.1.r1
  119.0 0.0 collective-permute-done.2.r2
  119.0 1.9 %collective-permute-done.3.r3 = f32[3,1024]{1,0:T(4,128)S(1)} collective-permute-done((f32[3,1024]{1,0:T(4,128)S(1)}, f32[3,1024]{1,0:T(4,128)S(1)}, u32[]{:S(2)}, u32[]{:S(2)}) %collective-permute-start.3) | collective-permute-done | bytes 12320 | tf_op jit(solution)/shard_map/ppermute | solution.py:557
  120.9 0.0 copy-done.9
  120.9 0.0 copy-done.12
  120.9 1.5 %assemble.1 = f32[3,9216]{1,0:T(4,128)} custom-call(f32[120,256]{1,0:T(8,128)S(1)} %get-tuple-element.11.own, s32[1,4,1024]{2,1,0:T(4,128)S(1)} %copy-done.10, f32[3,1024]{1,0:T(4,128)S(1)} %collective-permute-done.r0, f32[3,1024]{1,0:T(4,128)S(1)} %collective-permute-done.1.r1, f32[3,1024]{1,0:T(4,128)S(1)} %collective-permute-done.2.r2, ...), custom_call_target="tpu_custom_call" | custom-call | tf_op jit(solution)/shard_map/assemble/pallas_call | solution.py:449
  122.4 0.0 all-to-all-done.1.pieces
  122.4 0.7 copy-done.16
  123.1 1.7 %join_pieces.1 = f32[2,8,4096]{2,1,0:T(8,128)} custom-call(f32[32,2,8,128]{3,2,1,0:T(8,128)} %copy-done.16), custom_call_target="tpu_custom_call" | custom-call | tf_op jit(solution)/shard_map/join_pieces/pallas_call | solution.py:500
  (5 shorter events, 0.0 us)
Async XLA Ops:
  0.6 0.7 copy-start.15
  0.6 0.7 copy-start.14
  1.3 1.1 copy-start
  2.5 0.9 copy-start.2
  3.4 1.1 copy-start.4
  4.6 0.9 copy-start.5
  5.5 1.0 copy-start.7
  6.5 1.0 copy-start.8
  14.4 55.0 %all-to-all-start = ((f32[128,8,128]{2,1,0:T(8,128)}), f32[128,8,128]{2,1,0:T(8,128)S(1)}, u32[]{:S(2)}, u32[]{:S(2)}) async-start(f32[128,8,128]{2,1,0:T(8,128)} %get-tuple-element.16), calls=%async_computation | async-start | bytes 1048576 | tf_op jit(solution)/shard_map/all_to_all | solution.py:537
  24.6 53.1 %copy-start.1 = (f32[3,8,8192]{2,1,0:T(8,128)S(1)}, f32[3,8,8192]{2,1,0:T(8,128)}, u32[]{:S(2)}) copy-start(f32[3,8,8192]{2,1,0:T(8,128)} %grads.3) | copy-start | bytes 2359300
  71.0 6.7 %copy-start.3 = (s32[8,8192]{1,0:T(8,128)S(1)}, s32[8,8192]{1,0:T(8,128)}, u32[]{:S(2)}) copy-start(s32[8,8192]{1,0:T(8,128)} %nm.3) | copy-start | bytes 786436
  71.0 6.7 %copy-start.6 = (f32[3,9216]{1,0:T(4,128)S(1)}, f32[3,9216]{1,0:T(4,128)}, u32[]{:S(2)}) copy-start(f32[3,9216]{1,0:T(4,128)} %disp.3) | copy-start | bytes 331780
  71.0 6.7 %copy-start.10 = (s32[1,4,1024]{2,1,0:T(4,128)S(1)}, s32[1,4,1024]{2,1,0:T(4,128)}, u32[]{:S(2)}) copy-start(s32[1,4,1024]{2,1,0:T(4,128)} %shared.3) | copy-start | bytes 49156
  71.0 6.7 %copy-start.11 = (f32[2,8192]{1,0:T(2,128)S(1)}, f32[2,8192]{1,0:T(2,128)}, u32[]{:S(2)}) copy-start(f32[2,8192]{1,0:T(2,128)} %moduli.1) | copy-start | bytes 196612
  71.0 6.7 %copy-start.13 = (f32[8192]{0:T(1024)S(1)}, f32[8192]{0:T(1024)}, u32[]{:S(2)}) copy-start(f32[8192]{0:T(1024)} %param.17) | copy-start | bytes 98308
  71.1 51.3 %all-to-all-start.1 = ((f32[32,2,8,128]{3,2,1,0:T(8,128)}), f32[32,2,8,128]{3,2,1,0:T(8,128)S(1)}, u32[]{:S(2)}, u32[]{:S(2)}) async-start(f32[32,2,8,128]{3,2,1,0:T(8,128)} %sort_pieces.1), calls=%async_computation.1 | async-start | bytes 524288 | tf_op jit(solution)/shard_map/all_to_all | solution.py:561
  77.7 43.2 %copy-start.9 = (f32[3,9216]{1,0:T(4,128)S(1)}, f32[3,9216]{1,0:T(4,128)}, u32[]{:S(2)}) copy-start(f32[3,9216]{1,0:T(4,128)} %external.1) | copy-start | bytes 331780
  77.7 43.2 %copy-start.12 = (f32[9216]{0:T(1024)S(1)}, f32[9216]{0:T(1024)}, u32[]{:S(2)}) copy-start(f32[9216]{0:T(1024)} %param.20) | copy-start | bytes 110596
  104.8 14.2 %collective-permute-start = (f32[3,1024]{1,0:T(4,128)S(1)}, f32[3,1024]{1,0:T(4,128)S(1)}, u32[]{:S(2)}, u32[]{:S(2)}) collective-permute-start(f32[3,1024]{1,0:T(4,128)S(1)} %get-tuple-element.12), channel_id=1, source_target_pairs={{0,4},{4,8},{8,12},{12,16},{16,20},{20,24},{24,28},{28,32},{32,36}... | collective-permute-start | bytes 36872 | tf_op jit(solution)/shard_map/ppermute | solution.py:554
  106.9 12.1 %collective-permute-start.1 = (f32[3,1024]{1,0:T(4,128)S(1)}, f32[3,1024]{1,0:T(4,128)S(1)}, u32[]{:S(2)}, u32[]{:S(2)}) collective-permute-start(f32[3,1024]{1,0:T(4,128)S(1)} %get-tuple-element.13), channel_id=1, source_target_pairs={{4,0},{8,4},{12,8},{16,12},{20,16},{24,20},{28,24},{32,28},{36,32}... | collective-permute-start | bytes 36872 | tf_op jit(solution)/shard_map/ppermute | solution.py:555
  112.5 6.5 %collective-permute-start.2 = (f32[3,1024]{1,0:T(4,128)S(1)}, f32[3,1024]{1,0:T(4,128)S(1)}, u32[]{:S(2)}, u32[]{:S(2)}) collective-permute-start(f32[3,1024]{1,0:T(4,128)S(1)} %get-tuple-element.14), channel_id=1, source_target_pairs={{0,1},{1,2},{2,3},{4,5},{5,6},{6,7},{8,9},{9,10},{10,11},{12,13},{... | collective-permute-start | bytes 36872 | tf_op jit(solution)/shard_map/ppermute | solution.py:556
  115.3 5.6 %collective-permute-start.3 = (f32[3,1024]{1,0:T(4,128)S(1)}, f32[3,1024]{1,0:T(4,128)S(1)}, u32[]{:S(2)}, u32[]{:S(2)}) collective-permute-start(f32[3,1024]{1,0:T(4,128)S(1)} %get-tuple-element.15), channel_id=1, source_target_pairs={{1,0},{2,1},{3,2},{5,4},{6,5},{7,6},{9,8},{10,9},{11,10},{13,12},{... | collective-permute-start | bytes 36872 | tf_op jit(solution)/shard_map/ppermute | solution.py:557
  122.4 0.7 copy-start.16

commit v2 on v1

--- a/solution.py
+++ b/solution.py
@@ -1,3 +1,4 @@
+import functools
 import math
 
 import jax
@@ -15,6 +16,8 @@
 TILES = 32
 HI = 40
 LO = 256
+UNROLL = 2
+SPLIT = 32
 VMEM = pltpu.VMEM
 SMEM = pltpu.SMEM
 f32 = jnp.float32
@@ -250,6 +253,7 @@
                     value = value + shifts[k]
                 st[k, 8 * x : 8 * x + 8, :] = value
 
+    send[pl.ds(8, 4 * TILES, stride=9), :] = jnp.full((4 * TILES, LANES), -1.0, f32)
     result = jnp.zeros((8, LANES), f32)
     for k in range(4):
         live = k < count[0]
@@ -264,7 +268,11 @@
         def _():
             for i in range(TILES):
                 x, part = i // 2, i % 2
-                send[i * 4 + pool] = st[k, 8 * x : 8 * x + 8, part * LANES : (part + 1) * LANES]
+                send[pl.ds(9 * (4 * i + pool), 8), :] = st[
+                    k, 8 * x : 8 * x + 8, part * LANES : (part + 1) * LANES
+                ]
+            brick = (owner[0, k] >> 2).astype(f32)
+            send[pl.ds(9 * pool + 8, TILES, stride=36), :] = jnp.full((TILES, LANES), brick, f32)
 
     band_stress[...] = result[0:6, 0:4]
 
@@ -274,7 +282,7 @@
     return pl.pallas_call(
         cells_kernel,
         out_shape=(
-            jax.ShapeDtypeStruct((4 * TILES, 8, LANES), f32),
+            jax.ShapeDtypeStruct((36 * TILES, LANES), f32),
             jax.ShapeDtypeStruct((6, 4), f32),
         ),
         in_specs=[pl.BlockSpec(memory_space=SMEM)] * 3 + [pl.BlockSpec(memory_space=VMEM)] * 6,
@@ -284,7 +292,7 @@
             VMEM((rows, 2 * LANES), f32),
             VMEM((rows, 2 * LANES), f32),
         ],
-        compiler_params=pltpu.CompilerParams(vmem_limit_bytes=32 << 20),
+        compiler_params=pltpu.CompilerParams(vmem_limit_bytes=56 << 20),
         name="cells",
     )(count, owner, element, disp, nm, grads, micro, green, cmat)
 
@@ -306,8 +314,7 @@
     return high, value - high
 
 
-def macro_kernel(count, element, replace, disp, nm, grads, volumes, moduli, shared, own, f0, f1, f2, f3, sums):
-    sums[...] = jnp.zeros_like(sums)
+def macro_tiles(begin, end, unroll, count, element, replace, disp, nm, grads, volumes, moduli, sums):
     lane = lax.broadcasted_iota(jnp.int32, (1, LANES), 1)
     live = [k < count[0] for k in range(4)]
 
@@ -329,11 +336,9 @@
                 preferred_element_type=f32,
             )
             total = product if total is None else total + product
-        sums[...] += total
-
-    def body(step, carry):
-        scatter(carry[0], carry[1:])
-        t = jnp.minimum(step, 63)
+        return total
+
+    def forces_of(t):
         cols = pl.ds(pl.multiple_of(t * LANES, LANES), LANES)
         node = nm[:, cols]
         hi, lo = node >> 7, node & 127
@@ -374,8 +379,33 @@
         fz = xz * g[0] + yz * g[1] + zz * g[2]
         return node, fx, fy, fz
 
-    zero = jnp.zeros((8, LANES), f32)
-    lax.fori_loop(0, 65, body, (jnp.zeros((8, LANES), jnp.int32), zero, zero, zero))
+    def group(step):
+        return tuple(forces_of(begin + step * unroll + i) for i in range(unroll))
+
+    def add(carry):
+        total = None
+        for node, *forces in carry:
+            part = scatter(node, forces)
+            total = part if total is None else total + part
+        sums[...] += total
+
+    def body(step, carry):
+        add(carry)
+        return group(step)
+
+    add(lax.fori_loop(1, (end - begin) // unroll, body, group(0)))
+
+
+def macro_first_kernel(unroll, count, element, replace, disp, nm, grads, volumes, moduli, sums):
+    sums[...] = jnp.zeros_like(sums)
+    macro_tiles(0, SPLIT, unroll, count, element, replace, disp, nm, grads, volumes, moduli, sums)
+
+
+def macro_last_kernel(
+    unroll, count, element, replace, disp, nm, grads, volumes, moduli, so_far, shared, own, f0, f1, f2, f3, sums
+):
+    sums[...] = so_far[...]
+    macro_tiles(SPLIT, 64, unroll, count, element, replace, disp, nm, grads, volumes, moduli, sums)
 
     for c in range(3):
         at = 2 * c * HI
@@ -409,18 +439,30 @@
                 ]
 
 
-def macro_forces(count, element, replace, disp, nm, grads, volumes, moduli, shared):
+def macro_first(*arguments):
     vmem = pl.BlockSpec(memory_space=VMEM)
     return pl.pallas_call(
-        macro_kernel,
+        functools.partial(macro_first_kernel, UNROLL),
+        out_shape=jax.ShapeDtypeStruct((6 * HI, LO), f32),
+        in_specs=[pl.BlockSpec(memory_space=SMEM)] * 3 + [vmem] * 5,
+        out_specs=vmem,
+        compiler_params=pltpu.CompilerParams(vmem_limit_bytes=32 << 20),
+        name="macro_first",
+    )(*arguments)
+
+
+def macro_last(*arguments):
+    vmem = pl.BlockSpec(memory_space=VMEM)
+    return pl.pallas_call(
+        functools.partial(macro_last_kernel, UNROLL),
         out_shape=(jax.ShapeDtypeStruct((3 * HI, LO), f32),)
         + (jax.ShapeDtypeStruct((3, 1024), f32),) * 4,
-        in_specs=[pl.BlockSpec(memory_space=SMEM)] * 3 + [vmem] * 6,
+        in_specs=[pl.BlockSpec(memory_space=SMEM)] * 3 + [vmem] * 7,
         out_specs=(vmem,) * 5,
         scratch_shapes=[VMEM((6 * HI, LO), f32)],
         compiler_params=pltpu.CompilerParams(vmem_limit_bytes=32 << 20),
-        name="macro",
-    )(count, element, replace, disp, nm, grads, volumes, moduli, shared)
+        name="macro_last",
+    )(*arguments)
 
 
 def assemble_kernel(own, shared, r0, r1, r2, r3, external, mass, out):
@@ -456,37 +498,32 @@
     )(own, shared, *arrived, external, mass)
 
 
-def sort_kernel(pool, owners, pieces, out, order, places, sem):
-    blocks = owners.shape[0]
+def sort_kernel(pieces, out, order, places, sem):
+    blocks = pieces.shape[0] // 9
     lane = lax.broadcasted_iota(jnp.int32, (blocks, LANES), 1)
     block = lax.broadcasted_iota(jnp.int32, (blocks, LANES), 0)
-    wanted = lane * 4 + pool[0]
-    hit = jnp.zeros((blocks, LANES), jnp.bool_)
-    for k in range(4):
-        hit = hit | (jnp.broadcast_to(owners[:, k : k + 1], (blocks, LANES)) == wanted)
-    first = jnp.min(jnp.where(hit, block, blocks - 1), axis=0, keepdims=True)
-    last = jnp.max(jnp.where(hit, block, 0), axis=0, keepdims=True)
-    order[0:1, :] = first
-    order[1:2, :] = last
+    hit = pieces[pl.ds(8, blocks, stride=9), :] == lane.astype(f32)
+    order[0:1, :] = jnp.min(jnp.where(hit, block, blocks - 1), axis=0, keepdims=True)
+    order[1:2, :] = jnp.max(jnp.where(hit, block, 0), axis=0, keepdims=True)
     copy = pltpu.make_async_copy(order, places, sem)
     copy.start()
     copy.wait()
     for b in range(out.shape[0]):
         for s in range(2):
-            out[b, s] = pieces[places[s, b]]
-
-
-def sort_pieces(pool, owners, pieces, bricks):
+            out[b, s] = pieces[pl.ds(9 * places[s, b], 8), :]
+
+
+def sort_pieces(pieces, bricks):
     vmem = pl.BlockSpec(memory_space=VMEM)
     return pl.pallas_call(
         sort_kernel,
         out_shape=jax.ShapeDtypeStruct((bricks, 2, 8, LANES), f32),
-        in_specs=[pl.BlockSpec(memory_space=SMEM), vmem, vmem],
+        in_specs=[vmem],
         out_specs=vmem,
         scratch_shapes=[VMEM((8, LANES), jnp.int32), SMEM((8, LANES), jnp.int32), pltpu.SemaphoreType.DMA],
         compiler_params=pltpu.CompilerParams(vmem_limit_bytes=32 << 20),
         name="sort_pieces",
-    )(pool, owners, pieces)
+    )(pieces)
 
 
 def join_kernel(pieces, out):
@@ -522,7 +559,6 @@
 ):
     both = ("brick", "pool")
     bricks, pools = lax.axis_size("brick"), lax.axis_size("pool")
-    owners = lax.all_gather(band_owner, both, axis=0, tiled=True)
     send, band_stress = solve_cells(
         band_count,
         band_owner,
@@ -534,8 +570,10 @@
         jnp.asarray(green_table()),
         jnp.asarray(plane_tables()),
     )
-    pieces = lax.all_to_all(send, both, split_axis=0, concat_axis=0, tiled=True)
-    own, f0, f1, f2, f3 = macro_forces(
+    pieces = lax.all_to_all(
+        send.reshape(bricks * pools, 1, 9 * LANES), both, split_axis=0, concat_axis=0, tiled=True
+    )
+    macro = (
         band_count,
         band_element,
         band_stress,
@@ -544,8 +582,12 @@
         shape_grads,
         volumes.reshape(64, LANES),
         elastic_moduli,
-        shared_nodes,
     )
+    so_far = macro_first(*macro)
+    pieces, so_far = lax.optimization_barrier((pieces, so_far))
+    sorted_pieces = sort_pieces(pieces.reshape(9 * bricks * pools, LANES), bricks)
+    mine = lax.all_to_all(sorted_pieces, "brick", split_axis=0, concat_axis=0, tiled=True)
+    own, f0, f1, f2, f3 = macro_last(*macro, so_far, shared_nodes)
     up_b = [(i, i + 1) for i in range(bricks - 1)]
     down_b = [(i + 1, i) for i in range(bricks - 1)]
     up_p = [(i, i + 1) for i in range(pools - 1)]
@@ -556,9 +598,6 @@
         lax.ppermute(f3, "pool", up_p),
         lax.ppermute(f2, "pool", down_p),
     )
-    pool = lax.axis_index("pool").astype(jnp.int32).reshape(1)
-    sorted_pieces = sort_pieces(pool, owners, pieces, bricks)
-    mine = lax.all_to_all(sorted_pieces, "brick", split_axis=0, concat_axis=0, tiled=True)
     acceleration = assemble(own, shared_nodes, arrived, external_force, nodal_mass.reshape(1, -1))
     owned_fields = join_pieces(mine)
     return (acceleration, band_stress, owned_fields)

time: 126 us -> 73.7 us (0.58)
  blocking collectives: 44.9 us -> 0 us
  local copies, waits for them, and re-layouts: 7.63 us -> 2 us
  Pallas kernels: 38.6 us -> 35.6 us
  waiting for transfers between devices: 1.88 us -> 3.75 us
    all_gather x1 -> x0, blocking collectives: 44.9 us -> none  [shards(): owners = lax.all_gather(band_owner, both, axis=0, tiled=True)]
    unnamed x35 -> x23, local copies, waits for them, and re-layouts: 7.63 us -> 2 us
    pallas_call x2 -> x3, Pallas kernels: 33.9 us -> 31.1 us  [the longest x1 12 us: macro_last(): pl.pallas_call(functools.partial(macro_last_kernel, UNROLL), out_shape=(j...]
  transfers between devices with their start and end apart: 6 -> 6, of which waited for: 1 -> 2; matrix products, arithmetic and copies ran while one was open for 1% -> 1% of each run, Pallas kernels for 23% -> 34%
where the time goes in v2:
time: 73.7 us; the launch traced here: 73.1 us
  Pallas kernels  35.6 us (48%)
  starting transfers between devices  30.2 us (41%)
  waiting for transfers between devices  3.75 us (5%)
  local copies, waits for them, and re-layouts  2 us (3%)
  between operations  1.48 us (2%)
    pallas_call x1, Pallas kernels, macro_last(): pl.pallas_call(functools.partial(macro_last_kernel, UNROLL), out_shape=(j...  12 us
    pallas_call x1, Pallas kernels, macro_first(): pl.pallas_call(functools.partial(macro_first_kernel, UNROLL), out_shape=j...  11.1 us
    all_to_all x1, starting transfers between devices, shards(): lax.all_to_all(send.reshape(bricks * pools, 1, 9 * LANES), both, split_ax...  10.2 us
    pallas_call x1, Pallas kernels, solve_cells(): pl.pallas_call(cells_kernel, out_shape=(jax.ShapeDtypeStruct((36 * TILES,...  7.93 us
    all_to_all x1, starting transfers between devices, shards(): lax.all_to_all(sorted_pieces, 'brick', split_axis=0, concat_axis=0, tiled...  6.51 us
    ppermute x1, starting transfers between devices, shards(): lax.ppermute(f0, 'brick', down_b)  5.62 us
    ppermute x1, starting transfers between devices, shards(): lax.ppermute(f3, 'pool', up_p)  3.64 us
    ppermute x1, waiting for transfers between devices, shards(): lax.ppermute(f2, 'pool', down_p)  2.75 us
  transfers between devices with their start and end apart: 6, of which 2 were waited for; matrix products, arithmetic and copies ran while one was open for 1% of the time, Pallas kernels for 34%

profile of v2, /device:TPU:40, one launch (start us, length us, event | category | flops | bytes accessed | tf_op | source)
XLA Modules:
  0.0 73.1 jit_solution(6060300057544251401)
XLA Ops:
  1.3 0.0 copy-start.2
  1.3 7.9 %cells.1 = (f32[1152,128]{1,0:T(8,128)}, f32[6,4]{1,0:T(8,128)}) custom-call(s32[1]{0:T(128)S(6)} %copy.20.count, s32[1,4]{1,0:T(1,128)} %owner.1, s32[1,4]{1,0:T(1,128)} %element.5, f32[3,9216]{1,0:T(4,128)} %disp.5, s32[8,8192]{1,0:T(8,128)} %nm.5, f32[3,8,8192]{2,1,0:T(8,128)} %grads.5, f32[4,8,4096]{2,1,0:T(8,128)} %micro.1, ...), custom_call_target="tpu_custom_call" | custom-call | tf_op jit(solution)/shard_map/cells/pallas_call | solution.py:282
  9.2 0.0 copy-start
  9.2 0.0 copy-start.1
  9.2 0.0 copy-start.3
  9.2 0.0 copy-start.5
  9.3 0.0 copy-start.7
  9.3 10.2 %all-to-all-start = ((f32[128,1,1152]{2,1,0:T(1,128)}), f32[128,1,1152]{2,1,0:T(1,128)S(1)}, u32[]{:S(2)}, u32[]{:S(2)}) async-start(f32[128,1,1152]{2,1,0:T(1,128)} %bitcast.8), calls=%async_computation | async-start | bytes 1179648 | tf_op jit(solution)/shard_map/all_to_all | solution.py:573
  19.5 0.0 copy-start.9
  19.5 0.0 copy-done.2
  19.5 0.0 copy-done
  19.5 0.0 copy-done.1
  19.5 0.0 copy-done.3
  19.5 0.0 copy-done.5
  19.5 0.0 copy-done.7
  19.5 0.6 copy-done.9
  20.1 11.1 %macro_first.1.so_far = f32[240,256]{1,0:T(8,128)S(1)} custom-call(s32[1]{0:T(128)S(6)} %copy.20.count, s32[1,4]{1,0:T(1,128)S(1)} %copy-done.9, f32[6,4]{1,0:T(8,128)S(1)} %copy-done.7, f32[3,9216]{1,0:T(4,128)S(1)} %copy-done.2, s32[8,8192]{1,0:T(8,128)S(1)} %copy-done.1, f32[3,8,8192]{2,1,0:T(8,128)S(1)} %copy-done, f32[64,128]{1,0:T(8,128)S(1)} %bitcast.5, ...), custom_call_target="tpu_custom_call" | custom-call | tf_op jit(solution)/shard_map/macro_first/pallas_call | solution.py:444
  31.2 1.0 %all-to-all-done = f32[128,1,1152]{2,1,0:T(1,128)S(1)} async-done(((f32[128,1,1152]{2,1,0:T(1,128)}), f32[128,1,1152]{2,1,0:T(1,128)S(1)}, u32[]{:S(2)}, u32[]{:S(2)}) %all-to-all-start) | async-done | bytes 589856 | tf_op jit(solution)/shard_map/all_to_all | solution.py:573
  32.2 1.4 %sort_pieces.1 = f32[32,2,8,128]{3,2,1,0:T(8,128)} custom-call(f32[1152,128]{1,0:T(8,128)S(1)} %bitcast.4), custom_call_target="tpu_custom_call" | custom-call | tf_op jit(solution)/shard_map/sort_pieces/pallas_call | solution.py:518
  33.6 0.0 copy-start.6
  33.6 6.5 %all-to-all-start.1 = ((f32[32,2,8,128]{3,2,1,0:T(8,128)}), f32[32,2,8,128]{3,2,1,0:T(8,128)S(1)}, u32[]{:S(2)}, u32[]{:S(2)}) async-start(f32[32,2,8,128]{3,2,1,0:T(8,128)} %sort_pieces.1), calls=%async_computation.1 | async-start | bytes 524288 | tf_op jit(solution)/shard_map/all_to_all | solution.py:589
  40.2 0.0 copy-done.6
  40.2 0.0 copy-start.4
  40.2 0.0 copy-start.8
  40.2 12.0 %macro_last.1 = (f32[120,256]{1,0:T(8,128)S(1)}, f32[3,1024]{1,0:T(4,128)S(1)}, f32[3,1024]{1,0:T(4,128)S(1)}, f32[3,1024]{1,0:T(4,128)S(1)}, f32[3,1024]{1,0:T(4,128)S(1)}) custom-call(s32[1]{0:T(128)S(6)} %copy.20.count, s32[1,4]{1,0:T(1,128)S(1)} %copy-done.9, f32[6,4]{1,0:T(8,128)S(1)} %copy-done.7, f32[3,9216]{1,0:T(4,128)S(1)} %copy-done.2, ...), custom_call_target="tpu_custom_call" | custom-call | tf_op jit(solution)/shard_map/macro_last/pallas_call | solution.py:456
  52.2 2.1 %collective-permute-start = (f32[3,1024]{1,0:T(4,128)S(1)}, f32[3,1024]{1,0:T(4,128)S(1)}, u32[]{:S(2)}, u32[]{:S(2)}) collective-permute-start(f32[3,1024]{1,0:T(4,128)S(1)} %get-tuple-element.16), channel_id=1, source_target_pairs={{0,4},{4,8},{8,12},{12,16},{16,20},{20,24},{24,28},{28,32},{32,36}... | collective-permute-start | bytes 36872 | tf_op jit(solution)/shard_map/ppermute | solution.py:596
  54.3 5.6 %collective-permute-start.1 = (f32[3,1024]{1,0:T(4,128)S(1)}, f32[3,1024]{1,0:T(4,128)S(1)}, u32[]{:S(2)}, u32[]{:S(2)}) collective-permute-start(f32[3,1024]{1,0:T(4,128)S(1)} %get-tuple-element.17), channel_id=1, source_target_pairs={{4,0},{8,4},{12,8},{16,12},{20,16},{24,20},{28,24},{32,28},{36,32}... | collective-permute-start | bytes 36872 | tf_op jit(solution)/shard_map/ppermute | solution.py:597
  59.9 3.6 %collective-permute-start.2 = (f32[3,1024]{1,0:T(4,128)S(1)}, f32[3,1024]{1,0:T(4,128)S(1)}, u32[]{:S(2)}, u32[]{:S(2)}) collective-permute-start(f32[3,1024]{1,0:T(4,128)S(1)} %get-tuple-element.18), channel_id=1, source_target_pairs={{0,1},{1,2},{2,3},{4,5},{5,6},{6,7},{8,9},{9,10},{10,11},{12,13},{... | collective-permute-start | bytes 36872 | tf_op jit(solution)/shard_map/ppermute | solution.py:598
  63.5 2.2 %collective-permute-start.3 = (f32[3,1024]{1,0:T(4,128)S(1)}, f32[3,1024]{1,0:T(4,128)S(1)}, u32[]{:S(2)}, u32[]{:S(2)}) collective-permute-start(f32[3,1024]{1,0:T(4,128)S(1)} %get-tuple-element.19), channel_id=1, source_target_pairs={{1,0},{2,1},{3,2},{5,4},{6,5},{7,6},{9,8},{10,9},{11,10},{13,12},{... | collective-permute-start | bytes 36872 | tf_op jit(solution)/shard_map/ppermute | solution.py:599
  65.8 0.7 copy.19
  66.4 0.0 collective-permute-done.r0
  66.4 0.0 collective-permute-done.1.r1
  66.4 0.0 collective-permute-done.2.r2
  66.4 2.7 %collective-permute-done.3.r3 = f32[3,1024]{1,0:T(4,128)S(1)} collective-permute-done((f32[3,1024]{1,0:T(4,128)S(1)}, f32[3,1024]{1,0:T(4,128)S(1)}, u32[]{:S(2)}, u32[]{:S(2)}) %collective-permute-start.3) | collective-permute-done | bytes 12320 | tf_op jit(solution)/shard_map/ppermute | solution.py:599
  69.2 0.0 copy-done.4
  69.2 0.0 copy-done.8
  69.2 1.5 %assemble.1 = f32[3,9216]{1,0:T(4,128)} custom-call(f32[120,256]{1,0:T(8,128)S(1)} %get-tuple-element.15.own, s32[1,4,1024]{2,1,0:T(4,128)S(1)} %copy-done.6, f32[3,1024]{1,0:T(4,128)S(1)} %collective-permute-done.r0, f32[3,1024]{1,0:T(4,128)S(1)} %collective-permute-done.1.r1, f32[3,1024]{1,0:T(4,128)S(1)} %collective-permute-done.2.r2, ...), custom_call_target="tpu_custom_call" | custom-call | tf_op jit(solution)/shard_map/assemble/pallas_call | solution.py:491
  70.7 0.0 all-to-all-done.1.pieces
  70.7 0.0 copy-start.10
  70.7 0.7 copy-done.10
  71.4 1.7 %join_pieces.1 = f32[2,8,4096]{2,1,0:T(8,128)} custom-call(f32[32,2,8,128]{3,2,1,0:T(8,128)} %copy-done.10), custom_call_target="tpu_custom_call" | custom-call | tf_op jit(solution)/shard_map/join_pieces/pallas_call | solution.py:537
Async XLA Ops:
  1.3 18.2 %copy-start.2 = (f32[3,9216]{1,0:T(4,128)S(1)}, f32[3,9216]{1,0:T(4,128)}, u32[]{:S(2)}) copy-start(f32[3,9216]{1,0:T(4,128)} %disp.5) | copy-start | bytes 331780
  9.2 10.3 %copy-start = (f32[3,8,8192]{2,1,0:T(8,128)S(1)}, f32[3,8,8192]{2,1,0:T(8,128)}, u32[]{:S(2)}) copy-start(f32[3,8,8192]{2,1,0:T(8,128)} %grads.5) | copy-start | bytes 2359300
  9.2 10.3 %copy-start.1 = (s32[8,8192]{1,0:T(8,128)S(1)}, s32[8,8192]{1,0:T(8,128)}, u32[]{:S(2)}) copy-start(s32[8,8192]{1,0:T(8,128)} %nm.5) | copy-start | bytes 786436
  9.2 10.3 %copy-start.3 = (f32[2,8192]{1,0:T(2,128)S(1)}, f32[2,8192]{1,0:T(2,128)}, u32[]{:S(2)}) copy-start(f32[2,8192]{1,0:T(2,128)} %moduli.3) | copy-start | bytes 196612
  9.2 10.3 %copy-start.5 = (f32[8192]{0:T(1024)S(1)}, f32[8192]{0:T(1024)}, u32[]{:S(2)}) copy-start(f32[8192]{0:T(1024)} %param.17) | copy-start | bytes 98308
  9.3 10.3 %copy-start.7 = (f32[6,4]{1,0:T(8,128)S(1)}, f32[6,4]{1,0:T(8,128)}, u32[]{:S(2)}) copy-start(f32[6,4]{1,0:T(8,128)} %get-tuple-element.25.replace) | copy-start | bytes 292
  9.3 23.0 %all-to-all-start = ((f32[128,1,1152]{2,1,0:T(1,128)}), f32[128,1,1152]{2,1,0:T(1,128)S(1)}, u32[]{:S(2)}, u32[]{:S(2)}) async-start(f32[128,1,1152]{2,1,0:T(1,128)} %bitcast.8), calls=%async_computation | async-start | bytes 1179648 | tf_op jit(solution)/shard_map/all_to_all | solution.py:573
  19.5 0.7 copy-start.9
  33.6 6.5 %copy-start.6 = (s32[1,4,1024]{2,1,0:T(4,128)S(1)}, s32[1,4,1024]{2,1,0:T(4,128)}, u32[]{:S(2)}) copy-start(s32[1,4,1024]{2,1,0:T(4,128)} %shared.3) | copy-start | bytes 49156
  33.6 37.0 %all-to-all-start.1 = ((f32[32,2,8,128]{3,2,1,0:T(8,128)}), f32[32,2,8,128]{3,2,1,0:T(8,128)S(1)}, u32[]{:S(2)}, u32[]{:S(2)}) async-start(f32[32,2,8,128]{3,2,1,0:T(8,128)} %sort_pieces.1), calls=%async_computation.1 | async-start | bytes 524288 | tf_op jit(solution)/shard_map/all_to_all | solution.py:589
  40.2 29.0 %copy-start.4 = (f32[3,9216]{1,0:T(4,128)S(1)}, f32[3,9216]{1,0:T(4,128)}, u32[]{:S(2)}) copy-start(f32[3,9216]{1,0:T(4,128)} %external.1) | copy-start | bytes 331780
  40.2 29.0 %copy-start.8 = (f32[9216]{0:T(1024)S(1)}, f32[9216]{0:T(1024)}, u32[]{:S(2)}) copy-start(f32[9216]{0:T(1024)} %param.20) | copy-start | bytes 110596
  52.2 14.2 %collective-permute-start = (f32[3,1024]{1,0:T(4,128)S(1)}, f32[3,1024]{1,0:T(4,128)S(1)}, u32[]{:S(2)}, u32[]{:S(2)}) collective-permute-start(f32[3,1024]{1,0:T(4,128)S(1)} %get-tuple-element.16), channel_id=1, source_target_pairs={{0,4},{4,8},{8,12},{12,16},{16,20},{20,24},{24,28},{28,32},{32,36}... | collective-permute-start | bytes 36872 | tf_op jit(solution)/shard_map/ppermute | solution.py:596
  54.3 12.1 %collective-permute-start.1 = (f32[3,1024]{1,0:T(4,128)S(1)}, f32[3,1024]{1,0:T(4,128)S(1)}, u32[]{:S(2)}, u32[]{:S(2)}) collective-permute-start(f32[3,1024]{1,0:T(4,128)S(1)} %get-tuple-element.17), channel_id=1, source_target_pairs={{4,0},{8,4},{12,8},{16,12},{20,16},{24,20},{28,24},{32,28},{36,32}... | collective-permute-start | bytes 36872 | tf_op jit(solution)/shard_map/ppermute | solution.py:597
  59.9 6.5 %collective-permute-start.2 = (f32[3,1024]{1,0:T(4,128)S(1)}, f32[3,1024]{1,0:T(4,128)S(1)}, u32[]{:S(2)}, u32[]{:S(2)}) collective-permute-start(f32[3,1024]{1,0:T(4,128)S(1)} %get-tuple-element.18), channel_id=1, source_target_pairs={{0,1},{1,2},{2,3},{4,5},{5,6},{6,7},{8,9},{9,10},{10,11},{12,13},{... | collective-permute-start | bytes 36872 | tf_op jit(solution)/shard_map/ppermute | solution.py:598
  63.5 5.6 %collective-permute-start.3 = (f32[3,1024]{1,0:T(4,128)S(1)}, f32[3,1024]{1,0:T(4,128)S(1)}, u32[]{:S(2)}, u32[]{:S(2)}) collective-permute-start(f32[3,1024]{1,0:T(4,128)S(1)} %get-tuple-element.19), channel_id=1, source_target_pairs={{1,0},{2,1},{3,2},{5,4},{6,5},{7,6},{9,8},{10,9},{11,10},{13,12},{... | collective-permute-start | bytes 36872 | tf_op jit(solution)/shard_map/ppermute | solution.py:599
  70.7 0.7 copy-start.10

commit v3 on v2

--- a/solution.py
+++ b/solution.py
@@ -17,7 +17,9 @@
 HI = 40
 LO = 256
 UNROLL = 2
-SPLIT = 32
+SPLIT = 40
+BRICK = ("row", "pair", "core")
+BOTH = BRICK + ("pool",)
 VMEM = pltpu.VMEM
 SMEM = pltpu.SMEM
 f32 = jnp.float32
@@ -402,7 +404,24 @@
 
 
 def macro_last_kernel(
-    unroll, count, element, replace, disp, nm, grads, volumes, moduli, so_far, shared, own, f0, f1, f2, f3, sums
+    unroll,
+    count,
+    element,
+    replace,
+    core_index,
+    pool_index,
+    disp,
+    nm,
+    grads,
+    volumes,
+    moduli,
+    so_far,
+    shared,
+    own,
+    inner,
+    outer,
+    sums,
+    faces,
 ):
     sums[...] = so_far[...]
     macro_tiles(SPLIT, 64, unroll, count, element, replace, disp, nm, grads, volumes, moduli, sums)
@@ -411,7 +430,6 @@
         at = 2 * c * HI
         own[c * HI : (c + 1) * HI, :] = sums[at : at + HI, :] + sums[at + HI : at + 2 * HI, :]
 
-    faces = (f0, f1, f2, f3)
     for pair in range(4):
         first, second = 2 * pair, 2 * pair + 1
         node = jnp.concatenate(
@@ -433,10 +451,23 @@
                 picked[c] = jnp.where(hit, found, picked[c])
         for c in range(3):
             for face in range(4):
-                faces[face][c : c + 1, first * LANES : (first + 1) * LANES] = picked[c][face : face + 1]
-                faces[face][c : c + 1, second * LANES : (second + 1) * LANES] = picked[c][
+                faces[face, c : c + 1, first * LANES : (first + 1) * LANES] = picked[c][face : face + 1]
+                faces[face, c : c + 1, second * LANES : (second + 1) * LANES] = picked[c][
                     4 + face : 5 + face
                 ]
+    core, pool = core_index[0], pool_index[0]
+    pools = inner.shape[0] // 2
+    inner[...] = jnp.zeros_like(inner)
+    inner[(1 - core) * pools + pool] = faces[1 - core]
+    outer[...] = faces[core]
+
+    @pl.when(pool > 0)
+    def _():
+        inner[core * pools + pool - 1] = faces[2]
+
+    @pl.when(pool < pools - 1)
+    def _():
+        inner[core * pools + pool + 1] = faces[3]
 
 
 def macro_first(*arguments):
@@ -451,29 +482,44 @@
     )(*arguments)
 
 
-def macro_last(*arguments):
+def macro_last(pools, *arguments):
     vmem = pl.BlockSpec(memory_space=VMEM)
     return pl.pallas_call(
         functools.partial(macro_last_kernel, UNROLL),
-        out_shape=(jax.ShapeDtypeStruct((3 * HI, LO), f32),)
-        + (jax.ShapeDtypeStruct((3, 1024), f32),) * 4,
-        in_specs=[pl.BlockSpec(memory_space=SMEM)] * 3 + [vmem] * 7,
-        out_specs=(vmem,) * 5,
-        scratch_shapes=[VMEM((6 * HI, LO), f32)],
+        out_shape=(
+            jax.ShapeDtypeStruct((3 * HI, LO), f32),
+            jax.ShapeDtypeStruct((2 * pools, 3, 1024), f32),
+            jax.ShapeDtypeStruct((3, 1024), f32),
+        ),
+        in_specs=[pl.BlockSpec(memory_space=SMEM)] * 5 + [vmem] * 7,
+        out_specs=(vmem,) * 3,
+        scratch_shapes=[VMEM((6 * HI, LO), f32), VMEM((4, 3, 1024), f32)],
         compiler_params=pltpu.CompilerParams(vmem_limit_bytes=32 << 20),
         name="macro_last",
     )(*arguments)
 
 
-def assemble_kernel(own, shared, r0, r1, r2, r3, external, mass, out):
+def assemble_kernel(core_index, pool_index, own, shared, inner, outer, external, mass, out):
+    core, pool = core_index[0], pool_index[0]
+    pools = inner.shape[0] // 2
+    below, above = jnp.maximum(pool - 1, 0), jnp.minimum(pool + 1, pools - 1)
+    arrivals = (
+        (1 - core, True, lambda c, cols: inner[(1 - core) * pools + pool, c : c + 1, cols]),
+        (core, True, lambda c, cols: outer[c : c + 1, cols]),
+        (2, pool > 0, lambda c, cols: inner[core * pools + below, c : c + 1, cols]),
+        (3, pool < pools - 1, lambda c, cols: inner[core * pools + above, c : c + 1, cols]),
+    )
     total = None
-    for face, arrived in enumerate((r0, r1, r2, r3)):
+    for face, there, arrived in arrivals:
         for part in range(4):
             cols = slice(part * LO, (part + 1) * LO)
             values = []
             for c in range(3):
-                values += list(halves(arrived[c : c + 1, cols]))
-            left, right = one_hot_sum(shared[0, face : face + 1, cols], values, LO)
+                value = arrived(c, cols)
+                if there is not True:
+                    value = jnp.where(there, value, 0.0)
+                values += list(halves(value))
+            left, right = one_hot_sum(shared[0, pl.ds(face, 1), cols], values, LO)
             product = lax.dot_general(
                 left, right, (((1,), (1,)), ((), ())), preferred_element_type=f32
             )
@@ -486,16 +532,16 @@
     out[...] = (external[...] - out[...]) / mass[...]
 
 
-def assemble(own, shared, arrived, external, mass):
+def assemble(place, own, shared, inner, outer, external, mass):
     vmem = pl.BlockSpec(memory_space=VMEM)
     return pl.pallas_call(
         assemble_kernel,
         out_shape=jax.ShapeDtypeStruct(external.shape, f32),
-        in_specs=[vmem] * 8,
+        in_specs=[pl.BlockSpec(memory_space=SMEM)] * 2 + [vmem] * 6,
         out_specs=vmem,
         compiler_params=pltpu.CompilerParams(vmem_limit_bytes=32 << 20),
         name="assemble",
-    )(own, shared, *arrived, external, mass)
+    )(*place, own, shared, inner, outer, external, mass)
 
 
 def sort_kernel(pieces, out, order, places, sem):
@@ -557,8 +603,8 @@
     band_element,
     micro_fields,
 ):
-    both = ("brick", "pool")
-    bricks, pools = lax.axis_size("brick"), lax.axis_size("pool")
+    bricks, pools = lax.axis_size(BRICK), lax.axis_size("pool")
+    place = tuple(lax.axis_index(axis).astype(jnp.int32).reshape(1) for axis in ("core", "pool"))
     send, band_stress = solve_cells(
         band_count,
         band_owner,
@@ -571,58 +617,50 @@
         jnp.asarray(plane_tables()),
     )
     pieces = lax.all_to_all(
-        send.reshape(bricks * pools, 1, 9 * LANES), both, split_axis=0, concat_axis=0, tiled=True
+        send.reshape(bricks * pools, 1, 9 * LANES), BOTH, split_axis=0, concat_axis=0, tiled=True
     )
-    macro = (
-        band_count,
-        band_element,
-        band_stress,
-        displacement,
-        node_map,
-        shape_grads,
-        volumes.reshape(64, LANES),
-        elastic_moduli,
-    )
-    so_far = macro_first(*macro)
+    sparse = (band_count, band_element, band_stress)
+    dense = (displacement, node_map, shape_grads, volumes.reshape(64, LANES), elastic_moduli)
+    so_far = macro_first(*sparse, *dense)
     pieces, so_far = lax.optimization_barrier((pieces, so_far))
     sorted_pieces = sort_pieces(pieces.reshape(9 * bricks * pools, LANES), bricks)
-    mine = lax.all_to_all(sorted_pieces, "brick", split_axis=0, concat_axis=0, tiled=True)
-    own, f0, f1, f2, f3 = macro_last(*macro, so_far, shared_nodes)
-    up_b = [(i, i + 1) for i in range(bricks - 1)]
-    down_b = [(i + 1, i) for i in range(bricks - 1)]
-    up_p = [(i, i + 1) for i in range(pools - 1)]
-    down_p = [(i + 1, i) for i in range(pools - 1)]
-    arrived = (
-        lax.ppermute(f1, "brick", up_b),
-        lax.ppermute(f0, "brick", down_b),
-        lax.ppermute(f3, "pool", up_p),
-        lax.ppermute(f2, "pool", down_p),
+    sorted_pieces, so_far = lax.optimization_barrier((sorted_pieces, so_far))
+    mine = lax.all_to_all(sorted_pieces, BRICK, split_axis=0, concat_axis=0, tiled=True)
+    own, inner, outer = macro_last(pools, *sparse, *place, *dense, so_far, shared_nodes)
+    inner = lax.all_to_all(inner, ("core", "pool"), split_axis=0, concat_axis=0, tiled=True)
+    steps = [(i, i + 1) for i in range(1, bricks - 1, 2)]
+    outer = lax.ppermute(outer, BRICK, steps + [(j, i) for i, j in steps])
+    owned_fields = join_pieces(mine)
+    inner, outer, owned_fields = lax.optimization_barrier((inner, outer, owned_fields))
+    acceleration = assemble(
+        place, own, shared_nodes, inner, outer, external_force, nodal_mass.reshape(1, -1)
     )
-    acceleration = assemble(own, shared_nodes, arrived, external_force, nodal_mass.reshape(1, -1))
-    owned_fields = join_pieces(mine)
     return (acceleration, band_stress, owned_fields)
 
 
 def solution(mesh):
-    both = ("brick", "pool")
+    bricks, pools = mesh.devices.shape
+    split = jax.sharding.Mesh(
+        mesh.devices.reshape(4, bricks // 8, 2, pools), ("row", "pair", "core", "pool")
+    )
     placed = (
-        P(None, both),
-        P(None, both),
-        P(None, None, both),
-        P(both),
-        P(None, both),
-        P(None, both),
-        P(both),
-        P(both, None, None),
-        P(both),
-        P(both, None),
-        P(both, None),
-        P(both, None, None),
+        P(None, BOTH),
+        P(None, BOTH),
+        P(None, None, BOTH),
+        P(BOTH),
+        P(None, BOTH),
+        P(None, BOTH),
+        P(BOTH),
+        P(BOTH, None, None),
+        P(BOTH),
+        P(BOTH, None),
+        P(BOTH, None),
+        P(BOTH, None, None),
     )
     return jax.shard_map(
         shards,
-        mesh=mesh,
+        mesh=split,
         in_specs=placed,
-        out_specs=(P(None, both), P(None, both), P(both, None, None)),
+        out_specs=(P(None, BOTH), P(None, BOTH), P(BOTH, None, None)),
         check_vma=False,
     )

time: 73.7 us -> 68 us (0.923)
  waiting for transfers between devices: 3.75 us -> 0.44 us
  starting transfers between devices: 30.2 us -> 27.1 us
  Pallas kernels: 35.6 us -> 36.7 us
    ppermute x4 -> x1, starting transfers between devices: 13.5 us -> 4.33 us  [shards(): outer = lax.ppermute(outer, BRICK, steps + [(j, i) for i, j in steps])]
    all_to_all x2 -> x3, starting transfers between devices: 16.7 us -> 22.7 us  [the longest x1 10.2 us: shards(): lax.all_to_all(send.reshape(bricks * pools, 1, 9 * LANES), BOTH, split_ax...]
    pallas_call x1, Pallas kernels: 11.1 us -> 13.9 us  [macro_first(): pl.pallas_call(functools.partial(macro_first_kernel, UNROLL), out_shape=j...]
    ppermute x4 -> x1, waiting for transfers between devices: 2.75 us -> 0.44 us  [shards(): outer = lax.ppermute(outer, BRICK, steps + [(j, i) for i, j in steps])]
    pallas_call x1, Pallas kernels: 12 us -> 10.3 us  [macro_last(): pl.pallas_call(functools.partial(macro_last_kernel, UNROLL), out_shape=(j...]
    all_to_all x2 -> x3, waiting for transfers between devices: 1 us -> 0.01 us  [the longest x1 0.01 us: shards(): lax.all_to_all(send.reshape(bricks * pools, 1, 9 * LANES), BOTH, split_ax...]
  transfers between devices with their start and end apart: 6 -> 4, of which waited for: 2 -> 1; matrix products, arithmetic and copies ran while one was open for 1% -> 1% of each run, Pallas kernels for 34% -> 39%
where the time goes in v3:
time: 68 us; the launch traced here: 67 us
  Pallas kernels  36.7 us (54%)
  starting transfers between devices  27.1 us (40%)
  between operations  1.45 us (2%)
  local copies, waits for them, and re-layouts  1.3 us (2%)
    pallas_call x1, Pallas kernels, macro_first(): pl.pallas_call(functools.partial(macro_first_kernel, UNROLL), out_shape=j...  13.9 us
    pallas_call x1, Pallas kernels, macro_last(): pl.pallas_call(functools.partial(macro_last_kernel, UNROLL), out_shape=(j...  10.3 us
    all_to_all x1, starting transfers between devices, shards(): lax.all_to_all(send.reshape(bricks * pools, 1, 9 * LANES), BOTH, split_ax...  10.2 us
    pallas_call x1, Pallas kernels, solve_cells(): pl.pallas_call(cells_kernel, out_shape=(jax.ShapeDtypeStruct((36 * TILES,...  7.93 us
    all_to_all x1, starting transfers between devices, shards(): lax.all_to_all(sorted_pieces, BRICK, split_axis=0, concat_axis=0, tiled=T...  7.48 us
    all_to_all x1, starting transfers between devices, shards(): lax.all_to_all(inner, ('core', 'pool'), split_axis=0, concat_axis=0, tile...  5.08 us
    ppermute x1, starting transfers between devices, shards(): outer = lax.ppermute(outer, BRICK, steps + [(j, i) for i, j in steps])  4.33 us
    pallas_call x1, Pallas kernels, join_pieces(): pl.pallas_call(join_kernel, out_shape=jax.ShapeDtypeStruct((2, 8, NV), f3...  1.71 us
  transfers between devices with their start and end apart: 4, of which 1 were waited for; matrix products, arithmetic and copies ran while one was open for 1% of the time, Pallas kernels for 39%

profile of v3, /device:TPU:40, one launch (start us, length us, event | category | flops | bytes accessed | tf_op | source)
XLA Modules:
  0.0 67.0 jit_solution(5797557328262704605)
XLA Ops:
  1.3 0.0 copy-start.2
  1.3 7.9 %cells.1 = (f32[1152,128]{1,0:T(8,128)}, f32[6,4]{1,0:T(8,128)}) custom-call(s32[1]{0:T(128)S(6)} %copy.20.count, s32[1,4]{1,0:T(1,128)} %owner.1, s32[1,4]{1,0:T(1,128)} %element.5, f32[3,9216]{1,0:T(4,128)} %disp.5, s32[8,8192]{1,0:T(8,128)} %nm.5, f32[3,8,8192]{2,1,0:T(8,128)} %grads.5, f32[4,8,4096]{2,1,0:T(8,128)} %micro.1, ...), custom_call_target="tpu_custom_call" | custom-call | tf_op jit(solution)/shard_map/cells/pallas_call | solution.py:284
  9.2 0.0 copy-start
  9.2 0.0 copy-start.1
  9.2 0.0 copy-start.3
  9.2 0.0 copy-start.5
  9.2 0.0 copy-start.7
  9.3 10.2 %all-to-all-start = ((f32[128,1,1152]{2,1,0:T(1,128)}), f32[128,1,1152]{2,1,0:T(1,128)S(1)}, u32[]{:S(2)}, u32[]{:S(2)}) async-start(f32[128,1,1152]{2,1,0:T(1,128)} %bitcast.10), calls=%async_computation | async-start | bytes 1179648 | tf_op jit(solution)/shard_map/all_to_all | solution.py:619
  19.4 0.0 copy-start.9
  19.5 0.0 copy-done.2
  19.5 0.0 copy-done
  19.5 0.0 copy-done.1
  19.5 0.0 copy-done.3
  19.5 0.0 copy-done.5
  19.5 0.0 copy-done.7
  19.5 0.6 copy-done.9
  20.1 13.9 %macro_first.1.so_far = f32[240,256]{1,0:T(8,128)S(1)} custom-call(s32[1]{0:T(128)S(6)} %copy.20.count, s32[1,4]{1,0:T(1,128)S(1)} %copy-done.9, f32[6,4]{1,0:T(8,128)S(1)} %copy-done.7, f32[3,9216]{1,0:T(4,128)S(1)} %copy-done.2, s32[8,8192]{1,0:T(8,128)S(1)} %copy-done.1, f32[3,8,8192]{2,1,0:T(8,128)S(1)} %copy-done, f32[64,128]{1,0:T(8,128)S(1)} %bitcast.7, ...), custom_call_target="tpu_custom_call" | custom-call | tf_op jit(solution)/shard_map/macro_first/pallas_call | solution.py:475
  34.0 0.0 all-to-all-done
  34.1 1.4 %sort_pieces.1 = f32[32,2,8,128]{3,2,1,0:T(8,128)} custom-call(f32[1152,128]{1,0:T(8,128)S(1)} %bitcast.6), custom_call_target="tpu_custom_call" | custom-call | tf_op jit(solution)/shard_map/sort_pieces/pallas_call | solution.py:564
  35.5 0.0 copy-start.6
  35.5 7.5 %all-to-all-start.2 = ((f32[32,2,8,128]{3,2,1,0:T(8,128)}), f32[32,2,8,128]{3,2,1,0:T(8,128)S(1)}, u32[]{:S(2)}, u32[]{:S(2)}) async-start(f32[32,2,8,128]{3,2,1,0:T(8,128)} %sort_pieces.1), calls=%async_computation.2 | async-start | bytes 524288 | tf_op jit(solution)/shard_map/all_to_all | solution.py:628
  43.0 0.0 copy-done.6
  43.0 10.3 %macro_last.1 = (f32[120,256]{1,0:T(8,128)S(1)}, f32[8,3,1024]{2,1,0:T(4,128)}, f32[3,1024]{1,0:T(4,128)S(1)}) custom-call(s32[1]{0:T(128)S(6)} %copy.20.count, s32[1,4]{1,0:T(1,128)S(1)} %copy-done.9, f32[6,4]{1,0:T(8,128)S(1)} %copy-done.7, s32[1]{0:T(128)} %bitcast.core_index, s32[1]{0:T(128)} %bitcast.1.pool_index, f32[3,9216]{1,0:T(4,128)S(1)} %copy-done.2, ...), custom_call_target="tpu_custom_call" | custom-call | tf_op jit(solution)/shard_map/macro_last/pallas_call | solution.py:487
  53.3 0.0 all-to-all-done.2.pieces
  53.3 0.0 copy-start.10
  53.3 5.1 %all-to-all-start.1 = ((f32[8,3,1024]{2,1,0:T(4,128)}), f32[8,3,1024]{2,1,0:T(4,128)S(1)}, u32[]{:S(2)}, u32[]{:S(2)}) async-start(f32[8,3,1024]{2,1,0:T(4,128)} %get-tuple-element.21), calls=%async_computation.1 | async-start | bytes 262144 | tf_op jit(solution)/shard_map/all_to_all | solution.py:630
  58.3 4.3 %collective-permute-start = (f32[3,1024]{1,0:T(4,128)S(1)}, f32[3,1024]{1,0:T(4,128)S(1)}, u32[]{:S(2)}, u32[]{:S(2)}) collective-permute-start(f32[3,1024]{1,0:T(4,128)S(1)} %get-tuple-element.22), channel_id=1, source_target_pairs={{4,8},{12,16},{20,24},{28,32},{36,40},{44,48},{52,56},{60,64},{68,... | collective-permute-start | bytes 36872 | tf_op jit(solution)/shard_map/ppermute | solution.py:632
  62.7 0.7 copy.19
  63.3 0.0 copy-done.10
  63.3 0.0 copy-start.4
  63.3 0.0 copy-start.8
  63.3 1.7 %join_pieces.1 = f32[2,8,4096]{2,1,0:T(8,128)} custom-call(f32[32,2,8,128]{3,2,1,0:T(8,128)} %copy-done.10), custom_call_target="tpu_custom_call" | custom-call | tf_op jit(solution)/shard_map/join_pieces/pallas_call | solution.py:583
  65.1 0.4 collective-permute-done.outer
  65.5 0.0 all-to-all-done.1.inner
  65.5 0.0 copy-done.4
  65.5 0.0 copy-done.8
  65.5 1.5 %assemble.1 = f32[3,9216]{1,0:T(4,128)} custom-call(s32[1]{0:T(128)} %bitcast.core_index, s32[1]{0:T(128)} %bitcast.1.pool_index, f32[120,256]{1,0:T(8,128)S(1)} %get-tuple-element.20.own, s32[1,4,1024]{2,1,0:T(4,128)S(1)} %copy-done.6, f32[8,3,1024]{2,1,0:T(4,128)S(1)} %all-to-all-done.1.inner, f32[3,1024]{1,0:T(4,128)S(1)} %collective-permute-done.outer, ...), custom_call_target="tpu_custom_call" | custom-call | tf_op jit(solution)/shard_map/assemble/pallas_call | solution.py:537
Async XLA Ops:
  1.3 18.2 %copy-start.2 = (f32[3,9216]{1,0:T(4,128)S(1)}, f32[3,9216]{1,0:T(4,128)}, u32[]{:S(2)}) copy-start(f32[3,9216]{1,0:T(4,128)} %disp.5) | copy-start | bytes 331780
  9.2 10.3 %copy-start = (f32[3,8,8192]{2,1,0:T(8,128)S(1)}, f32[3,8,8192]{2,1,0:T(8,128)}, u32[]{:S(2)}) copy-start(f32[3,8,8192]{2,1,0:T(8,128)} %grads.5) | copy-start | bytes 2359300
  9.2 10.3 %copy-start.1 = (s32[8,8192]{1,0:T(8,128)S(1)}, s32[8,8192]{1,0:T(8,128)}, u32[]{:S(2)}) copy-start(s32[8,8192]{1,0:T(8,128)} %nm.5) | copy-start | bytes 786436
  9.2 10.3 %copy-start.3 = (f32[2,8192]{1,0:T(2,128)S(1)}, f32[2,8192]{1,0:T(2,128)}, u32[]{:S(2)}) copy-start(f32[2,8192]{1,0:T(2,128)} %moduli.3) | copy-start | bytes 196612
  9.2 10.3 %copy-start.5 = (f32[8192]{0:T(1024)S(1)}, f32[8192]{0:T(1024)}, u32[]{:S(2)}) copy-start(f32[8192]{0:T(1024)} %param.17) | copy-start | bytes 98308
  9.2 10.3 %copy-start.7 = (f32[6,4]{1,0:T(8,128)S(1)}, f32[6,4]{1,0:T(8,128)}, u32[]{:S(2)}) copy-start(f32[6,4]{1,0:T(8,128)} %get-tuple-element.31.replace) | copy-start | bytes 292
  9.3 24.8 %all-to-all-start = ((f32[128,1,1152]{2,1,0:T(1,128)}), f32[128,1,1152]{2,1,0:T(1,128)S(1)}, u32[]{:S(2)}, u32[]{:S(2)}) async-start(f32[128,1,1152]{2,1,0:T(1,128)} %bitcast.10), calls=%async_computation | async-start | bytes 1179648 | tf_op jit(solution)/shard_map/all_to_all | solution.py:619
  19.4 0.7 copy-start.9
  35.5 7.5 %copy-start.6 = (s32[1,4,1024]{2,1,0:T(4,128)S(1)}, s32[1,4,1024]{2,1,0:T(4,128)}, u32[]{:S(2)}) copy-start(s32[1,4,1024]{2,1,0:T(4,128)} %shared.3) | copy-start | bytes 49156
  35.5 17.8 %all-to-all-start.2 = ((f32[32,2,8,128]{3,2,1,0:T(8,128)}), f32[32,2,8,128]{3,2,1,0:T(8,128)S(1)}, u32[]{:S(2)}, u32[]{:S(2)}) async-start(f32[32,2,8,128]{3,2,1,0:T(8,128)} %sort_pieces.1), calls=%async_computation.2 | async-start | bytes 524288 | tf_op jit(solution)/shard_map/all_to_all | solution.py:628
  53.3 10.1 %copy-start.10 = (f32[32,2,8,128]{3,2,1,0:T(8,128)}, f32[32,2,8,128]{3,2,1,0:T(8,128)S(1)}, u32[]{:S(2)}) copy-start(f32[32,2,8,128]{3,2,1,0:T(8,128)S(1)} %all-to-all-done.2.pieces) | copy-start | bytes 786436
  53.3 12.2 %all-to-all-start.1 = ((f32[8,3,1024]{2,1,0:T(4,128)}), f32[8,3,1024]{2,1,0:T(4,128)S(1)}, u32[]{:S(2)}, u32[]{:S(2)}) async-start(f32[8,3,1024]{2,1,0:T(4,128)} %get-tuple-element.21), calls=%async_computation.1 | async-start | bytes 262144 | tf_op jit(solution)/shard_map/all_to_all | solution.py:630
  58.3 7.2 %collective-permute-start = (f32[3,1024]{1,0:T(4,128)S(1)}, f32[3,1024]{1,0:T(4,128)S(1)}, u32[]{:S(2)}, u32[]{:S(2)}) collective-permute-start(f32[3,1024]{1,0:T(4,128)S(1)} %get-tuple-element.22), channel_id=1, source_target_pairs={{4,8},{12,16},{20,24},{28,32},{36,40},{44,48},{52,56},{60,64},{68,... | collective-permute-start | bytes 36872 | tf_op jit(solution)/shard_map/ppermute | solution.py:632
  63.3 2.2 %copy-start.4 = (f32[3,9216]{1,0:T(4,128)S(1)}, f32[3,9216]{1,0:T(4,128)}, u32[]{:S(2)}) copy-start(f32[3,9216]{1,0:T(4,128)} %external.1) | copy-start | bytes 331780
  63.3 2.2 %copy-start.8 = (f32[9216]{0:T(1024)S(1)}, f32[9216]{0:T(1024)}, u32[]{:S(2)}) copy-start(f32[9216]{0:T(1024)} %param.20) | copy-start | bytes 110596

commit v4 on v3

--- a/solution.py
+++ b/solution.py
@@ -66,17 +66,41 @@
 
     ix, iy, iz = index[:, None, None], index[None, :, None], index[None, None, :]
     table = 0.5 * (operator(ix, iy, iz) + operator((-ix) % G, (-iy) % G, (-iz) % G)) / NV
-    return table.reshape(6, 8, G, G * G).transpose(2, 0, 1, 3).astype(np.float32)
+    table = table.reshape(6, 8, G, G * G).transpose(2, 0, 1, 3)
+    pairs, alone = half_plane()
+    even, odd = np.concatenate([pairs, alone[:2]]), np.concatenate([pairs, alone[2:]])
+    return np.stack([table[..., even], table[..., odd]]).astype(np.float32)
+
+
+def half_plane():
+    index = np.arange(G * G)
+    mirror = (-(index // G)) % G * G + (-(index % G)) % G
+    return index[index < mirror], index[index == mirror]
 
 
 def plane_tables():
+    pairs, alone = half_plane()
     plane = np.arange(G * G)
-    phase = (plane[:, None] // G * (plane[None, :] // G) + plane[:, None] % G * (plane[None, :] % G)) % G
+
+    def angle(k):
+        turns = (plane[:, None] // G * (k // G)[None, :] + plane[:, None] % G * (k % G)[None, :]) % G
+        return turns * (2 * np.pi / G)
+
+    there = np.concatenate(
+        [
+            np.cos(angle(pairs)),
+            np.cos(angle(alone[:2])),
+            -np.sin(angle(pairs)),
+            np.cos(angle(alone[2:])),
+        ],
+        axis=1,
+    )
+    weight = np.full((G * G, 1), 2.0)
+    weight[[126, 127, 254, 255]] = 1.0
     parts = []
-    for table in (np.cos(phase * (2 * np.pi / G)), np.sin(phase * (2 * np.pi / G))):
-        table = table.astype(np.float32)
-        high = table.astype(bf16)
-        parts += [high, (table - high.astype(np.float32)).astype(bf16)]
+    for table in (there, weight * there.T):
+        high = table.astype(np.float32).astype(bf16)
+        parts += [high, (table - high.astype(np.float64)).astype(np.float32).astype(bf16)]
     return np.stack(parts)
 
 
@@ -136,24 +160,16 @@
     return twice * d + jnp.where(first_rows, lam_trace, 0.0)
 
 
-def plane_products(sr, si, cmat):
-    x = jnp.concatenate([sr[...], si[...]], axis=0)
+def plane_product(x, cmat, at):
     high = x.astype(bf16)
     low = (x - high.astype(f32)).astype(bf16)
-
-    def times(at):
-        a, b = cmat[at], cmat[at + 1]
-        return (
-            jnp.dot(high, a, preferred_element_type=f32)
-            + jnp.dot(low, a, preferred_element_type=f32)
-            + jnp.dot(high, b, preferred_element_type=f32)
-        )
-
-    return times(0), times(2)
+    rows = x.shape[0]
+    both = jnp.dot(jnp.concatenate([high, low], axis=0), cmat[at], preferred_element_type=f32)
+    return both[:rows] + both[rows:] + jnp.dot(high, cmat[at + 1], preferred_element_type=f32)
 
 
 def cells_kernel(
-    count, owner, element, disp, nm, grads, micro, green, cmat, send, band_stress, st, sr, si
+    count, owner, element, disp, nm, grads, micro, green, cmat, send, band_stress, st, *work
 ):
     half_rows = 8 * G
     lane = lax.broadcasted_iota(jnp.int32, (8, LANES), 1)
@@ -211,49 +227,65 @@
         shift = jnp.where(row < 6, targets[k] - mean, 0.0)
         shifts.append(jnp.concatenate([shift, shift], axis=1))
 
+    re_cols, im_cols = slice(0, LANES), slice(LANES, 2 * LANES)
+    own_mirror = lane >= 126
+    whole_mirror = lax.broadcasted_iota(jnp.int32, (half_rows, LANES), 1) >= 126
     for iteration in range(ITERS):
         for pair in range(2):
-            for x in range(G):
-                at = pair * half_rows + 8 * x
-                sr[at : at + 8, :] = slab_stress(slab(2 * pair, x, iteration), first_rows)
-                si[at : at + 8, :] = slab_stress(slab(2 * pair + 1, x, iteration), first_rows)
-        by_cos, by_sin = plane_products(sr, si, cmat)
-        rows = 2 * half_rows
-        sr[...] = by_cos[:rows] + by_sin[rows:]
-        si[...] = by_cos[rows:] - by_sin[:rows]
-        for pair in range(2):
-            for part in range(2):
-                cols = slice(part * LANES, (part + 1) * LANES)
-                at = [pair * half_rows + 8 * x for x in range(G)]
-                values = dft16([(sr[a : a + 8, cols], si[a : a + 8, cols]) for a in at], -1)
+            plane, spectrum = work[2 * pair], work[2 * pair + 1]
+            at = [[cell * half_rows + 8 * x for x in range(G)] for cell in range(2)]
+            for cell in range(2):
                 for x in range(G):
-                    sr[at[x] : at[x] + 8, cols] = values[x][0]
-                    si[at[x] : at[x] + 8, cols] = values[x][1]
+                    a = at[cell][x]
+                    plane[a : a + 8, :] = slab_stress(slab(2 * pair + cell, x, iteration), first_rows)
+            plane[...] = plane_product(plane[...], cmat, 0)
+            for cell in range(2):
+                values = []
+                for x in range(G):
+                    a = at[cell][x]
+                    re, im = plane[a : a + 8, re_cols], plane[a : a + 8, im_cols]
+                    if cell == 0:
+                        other = at[1][x]
+                        im = jnp.where(own_mirror, plane[other : other + 8, re_cols], im)
+                    else:
+                        other = at[0][x]
+                        re = jnp.where(own_mirror, plane[other : other + 8, im_cols], re)
+                    values.append((re, im))
+                values = dft16(values, -1)
+                for x in range(G):
+                    a = at[cell][x]
+                    spectrum[a : a + 8, re_cols] = values[x][0]
+                    spectrum[a : a + 8, im_cols] = values[x][1]
+            for cell in range(2):
                 updates = []
                 for x in range(G):
                     re = im = None
                     for j in range(6):
-                        weight = green[x, j, :, cols]
-                        tr = weight * jnp.broadcast_to(sr[at[x] + j : at[x] + j + 1, cols], (8, LANES))
-                        ti = weight * jnp.broadcast_to(si[at[x] + j : at[x] + j + 1, cols], (8, LANES))
+                        weight = green[cell, x, j]
+                        a = at[cell][x] + j
+                        tr = weight * jnp.broadcast_to(spectrum[a : a + 1, re_cols], (8, LANES))
+                        ti = weight * jnp.broadcast_to(spectrum[a : a + 1, im_cols], (8, LANES))
                         re = tr if re is None else re + tr
                         im = ti if im is None else im + ti
                     updates.append((re, im))
                 values = dft16(updates, 1)
                 for x in range(G):
-                    sr[at[x] : at[x] + 8, cols] = values[x][0]
-                    si[at[x] : at[x] + 8, cols] = values[x][1]
-        by_cos, by_sin = plane_products(sr, si, cmat)
-        sr[...] = by_cos[:rows] - by_sin[rows:]
-        si[...] = by_cos[rows:] + by_sin[:rows]
-        for k in range(4):
-            source = (sr, si)[k % 2]
-            for x in range(G):
-                at = k // 2 * half_rows + 8 * x
-                value = slab(k, x, iteration) - source[at : at + 8, :]
-                if iteration == 0:
-                    value = value + shifts[k]
-                st[k, 8 * x : 8 * x + 8, :] = value
+                    a = at[cell][x]
+                    plane[a : a + 8, re_cols] = values[x][0]
+                    plane[a : a + 8, im_cols] = values[x][1]
+            first_im = plane[:half_rows, im_cols]
+            second_re = plane[half_rows:, re_cols]
+            plane[:half_rows, im_cols] = jnp.where(whole_mirror, second_re, first_im)
+            plane[half_rows:, re_cols] = jnp.where(whole_mirror, first_im, second_re)
+            update = plane_product(plane[...], cmat, 2)
+            for cell in range(2):
+                k = 2 * pair + cell
+                for x in range(G):
+                    a = at[cell][x]
+                    value = slab(k, x, iteration) - update[a : a + 8, :]
+                    if iteration == 0:
+                        value = value + shifts[k]
+                    st[k, 8 * x : 8 * x + 8, :] = value
 
     send[pl.ds(8, 4 * TILES, stride=9), :] = jnp.full((4 * TILES, LANES), -1.0, f32)
     result = jnp.zeros((8, LANES), f32)
@@ -280,7 +312,6 @@
 
 
 def solve_cells(count, owner, element, disp, nm, grads, micro, green, cmat):
-    rows = 16 * G
     return pl.pallas_call(
         cells_kernel,
         out_shape=(
@@ -291,9 +322,8 @@
         out_specs=(pl.BlockSpec(memory_space=VMEM), pl.BlockSpec(memory_space=VMEM)),
         scratch_shapes=[
             VMEM((4, 8 * G, 2 * LANES), f32),
-            VMEM((rows, 2 * LANES), f32),
-            VMEM((rows, 2 * LANES), f32),
-        ],
+        ]
+        + [VMEM((16 * G, 2 * LANES), f32)] * 4,
         compiler_params=pltpu.CompilerParams(vmem_limit_bytes=56 << 20),
         name="cells",
     )(count, owner, element, disp, nm, grads, micro, green, cmat)

time: 68 us -> 65.5 us (0.963)
  Pallas kernels: 36.7 us -> 34.2 us
    pallas_call x1, Pallas kernels: 7.93 us -> 5.41 us  [solve_cells(): pl.pallas_call(cells_kernel, out_shape=(jax.ShapeDtypeStruct((36 * TILES,...]
  transfers between devices with their start and end apart: 4 -> 4, of which waited for: 1 -> 1; matrix products, arithmetic and copies ran while one was open for 1% -> 1% of each run, Pallas kernels for 39% -> 40%
where the time goes in v4:
time: 65.5 us; the launch traced here: 64.4 us
  Pallas kernels  34.2 us (52%)
  starting transfers between devices  27.1 us (41%)
  between operations  1.45 us (2%)
  local copies, waits for them, and re-layouts  1.3 us (2%)
    pallas_call x1, Pallas kernels, macro_first(): pl.pallas_call(functools.partial(macro_first_kernel, UNROLL), out_shape=j...  13.9 us
    pallas_call x1, Pallas kernels, macro_last(): pl.pallas_call(functools.partial(macro_last_kernel, UNROLL), out_shape=(j...  10.3 us
    all_to_all x1, starting transfers between devices, shards(): lax.all_to_all(send.reshape(bricks * pools, 1, 9 * LANES), BOTH, split_ax...  10.2 us
    all_to_all x1, starting transfers between devices, shards(): lax.all_to_all(sorted_pieces, BRICK, split_axis=0, concat_axis=0, tiled=T...  7.48 us
    pallas_call x1, Pallas kernels, solve_cells(): pl.pallas_call(cells_kernel, out_shape=(jax.ShapeDtypeStruct((36 * TILES,...  5.41 us
    all_to_all x1, starting transfers between devices, shards(): lax.all_to_all(inner, ('core', 'pool'), split_axis=0, concat_axis=0, tile...  5.07 us
    ppermute x1, starting transfers between devices, shards(): outer = lax.ppermute(outer, BRICK, steps + [(j, i) for i, j in steps])  4.33 us
    pallas_call x1, Pallas kernels, join_pieces(): pl.pallas_call(join_kernel, out_shape=jax.ShapeDtypeStruct((2, 8, NV), f3...  1.71 us
  transfers between devices with their start and end apart: 4, of which 1 were waited for; matrix products, arithmetic and copies ran while one was open for 1% of the time, Pallas kernels for 40%

profile of v4, /device:TPU:40, one launch (start us, length us, event | category | flops | bytes accessed | tf_op | source)
XLA Modules:
  0.0 64.4 jit_solution(12291796544869866264)
XLA Ops:
  1.3 0.0 copy-start.2
  1.3 5.4 %cells.1 = (f32[1152,128]{1,0:T(8,128)}, f32[6,4]{1,0:T(8,128)}) custom-call(s32[1]{0:T(128)S(6)} %copy.20.count, s32[1,4]{1,0:T(1,128)} %owner.1, s32[1,4]{1,0:T(1,128)} %element.5, f32[3,9216]{1,0:T(4,128)} %disp.5, s32[8,8192]{1,0:T(8,128)} %nm.5, f32[3,8,8192]{2,1,0:T(8,128)} %grads.5, f32[4,8,4096]{2,1,0:T(8,128)} %micro.1, ...), custom_call_target="tpu_custom_call" | custom-call | tf_op jit(solution)/shard_map/cells/pallas_call | solution.py:315
  6.7 0.0 copy-start
  6.7 0.0 copy-start.1
  6.7 0.0 copy-start.3
  6.7 0.0 copy-start.5
  6.7 0.0 copy-start.7
  6.7 10.2 %all-to-all-start = ((f32[128,1,1152]{2,1,0:T(1,128)}), f32[128,1,1152]{2,1,0:T(1,128)S(1)}, u32[]{:S(2)}, u32[]{:S(2)}) async-start(f32[128,1,1152]{2,1,0:T(1,128)} %bitcast.10), calls=%async_computation | async-start | bytes 1179648 | tf_op jit(solution)/shard_map/all_to_all | solution.py:649
  16.9 0.0 copy-start.9
  16.9 0.0 copy-done.2
  16.9 0.0 copy-done
  17.0 0.0 copy-done.1
  17.0 0.0 copy-done.3
  17.0 0.0 copy-done.5
  17.0 0.0 copy-done.7
  17.0 0.6 copy-done.9
  17.6 13.9 %macro_first.1.so_far = f32[240,256]{1,0:T(8,128)S(1)} custom-call(s32[1]{0:T(128)S(6)} %copy.20.count, s32[1,4]{1,0:T(1,128)S(1)} %copy-done.9, f32[6,4]{1,0:T(8,128)S(1)} %copy-done.7, f32[3,9216]{1,0:T(4,128)S(1)} %copy-done.2, s32[8,8192]{1,0:T(8,128)S(1)} %copy-done.1, f32[3,8,8192]{2,1,0:T(8,128)S(1)} %copy-done, f32[64,128]{1,0:T(8,128)S(1)} %bitcast.7, ...), custom_call_target="tpu_custom_call" | custom-call | tf_op jit(solution)/shard_map/macro_first/pallas_call | solution.py:505
  31.5 0.0 all-to-all-done
  31.5 1.4 %sort_pieces.1 = f32[32,2,8,128]{3,2,1,0:T(8,128)} custom-call(f32[1152,128]{1,0:T(8,128)S(1)} %bitcast.6), custom_call_target="tpu_custom_call" | custom-call | tf_op jit(solution)/shard_map/sort_pieces/pallas_call | solution.py:594
  32.9 0.0 copy-start.6
  33.0 7.5 %all-to-all-start.2 = ((f32[32,2,8,128]{3,2,1,0:T(8,128)}), f32[32,2,8,128]{3,2,1,0:T(8,128)S(1)}, u32[]{:S(2)}, u32[]{:S(2)}) async-start(f32[32,2,8,128]{3,2,1,0:T(8,128)} %sort_pieces.1), calls=%async_computation.2 | async-start | bytes 524288 | tf_op jit(solution)/shard_map/all_to_all | solution.py:658
  40.4 0.0 copy-done.6
  40.5 10.3 %macro_last.1 = (f32[120,256]{1,0:T(8,128)S(1)}, f32[8,3,1024]{2,1,0:T(4,128)}, f32[3,1024]{1,0:T(4,128)S(1)}) custom-call(s32[1]{0:T(128)S(6)} %copy.20.count, s32[1,4]{1,0:T(1,128)S(1)} %copy-done.9, f32[6,4]{1,0:T(8,128)S(1)} %copy-done.7, s32[1]{0:T(128)} %bitcast.core_index, s32[1]{0:T(128)} %bitcast.1.pool_index, f32[3,9216]{1,0:T(4,128)S(1)} %copy-done.2, ...), custom_call_target="tpu_custom_call" | custom-call | tf_op jit(solution)/shard_map/macro_last/pallas_call | solution.py:517
  50.7 0.0 all-to-all-done.2.pieces
  50.7 0.0 copy-start.10
  50.7 5.1 %all-to-all-start.1 = ((f32[8,3,1024]{2,1,0:T(4,128)}), f32[8,3,1024]{2,1,0:T(4,128)S(1)}, u32[]{:S(2)}, u32[]{:S(2)}) async-start(f32[8,3,1024]{2,1,0:T(4,128)} %get-tuple-element.21), calls=%async_computation.1 | async-start | bytes 262144 | tf_op jit(solution)/shard_map/all_to_all | solution.py:660
  55.8 4.3 %collective-permute-start = (f32[3,1024]{1,0:T(4,128)S(1)}, f32[3,1024]{1,0:T(4,128)S(1)}, u32[]{:S(2)}, u32[]{:S(2)}) collective-permute-start(f32[3,1024]{1,0:T(4,128)S(1)} %get-tuple-element.22), channel_id=1, source_target_pairs={{4,8},{12,16},{20,24},{28,32},{36,40},{44,48},{52,56},{60,64},{68,... | collective-permute-start | bytes 36872 | tf_op jit(solution)/shard_map/ppermute | solution.py:662
  60.1 0.7 %copy.19 = f32[6,4]{0,1:T(4,128)} copy(f32[6,4]{1,0:T(8,128)S(1)} %copy-done.7) | data formatting | bytes 192
  60.8 0.0 copy-done.10
  60.8 0.0 copy-start.4
  60.8 0.0 copy-start.8
  60.8 1.7 %join_pieces.1 = f32[2,8,4096]{2,1,0:T(8,128)} custom-call(f32[32,2,8,128]{3,2,1,0:T(8,128)} %copy-done.10), custom_call_target="tpu_custom_call" | custom-call | tf_op jit(solution)/shard_map/join_pieces/pallas_call | solution.py:613
  62.5 0.4 collective-permute-done.outer
  63.0 0.0 all-to-all-done.1.inner
  63.0 0.0 copy-done.4
  63.0 0.0 copy-done.8
  63.0 1.5 %assemble.1 = f32[3,9216]{1,0:T(4,128)} custom-call(s32[1]{0:T(128)} %bitcast.core_index, s32[1]{0:T(128)} %bitcast.1.pool_index, f32[120,256]{1,0:T(8,128)S(1)} %get-tuple-element.20.own, s32[1,4,1024]{2,1,0:T(4,128)S(1)} %copy-done.6, f32[8,3,1024]{2,1,0:T(4,128)S(1)} %all-to-all-done.1.inner, f32[3,1024]{1,0:T(4,128)S(1)} %collective-permute-done.outer, ...), custom_call_target="tpu_custom_call" | custom-call | tf_op jit(solution)/shard_map/assemble/pallas_call | solution.py:567
Async XLA Ops:
  1.3 15.7 %copy-start.2 = (f32[3,9216]{1,0:T(4,128)S(1)}, f32[3,9216]{1,0:T(4,128)}, u32[]{:S(2)}) copy-start(f32[3,9216]{1,0:T(4,128)} %disp.5) | copy-start | bytes 331780
  6.7 10.3 %copy-start = (f32[3,8,8192]{2,1,0:T(8,128)S(1)}, f32[3,8,8192]{2,1,0:T(8,128)}, u32[]{:S(2)}) copy-start(f32[3,8,8192]{2,1,0:T(8,128)} %grads.5) | copy-start | bytes 2359300
  6.7 10.3 %copy-start.1 = (s32[8,8192]{1,0:T(8,128)S(1)}, s32[8,8192]{1,0:T(8,128)}, u32[]{:S(2)}) copy-start(s32[8,8192]{1,0:T(8,128)} %nm.5) | copy-start | bytes 786436
  6.7 10.3 %copy-start.3 = (f32[2,8192]{1,0:T(2,128)S(1)}, f32[2,8192]{1,0:T(2,128)}, u32[]{:S(2)}) copy-start(f32[2,8192]{1,0:T(2,128)} %moduli.3) | copy-start | bytes 196612
  6.7 10.3 %copy-start.5 = (f32[8192]{0:T(1024)S(1)}, f32[8192]{0:T(1024)}, u32[]{:S(2)}) copy-start(f32[8192]{0:T(1024)} %param.17) | copy-start | bytes 98308
  6.7 10.3 %copy-start.7 = (f32[6,4]{1,0:T(8,128)S(1)}, f32[6,4]{1,0:T(8,128)}, u32[]{:S(2)}) copy-start(f32[6,4]{1,0:T(8,128)} %get-tuple-element.31.replace) | copy-start | bytes 292
  6.7 24.8 %all-to-all-start = ((f32[128,1,1152]{2,1,0:T(1,128)}), f32[128,1,1152]{2,1,0:T(1,128)S(1)}, u32[]{:S(2)}, u32[]{:S(2)}) async-start(f32[128,1,1152]{2,1,0:T(1,128)} %bitcast.10), calls=%async_computation | async-start | bytes 1179648 | tf_op jit(solution)/shard_map/all_to_all | solution.py:649
  16.9 0.7 %copy-start.9 = (s32[1,4]{1,0:T(1,128)S(1)}, s32[1,4]{1,0:T(1,128)}, u32[]{:S(2)}) copy-start(s32[1,4]{1,0:T(1,128)} %element.5) | copy-start | bytes 52
  32.9 7.5 %copy-start.6 = (s32[1,4,1024]{2,1,0:T(4,128)S(1)}, s32[1,4,1024]{2,1,0:T(4,128)}, u32[]{:S(2)}) copy-start(s32[1,4,1024]{2,1,0:T(4,128)} %shared.3) | copy-start | bytes 49156
  33.0 17.8 %all-to-all-start.2 = ((f32[32,2,8,128]{3,2,1,0:T(8,128)}), f32[32,2,8,128]{3,2,1,0:T(8,128)S(1)}, u32[]{:S(2)}, u32[]{:S(2)}) async-start(f32[32,2,8,128]{3,2,1,0:T(8,128)} %sort_pieces.1), calls=%async_computation.2 | async-start | bytes 524288 | tf_op jit(solution)/shard_map/all_to_all | solution.py:658
  50.7 10.1 %copy-start.10 = (f32[32,2,8,128]{3,2,1,0:T(8,128)}, f32[32,2,8,128]{3,2,1,0:T(8,128)S(1)}, u32[]{:S(2)}) copy-start(f32[32,2,8,128]{3,2,1,0:T(8,128)S(1)} %all-to-all-done.2.pieces) | copy-start | bytes 786436
  50.7 12.2 %all-to-all-start.1 = ((f32[8,3,1024]{2,1,0:T(4,128)}), f32[8,3,1024]{2,1,0:T(4,128)S(1)}, u32[]{:S(2)}, u32[]{:S(2)}) async-start(f32[8,3,1024]{2,1,0:T(4,128)} %get-tuple-element.21), calls=%async_computation.1 | async-start | bytes 262144 | tf_op jit(solution)/shard_map/all_to_all | solution.py:660
  55.8 7.2 %collective-permute-start = (f32[3,1024]{1,0:T(4,128)S(1)}, f32[3,1024]{1,0:T(4,128)S(1)}, u32[]{:S(2)}, u32[]{:S(2)}) collective-permute-start(f32[3,1024]{1,0:T(4,128)S(1)} %get-tuple-element.22), channel_id=1, source_target_pairs={{4,8},{12,16},{20,24},{28,32},{36,40},{44,48},{52,56},{60,64},{68,... | collective-permute-start | bytes 36872 | tf_op jit(solution)/shard_map/ppermute | solution.py:662
  60.8 2.2 %copy-start.4 = (f32[3,9216]{1,0:T(4,128)S(1)}, f32[3,9216]{1,0:T(4,128)}, u32[]{:S(2)}) copy-start(f32[3,9216]{1,0:T(4,128)} %external.1) | copy-start | bytes 331780
  60.8 2.2 %copy-start.8 = (f32[9216]{0:T(1024)S(1)}, f32[9216]{0:T(1024)}, u32[]{:S(2)}) copy-start(f32[9216]{0:T(1024)} %param.20) | copy-start | bytes 110596

commit v5 on v4

--- a/solution.py
+++ b/solution.py
@@ -16,8 +16,10 @@
 TILES = 32
 HI = 40
 LO = 256
-UNROLL = 2
-SPLIT = 40
+STEPS = float((1 << 20) - 2)
+OFFSET = 1 << 20
+UNROLL = 4
+SPLIT = 48
 BRICK = ("row", "pair", "core")
 BOTH = BRICK + ("pool",)
 VMEM = pltpu.VMEM
@@ -169,7 +171,7 @@
 
 
 def cells_kernel(
-    count, owner, element, disp, nm, grads, micro, green, cmat, send, band_stress, st, *work
+    count, owner, element, disp, nm, grads, micro, green, cmat, send, band_stress, replace, st, *work
 ):
     half_rows = 8 * G
     lane = lax.broadcasted_iota(jnp.int32, (8, LANES), 1)
@@ -309,6 +311,10 @@
             send[pl.ds(9 * pool + 8, TILES, stride=36), :] = jnp.full((TILES, LANES), brick, f32)
 
     band_stress[...] = result[0:6, 0:4]
+    for k in range(4):
+        live_element = jnp.where(k < count[0], element[0, k], -1).astype(f32)
+        result = jnp.where((lane == k) & (row == 6), live_element, result)
+    replace[...] = result[:, 0:4]
 
 
 def solve_cells(count, owner, element, disp, nm, grads, micro, green, cmat):
@@ -317,9 +323,10 @@
         out_shape=(
             jax.ShapeDtypeStruct((36 * TILES, LANES), f32),
             jax.ShapeDtypeStruct((6, 4), f32),
+            jax.ShapeDtypeStruct((8, 4), f32),
         ),
         in_specs=[pl.BlockSpec(memory_space=SMEM)] * 3 + [pl.BlockSpec(memory_space=VMEM)] * 6,
-        out_specs=(pl.BlockSpec(memory_space=VMEM), pl.BlockSpec(memory_space=VMEM)),
+        out_specs=(pl.BlockSpec(memory_space=VMEM),) * 3,
         scratch_shapes=[
             VMEM((4, 8 * G, 2 * LANES), f32),
         ]
@@ -346,9 +353,30 @@
     return high, value - high
 
 
-def macro_tiles(begin, end, unroll, count, element, replace, disp, nm, grads, volumes, moduli, sums):
-    lane = lax.broadcasted_iota(jnp.int32, (1, LANES), 1)
-    live = [k < count[0] for k in range(4)]
+def pack_table(disp, table, step):
+    largest = jnp.zeros((3, LANES), f32)
+    for r in range(72):
+        largest = jnp.maximum(largest, jnp.abs(disp[:, r * LANES : (r + 1) * LANES]))
+    largest = jnp.maximum(jnp.max(largest, axis=0, keepdims=True), 1e-30)
+    step[...] = largest * (1.0 / STEPS)
+    scale = jnp.broadcast_to(STEPS / largest, (3, LANES))
+    for r in range(72):
+        cols = slice(r * LANES, (r + 1) * LANES)
+        level = jnp.floor(disp[:, cols] * scale + (OFFSET + 0.5)).astype(jnp.int32)
+        last = level[2:3]
+        parts = jnp.concatenate([(last & 0x7FF) << 21, (last >> 11) << 21], axis=0)
+        table[:, cols] = level[0:2] | parts
+
+
+def unpack(first, second, step):
+    mask = (1 << 21) - 1
+    last = lax.shift_right_logical(first, 21) | (lax.shift_right_logical(second, 21) << 11)
+    return [(level - OFFSET).astype(f32) * step for level in (first & mask, second & mask, last)]
+
+
+def macro_tiles(begin, end, unroll, replace, table, step_of, nm, grads, volumes, moduli, sums):
+    lane = lax.broadcasted_iota(jnp.int32, (1, LANES), 1).astype(f32)
+    steps = jnp.broadcast_to(step_of[...], (8, LANES))
 
     def scatter(node, forces):
         values = []
@@ -374,13 +402,14 @@
         cols = pl.ds(pl.multiple_of(t * LANES, LANES), LANES)
         node = nm[:, cols]
         hi, lo = node >> 7, node & 127
-        u = [jnp.zeros((8, LANES), f32) for _ in range(3)]
+        words = [jnp.zeros((8, LANES), jnp.int32) for _ in range(2)]
         for r in range(72):
             hit = hi == r
-            for c in range(3):
-                values = jnp.broadcast_to(disp[c : c + 1, r * LANES : (r + 1) * LANES], (8, LANES))
+            for w in range(2):
+                values = jnp.broadcast_to(table[w : w + 1, r * LANES : (r + 1) * LANES], (8, LANES))
                 found = jnp.take_along_axis(values, lo, axis=1, mode="promise_in_bounds")
-                u[c] = jnp.where(hit, found, u[c])
+                words[w] = jnp.where(hit, found, words[w])
+        u = unpack(*words, jnp.take_along_axis(steps, lo, axis=1, mode="promise_in_bounds"))
         g = [grads[j, :, cols] for j in range(3)]
 
         def total(value):
@@ -401,7 +430,7 @@
         stress = [spherical + 2.0 * mu * strain[c] for c in range(3)]
         stress += [2.0 * mu * strain[c] for c in range(3, 6)]
         for k in range(4):
-            hit = (lane + t * LANES == element[0, k]) & live[k]
+            hit = lane == replace[6, k] - lax.convert_element_type(t * LANES, f32)
             stress = [jnp.where(hit, replace[c, k], stress[c]) for c in range(6)]
         xx, yy, zz, yz, xz, xy = [
             jnp.broadcast_to(component * volume, (8, LANES)) for component in stress
@@ -428,19 +457,19 @@
     add(lax.fori_loop(1, (end - begin) // unroll, body, group(0)))
 
 
-def macro_first_kernel(unroll, count, element, replace, disp, nm, grads, volumes, moduli, sums):
+def macro_first_kernel(unroll, replace, disp, nm, grads, volumes, moduli, sums, table, step):
+    pack_table(disp, table, step)
     sums[...] = jnp.zeros_like(sums)
-    macro_tiles(0, SPLIT, unroll, count, element, replace, disp, nm, grads, volumes, moduli, sums)
+    macro_tiles(0, SPLIT, unroll, replace, table, step, nm, grads, volumes, moduli, sums)
 
 
 def macro_last_kernel(
     unroll,
-    count,
-    element,
     replace,
     core_index,
     pool_index,
-    disp,
+    table,
+    step,
     nm,
     grads,
     volumes,
@@ -454,7 +483,7 @@
     faces,
 ):
     sums[...] = so_far[...]
-    macro_tiles(SPLIT, 64, unroll, count, element, replace, disp, nm, grads, volumes, moduli, sums)
+    macro_tiles(SPLIT, 64, unroll, replace, table, step, nm, grads, volumes, moduli, sums)
 
     for c in range(3):
         at = 2 * c * HI
@@ -504,9 +533,13 @@
     vmem = pl.BlockSpec(memory_space=VMEM)
     return pl.pallas_call(
         functools.partial(macro_first_kernel, UNROLL),
-        out_shape=jax.ShapeDtypeStruct((6 * HI, LO), f32),
-        in_specs=[pl.BlockSpec(memory_space=SMEM)] * 3 + [vmem] * 5,
-        out_specs=vmem,
+        out_shape=(
+            jax.ShapeDtypeStruct((6 * HI, LO), f32),
+            jax.ShapeDtypeStruct((2, 72 * LANES), jnp.int32),
+            jax.ShapeDtypeStruct((1, LANES), f32),
+        ),
+        in_specs=[pl.BlockSpec(memory_space=SMEM)] + [vmem] * 5,
+        out_specs=(vmem,) * 3,
         compiler_params=pltpu.CompilerParams(vmem_limit_bytes=32 << 20),
         name="macro_first",
     )(*arguments)
@@ -521,7 +554,7 @@
             jax.ShapeDtypeStruct((2 * pools, 3, 1024), f32),
             jax.ShapeDtypeStruct((3, 1024), f32),
         ),
-        in_specs=[pl.BlockSpec(memory_space=SMEM)] * 5 + [vmem] * 7,
+        in_specs=[pl.BlockSpec(memory_space=SMEM)] * 3 + [vmem] * 8,
         out_specs=(vmem,) * 3,
         scratch_shapes=[VMEM((6 * HI, LO), f32), VMEM((4, 3, 1024), f32)],
         compiler_params=pltpu.CompilerParams(vmem_limit_bytes=32 << 20),
@@ -635,7 +668,7 @@
 ):
     bricks, pools = lax.axis_size(BRICK), lax.axis_size("pool")
     place = tuple(lax.axis_index(axis).astype(jnp.int32).reshape(1) for axis in ("core", "pool"))
-    send, band_stress = solve_cells(
+    send, band_stress, replace = solve_cells(
         band_count,
         band_owner,
         band_element,
@@ -649,14 +682,13 @@
     pieces = lax.all_to_all(
         send.reshape(bricks * pools, 1, 9 * LANES), BOTH, split_axis=0, concat_axis=0, tiled=True
     )
-    sparse = (band_count, band_element, band_stress)
-    dense = (displacement, node_map, shape_grads, volumes.reshape(64, LANES), elastic_moduli)
-    so_far = macro_first(*sparse, *dense)
+    dense = (node_map, shape_grads, volumes.reshape(64, LANES), elastic_moduli)
+    so_far, table, step = macro_first(replace, displacement, *dense)
     pieces, so_far = lax.optimization_barrier((pieces, so_far))
     sorted_pieces = sort_pieces(pieces.reshape(9 * bricks * pools, LANES), bricks)
     sorted_pieces, so_far = lax.optimization_barrier((sorted_pieces, so_far))
     mine = lax.all_to_all(sorted_pieces, BRICK, split_axis=0, concat_axis=0, tiled=True)
-    own, inner, outer = macro_last(pools, *sparse, *place, *dense, so_far, shared_nodes)
+    own, inner, outer = macro_last(pools, replace, *place, table, step, *dense, so_far, shared_nodes)
     inner = lax.all_to_all(inner, ("core", "pool"), split_axis=0, concat_axis=0, tiled=True)
     steps = [(i, i + 1) for i in range(1, bricks - 1, 2)]
     outer = lax.ppermute(outer, BRICK, steps + [(j, i) for i, j in steps])

time: 65.5 us -> 61.4 us (0.937)
  Pallas kernels: 34.2 us -> 29.8 us
    pallas_call x1, Pallas kernels: 10.3 us -> 6.73 us  [macro_last(): pl.pallas_call(functools.partial(macro_last_kernel, UNROLL), out_shape=(j...]
    pallas_call x1, Pallas kernels: 13.9 us -> 13.1 us  [macro_first(): pl.pallas_call(functools.partial(macro_first_kernel, UNROLL), out_shape=(...]
  transfers between devices with their start and end apart: 4 -> 4, of which waited for: 1 -> 1; matrix products, arithmetic and copies ran while one was open for 1% -> 1% of each run, Pallas kernels for 40% -> 36%
where the time goes in v5:
time: 61.4 us; the launch traced here: 60.4 us
  Pallas kernels  29.8 us (49%)
  starting transfers between devices  27.1 us (44%)
  between operations  1.44 us (2%)
  local copies, waits for them, and re-layouts  1.42 us (2%)
  waiting for transfers between devices  0.72 us (1%)
    pallas_call x1, Pallas kernels, macro_first(): pl.pallas_call(functools.partial(macro_first_kernel, UNROLL), out_shape=(...  13.1 us
    all_to_all x1, starting transfers between devices, shards(): lax.all_to_all(send.reshape(bricks * pools, 1, 9 * LANES), BOTH, split_ax...  10.2 us
    all_to_all x1, starting transfers between devices, shards(): lax.all_to_all(sorted_pieces, BRICK, split_axis=0, concat_axis=0, tiled=T...  7.48 us
    pallas_call x1, Pallas kernels, macro_last(): pl.pallas_call(functools.partial(macro_last_kernel, UNROLL), out_shape=(j...  6.73 us
    pallas_call x1, Pallas kernels, solve_cells(): pl.pallas_call(cells_kernel, out_shape=(jax.ShapeDtypeStruct((36 * TILES,...  5.41 us
    all_to_all x1, starting transfers between devices, shards(): lax.all_to_all(inner, ('core', 'pool'), split_axis=0, concat_axis=0, tile...  5.34 us
    ppermute x1, starting transfers between devices, shards(): outer = lax.ppermute(outer, BRICK, steps + [(j, i) for i, j in steps])  4.06 us
    pallas_call x1, Pallas kernels, join_pieces(): pl.pallas_call(join_kernel, out_shape=jax.ShapeDtypeStruct((2, 8, NV), f3...  1.71 us
  transfers between devices with their start and end apart: 4, of which 1 were waited for; matrix products, arithmetic and copies ran while one was open for 1% of the time, Pallas kernels for 36%

profile of v5, /device:TPU:40, one launch (start us, length us, event | category | flops | bytes accessed | tf_op | source)
XLA Modules:
  0.0 60.4 jit_solution(8322972551273857620)
XLA Ops:
  1.3 0.0 copy-start.2
  1.3 5.4 %cells.1 = (f32[1152,128]{1,0:T(8,128)}, f32[6,4]{1,0:T(8,128)}, f32[8,4]{1,0:T(8,128)}) custom-call(s32[1]{0:T(128)S(6)} %copy.20.count, s32[1,4]{1,0:T(1,128)} %owner.1, s32[1,4]{1,0:T(1,128)} %element.1, f32[3,9216]{1,0:T(4,128)} %disp.3, s32[8,8192]{1,0:T(8,128)} %nm.5, f32[3,8,8192]{2,1,0:T(8,128)} %grads.5, f32[4,8,4096]{2,1,0:T(8,128)} %micro.1, ...), custom_call_target="tpu_custom_call" | custom-call | tf_op jit(solution)/shard_map/cells/pallas_call | solution.py:321
  6.7 0.0 copy-start
  6.7 0.0 copy-start.1
  6.7 0.0 copy-start.3
  6.7 0.0 copy-start.5
  6.7 0.0 copy-start.8
  6.7 10.2 %all-to-all-start = ((f32[128,1,1152]{2,1,0:T(1,128)}), f32[128,1,1152]{2,1,0:T(1,128)S(1)}, u32[]{:S(2)}, u32[]{:S(2)}) async-start(f32[128,1,1152]{2,1,0:T(1,128)} %bitcast.10), calls=%async_computation | async-start | bytes 1179648 | tf_op jit(solution)/shard_map/all_to_all | solution.py:682
  16.9 0.0 copy-done.2
  16.9 0.0 copy-done
  16.9 0.0 copy-done.1
  17.0 0.0 copy-done.3
  17.0 0.0 copy-done.5
  17.0 0.0 copy-done.8
  17.0 13.1 %macro_first.1 = (f32[240,256]{1,0:T(8,128)S(1)}, s32[2,9216]{1,0:T(2,128)S(1)}, f32[1,128]{1,0:T(1,128)S(1)}) custom-call(f32[8,4]{1,0:T(8,128)S(1)} %copy-done.8, f32[3,9216]{1,0:T(4,128)S(1)} %copy-done.2, s32[8,8192]{1,0:T(8,128)S(1)} %copy-done.1, f32[3,8,8192]{2,1,0:T(8,128)S(1)} %copy-done, f32[64,128]{1,0:T(8,128)S(1)} %bitcast.7, ...), custom_call_target="tpu_custom_call" | custom-call | tf_op jit(solution)/shard_map/macro_first/pallas_call | solution.py:534
  30.1 0.0 all-to-all-done
  30.1 1.4 %sort_pieces.1 = f32[32,2,8,128]{3,2,1,0:T(8,128)} custom-call(f32[1152,128]{1,0:T(8,128)S(1)} %bitcast.6), custom_call_target="tpu_custom_call" | custom-call | tf_op jit(solution)/shard_map/sort_pieces/pallas_call | solution.py:627
  31.5 7.5 %all-to-all-start.2 = ((f32[32,2,8,128]{3,2,1,0:T(8,128)}), f32[32,2,8,128]{3,2,1,0:T(8,128)S(1)}, u32[]{:S(2)}, u32[]{:S(2)}) async-start(f32[32,2,8,128]{3,2,1,0:T(8,128)} %sort_pieces.1), calls=%async_computation.2 | async-start | bytes 524288 | tf_op jit(solution)/shard_map/all_to_all | solution.py:690
  39.0 0.0 copy-start.6
  39.0 0.7 %copy-done.6 = s32[1,4,1024]{2,1,0:T(4,128)S(1)} copy-done((s32[1,4,1024]{2,1,0:T(4,128)S(1)}, s32[1,4,1024]{2,1,0:T(4,128)}, u32[]{:S(2)}) %copy-start.6) | copy-done | bytes 16408
  39.7 6.7 %macro_last.1 = (f32[120,256]{1,0:T(8,128)S(1)}, f32[8,3,1024]{2,1,0:T(4,128)}, f32[3,1024]{1,0:T(4,128)S(1)}) custom-call(f32[8,4]{1,0:T(8,128)S(1)} %copy-done.8, s32[1]{0:T(128)} %bitcast.core_index, s32[1]{0:T(128)} %bitcast.1.pool_index, s32[2,9216]{1,0:T(2,128)S(1)} %get-tuple-element.20.table, f32[1,128]{1,0:T(1,128)S(1)} %get-tuple-element.21.step, ...), custom_call_target="tpu_custom_call" | custom-call | tf_op jit(solution)/shard_map/macro_last/pallas_call | solution.py:550
  46.4 0.0 all-to-all-done.2.pieces
  46.4 0.0 copy-start.9
  46.4 0.0 copy-start.10
  46.4 5.3 %all-to-all-start.1 = ((f32[8,3,1024]{2,1,0:T(4,128)}), f32[8,3,1024]{2,1,0:T(4,128)S(1)}, u32[]{:S(2)}, u32[]{:S(2)}) async-start(f32[8,3,1024]{2,1,0:T(4,128)} %get-tuple-element.28), calls=%async_computation.1 | async-start | bytes 262144 | tf_op jit(solution)/shard_map/all_to_all | solution.py:692
  51.8 4.1 %collective-permute-start = (f32[3,1024]{1,0:T(4,128)S(1)}, f32[3,1024]{1,0:T(4,128)S(1)}, u32[]{:S(2)}, u32[]{:S(2)}) collective-permute-start(f32[3,1024]{1,0:T(4,128)S(1)} %get-tuple-element.29), channel_id=1, source_target_pairs={{4,8},{12,16},{20,24},{28,32},{36,40},{44,48},{52,56},{60,64},{68,... | collective-permute-start | bytes 36872 | tf_op jit(solution)/shard_map/ppermute | solution.py:694
  55.8 0.0 copy-done.10
  55.9 0.7 %copy.19 = f32[6,4]{0,1:T(4,128)} copy(f32[6,4]{1,0:T(8,128)S(1)} %copy-done.10) | data formatting | bytes 192
  56.5 0.0 copy-done.9
  56.5 0.0 copy-start.4
  56.5 0.0 copy-start.7
  56.5 1.7 %join_pieces.1 = f32[2,8,4096]{2,1,0:T(8,128)} custom-call(f32[32,2,8,128]{3,2,1,0:T(8,128)} %copy-done.9), custom_call_target="tpu_custom_call" | custom-call | tf_op jit(solution)/shard_map/join_pieces/pallas_call | solution.py:646
  58.2 0.7 %collective-permute-done.outer = f32[3,1024]{1,0:T(4,128)S(1)} collective-permute-done((f32[3,1024]{1,0:T(4,128)S(1)}, f32[3,1024]{1,0:T(4,128)S(1)}, u32[]{:S(2)}, u32[]{:S(2)}) %collective-permute-start) | collective-permute-done | bytes 12320 | tf_op jit(solution)/shard_map/ppermute | solution.py:694
  58.9 0.0 all-to-all-done.1.inner
  58.9 0.0 copy-done.4
  58.9 0.0 copy-done.7
  59.0 1.5 %assemble.1 = f32[3,9216]{1,0:T(4,128)} custom-call(s32[1]{0:T(128)} %bitcast.core_index, s32[1]{0:T(128)} %bitcast.1.pool_index, f32[120,256]{1,0:T(8,128)S(1)} %get-tuple-element.27.own, s32[1,4,1024]{2,1,0:T(4,128)S(1)} %copy-done.6, f32[8,3,1024]{2,1,0:T(4,128)S(1)} %all-to-all-done.1.inner, f32[3,1024]{1,0:T(4,128)S(1)} %collective-permute-done.outer, ...), custom_call_target="tpu_custom_call" | custom-call | tf_op jit(solution)/shard_map/assemble/pallas_call | solution.py:600
Async XLA Ops:
  1.3 15.7 %copy-start.2 = (f32[3,9216]{1,0:T(4,128)S(1)}, f32[3,9216]{1,0:T(4,128)}, u32[]{:S(2)}) copy-start(f32[3,9216]{1,0:T(4,128)} %disp.3) | copy-start | bytes 331780
  6.7 10.2 %copy-start = (f32[3,8,8192]{2,1,0:T(8,128)S(1)}, f32[3,8,8192]{2,1,0:T(8,128)}, u32[]{:S(2)}) copy-start(f32[3,8,8192]{2,1,0:T(8,128)} %grads.5) | copy-start | bytes 2359300
  6.7 10.3 %copy-start.1 = (s32[8,8192]{1,0:T(8,128)S(1)}, s32[8,8192]{1,0:T(8,128)}, u32[]{:S(2)}) copy-start(s32[8,8192]{1,0:T(8,128)} %nm.5) | copy-start | bytes 786436
  6.7 10.3 %copy-start.3 = (f32[2,8192]{1,0:T(2,128)S(1)}, f32[2,8192]{1,0:T(2,128)}, u32[]{:S(2)}) copy-start(f32[2,8192]{1,0:T(2,128)} %moduli.3) | copy-start | bytes 196612
  6.7 10.3 %copy-start.5 = (f32[8192]{0:T(1024)S(1)}, f32[8192]{0:T(1024)}, u32[]{:S(2)}) copy-start(f32[8192]{0:T(1024)} %param.17) | copy-start | bytes 98308
  6.7 10.3 %copy-start.8 = (f32[8,4]{1,0:T(8,128)S(1)}, f32[8,4]{1,0:T(8,128)}, u32[]{:S(2)}) copy-start(f32[8,4]{1,0:T(8,128)} %get-tuple-element.19.replace) | copy-start | bytes 388
  6.7 23.3 %all-to-all-start = ((f32[128,1,1152]{2,1,0:T(1,128)}), f32[128,1,1152]{2,1,0:T(1,128)S(1)}, u32[]{:S(2)}, u32[]{:S(2)}) async-start(f32[128,1,1152]{2,1,0:T(1,128)} %bitcast.10), calls=%async_computation | async-start | bytes 1179648 | tf_op jit(solution)/shard_map/all_to_all | solution.py:682
  31.5 14.9 %all-to-all-start.2 = ((f32[32,2,8,128]{3,2,1,0:T(8,128)}), f32[32,2,8,128]{3,2,1,0:T(8,128)S(1)}, u32[]{:S(2)}, u32[]{:S(2)}) async-start(f32[32,2,8,128]{3,2,1,0:T(8,128)} %sort_pieces.1), calls=%async_computation.2 | async-start | bytes 524288 | tf_op jit(solution)/shard_map/all_to_all | solution.py:690
  39.0 0.7 %copy-start.6 = (s32[1,4,1024]{2,1,0:T(4,128)S(1)}, s32[1,4,1024]{2,1,0:T(4,128)}, u32[]{:S(2)}) copy-start(s32[1,4,1024]{2,1,0:T(4,128)} %shared.3) | copy-start | bytes 49156
  46.4 10.1 %copy-start.9 = (f32[32,2,8,128]{3,2,1,0:T(8,128)}, f32[32,2,8,128]{3,2,1,0:T(8,128)S(1)}, u32[]{:S(2)}) copy-start(f32[32,2,8,128]{3,2,1,0:T(8,128)S(1)} %all-to-all-done.2.pieces) | copy-start | bytes 786436
  46.4 9.4 %copy-start.10 = (f32[6,4]{1,0:T(8,128)S(1)}, f32[6,4]{1,0:T(8,128)}, u32[]{:S(2)}) copy-start(f32[6,4]{1,0:T(8,128)} %get-tuple-element.39) | copy-start | bytes 292
  46.4 12.5 %all-to-all-start.1 = ((f32[8,3,1024]{2,1,0:T(4,128)}), f32[8,3,1024]{2,1,0:T(4,128)S(1)}, u32[]{:S(2)}, u32[]{:S(2)}) async-start(f32[8,3,1024]{2,1,0:T(4,128)} %get-tuple-element.28), calls=%async_computation.1 | async-start | bytes 262144 | tf_op jit(solution)/shard_map/all_to_all | solution.py:692
  51.8 7.2 %collective-permute-start = (f32[3,1024]{1,0:T(4,128)S(1)}, f32[3,1024]{1,0:T(4,128)S(1)}, u32[]{:S(2)}, u32[]{:S(2)}) collective-permute-start(f32[3,1024]{1,0:T(4,128)S(1)} %get-tuple-element.29), channel_id=1, source_target_pairs={{4,8},{12,16},{20,24},{28,32},{36,40},{44,48},{52,56},{60,64},{68,... | collective-permute-start | bytes 36872 | tf_op jit(solution)/shard_map/ppermute | solution.py:694
  56.5 2.4 %copy-start.4 = (f32[3,9216]{1,0:T(4,128)S(1)}, f32[3,9216]{1,0:T(4,128)}, u32[]{:S(2)}) copy-start(f32[3,9216]{1,0:T(4,128)} %external.1) | copy-start | bytes 331780
  56.5 2.4 %copy-start.7 = (f32[9216]{0:T(1024)S(1)}, f32[9216]{0:T(1024)}, u32[]{:S(2)}) copy-start(f32[9216]{0:T(1024)} %param.20) | copy-start | bytes 110596

commit v6 on v5

--- a/solution.py
+++ b/solution.py
@@ -14,7 +14,7 @@
 ITERS = 2
 LANES = 128
 TILES = 32
-HI = 40
+HI = 48
 LO = 256
 STEPS = float((1 << 20) - 2)
 OFFSET = 1 << 20
@@ -337,14 +337,20 @@
 
 
 def one_hot_sum(node, values, width):
-    hi = jnp.broadcast_to(node >> 8, (HI, width))
-    lo = jnp.broadcast_to(node & 255, (LO, width))
-    coarse = lax.broadcasted_iota(jnp.int32, (HI, width), 0) == hi
-    fine = lax.broadcasted_iota(jnp.int32, (LO, width), 0) == lo
+    def spread(row, rows):
+        return jnp.broadcast_to(jnp.broadcast_to(row, (16, width)).astype(bf16)[None], (rows // 16, 16, width)).reshape(
+            rows, width
+        )
+
+    def index(rows):
+        return lax.broadcasted_iota(jnp.int32, (rows, width), 0).astype(f32).astype(bf16)
+
+    coarse = index(HI) == spread((node >> 8).astype(f32), HI)
+    fine = index(LO) == spread((node & 255).astype(f32), LO)
     left = jnp.concatenate(
-        [jnp.where(coarse, jnp.broadcast_to(v, (HI, width)), 0.0) for v in values], axis=0
-    ).astype(bf16)
-    right = jnp.where(fine, 1.0, 0.0).astype(bf16)
+        [jnp.where(coarse, spread(v, HI), jnp.zeros((HI, width), bf16)) for v in values], axis=0
+    )
+    right = jnp.where(fine, jnp.ones((LO, width), bf16), jnp.zeros((LO, width), bf16))
     return left, right
 
 

time: 61.4 us -> 60.5 us (0.985)
  Pallas kernels: 29.8 us -> 28.8 us
  waiting for transfers between devices: 0.72 us -> 1.51 us
  starting transfers between devices: 27.1 us -> 26.4 us
    pallas_call x1, Pallas kernels: 13.1 us -> 12.1 us  [macro_first(): pl.pallas_call(functools.partial(macro_first_kernel, UNROLL), out_shape=(...]
  transfers between devices with their start and end apart: 4 -> 4, of which waited for: 1 -> 3; matrix products, arithmetic and copies ran while one was open for 1% -> 1% of each run, Pallas kernels for 36% -> 34%
where the time goes in v6:
time: 60.5 us; the launch traced here: 59.6 us
  Pallas kernels  28.8 us (48%)
  starting transfers between devices  26.4 us (44%)
  waiting for transfers between devices  1.51 us (2%)
  between operations  1.43 us (2%)
  local copies, waits for them, and re-layouts  1.42 us (2%)
    pallas_call x1, Pallas kernels, macro_first(): pl.pallas_call(functools.partial(macro_first_kernel, UNROLL), out_shape=(...  12.1 us
    all_to_all x1, starting transfers between devices, shards(): lax.all_to_all(send.reshape(bricks * pools, 1, 9 * LANES), BOTH, split_ax...  10.2 us
    all_to_all x1, starting transfers between devices, shards(): lax.all_to_all(sorted_pieces, BRICK, split_axis=0, concat_axis=0, tiled=T...  6.93 us
    pallas_call x1, Pallas kernels, macro_last(): pl.pallas_call(functools.partial(macro_last_kernel, UNROLL), out_shape=(j...  6.59 us
    pallas_call x1, Pallas kernels, solve_cells(): pl.pallas_call(cells_kernel, out_shape=(jax.ShapeDtypeStruct((36 * TILES,...  5.41 us
    all_to_all x1, starting transfers between devices, shards(): lax.all_to_all(inner, ('core', 'pool'), split_axis=0, concat_axis=0, tile...  5.38 us
    ppermute x1, starting transfers between devices, shards(): outer = lax.ppermute(outer, BRICK, steps + [(j, i) for i, j in steps])  3.95 us
    pallas_call x1, Pallas kernels, join_pieces(): pl.pallas_call(join_kernel, out_shape=jax.ShapeDtypeStruct((2, 8, NV), f3...  1.71 us
  transfers between devices with their start and end apart: 4, of which 3 were waited for; matrix products, arithmetic and copies ran while one was open for 1% of the time, Pallas kernels for 34%

profile of v6, /device:TPU:40, one launch (start us, length us, event | category | flops | bytes accessed | tf_op | source)
XLA Modules:
  0.0 59.6 jit_solution(13747979139102595044)
XLA Ops:
  1.3 0.0 copy-start.2
  1.3 5.4 %cells.1 = (f32[1152,128]{1,0:T(8,128)}, f32[6,4]{1,0:T(8,128)}, f32[8,4]{1,0:T(8,128)}) custom-call(s32[1]{0:T(128)S(6)} %copy.20.count, s32[1,4]{1,0:T(1,128)} %owner.1, s32[1,4]{1,0:T(1,128)} %element.1, f32[3,9216]{1,0:T(4,128)} %disp.3, s32[8,8192]{1,0:T(8,128)} %nm.5, f32[3,8,8192]{2,1,0:T(8,128)} %grads.5, f32[4,8,4096]{2,1,0:T(8,128)} %micro.1, ...), custom_call_target="tpu_custom_call" | custom-call | tf_op jit(solution)/shard_map/cells/pallas_call | solution.py:321
  6.7 0.0 copy-start
  6.7 0.0 copy-start.1
  6.7 0.0 copy-start.3
  6.7 0.0 copy-start.5
  6.7 0.0 copy-start.8
  6.7 10.2 %all-to-all-start = ((f32[128,1,1152]{2,1,0:T(1,128)}), f32[128,1,1152]{2,1,0:T(1,128)S(1)}, u32[]{:S(2)}, u32[]{:S(2)}) async-start(f32[128,1,1152]{2,1,0:T(1,128)} %bitcast.10), calls=%async_computation | async-start | bytes 1179648 | tf_op jit(solution)/shard_map/all_to_all | solution.py:688
  16.9 0.0 copy-done.2
  16.9 0.0 copy-done
  16.9 0.0 copy-done.1
  17.0 0.0 copy-done.3
  17.0 0.0 copy-done.5
  17.0 0.0 copy-done.8
  17.0 12.1 %macro_first.1 = (f32[288,256]{1,0:T(8,128)S(1)}, s32[2,9216]{1,0:T(2,128)S(1)}, f32[1,128]{1,0:T(1,128)S(1)}) custom-call(f32[8,4]{1,0:T(8,128)S(1)} %copy-done.8, f32[3,9216]{1,0:T(4,128)S(1)} %copy-done.2, s32[8,8192]{1,0:T(8,128)S(1)} %copy-done.1, f32[3,8,8192]{2,1,0:T(8,128)S(1)} %copy-done, f32[64,128]{1,0:T(8,128)S(1)} %bitcast.7, ...), custom_call_target="tpu_custom_call" | custom-call | tf_op jit(solution)/shard_map/macro_first/pallas_call | solution.py:540
  29.1 0.6 all-to-all-done
  29.7 1.4 %sort_pieces.1 = f32[32,2,8,128]{3,2,1,0:T(8,128)} custom-call(f32[1152,128]{1,0:T(8,128)S(1)} %bitcast.6), custom_call_target="tpu_custom_call" | custom-call | tf_op jit(solution)/shard_map/sort_pieces/pallas_call | solution.py:633
  31.1 6.9 %all-to-all-start.2 = ((f32[32,2,8,128]{3,2,1,0:T(8,128)}), f32[32,2,8,128]{3,2,1,0:T(8,128)S(1)}, u32[]{:S(2)}, u32[]{:S(2)}) async-start(f32[32,2,8,128]{3,2,1,0:T(8,128)} %sort_pieces.1), calls=%async_computation.2 | async-start | bytes 524288 | tf_op jit(solution)/shard_map/all_to_all | solution.py:696
  38.0 0.0 copy-start.6
  38.0 0.7 %copy-done.6 = s32[1,4,1024]{2,1,0:T(4,128)S(1)} copy-done((s32[1,4,1024]{2,1,0:T(4,128)S(1)}, s32[1,4,1024]{2,1,0:T(4,128)}, u32[]{:S(2)}) %copy-start.6) | copy-done | bytes 16408
  38.8 6.6 %macro_last.1 = (f32[144,256]{1,0:T(8,128)S(1)}, f32[8,3,1024]{2,1,0:T(4,128)}, f32[3,1024]{1,0:T(4,128)S(1)}) custom-call(f32[8,4]{1,0:T(8,128)S(1)} %copy-done.8, s32[1]{0:T(128)} %bitcast.core_index, s32[1]{0:T(128)} %bitcast.1.pool_index, s32[2,9216]{1,0:T(2,128)S(1)} %get-tuple-element.20.table, f32[1,128]{1,0:T(1,128)S(1)} %get-tuple-element.21.step, ...), custom_call_target="tpu_custom_call" | custom-call | tf_op jit(solution)/shard_map/macro_last/pallas_call | solution.py:556
  45.3 0.1 all-to-all-done.2.pieces
  45.5 0.0 copy-start.9
  45.5 0.0 copy-start.10
  45.5 5.4 %all-to-all-start.1 = ((f32[8,3,1024]{2,1,0:T(4,128)}), f32[8,3,1024]{2,1,0:T(4,128)S(1)}, u32[]{:S(2)}, u32[]{:S(2)}) async-start(f32[8,3,1024]{2,1,0:T(4,128)} %get-tuple-element.28), calls=%async_computation.1 | async-start | bytes 262144 | tf_op jit(solution)/shard_map/all_to_all | solution.py:698
  50.9 3.9 %collective-permute-start = (f32[3,1024]{1,0:T(4,128)S(1)}, f32[3,1024]{1,0:T(4,128)S(1)}, u32[]{:S(2)}, u32[]{:S(2)}) collective-permute-start(f32[3,1024]{1,0:T(4,128)S(1)} %get-tuple-element.29), channel_id=1, source_target_pairs={{4,8},{12,16},{20,24},{28,32},{36,40},{44,48},{52,56},{60,64},{68,... | collective-permute-start | bytes 36872 | tf_op jit(solution)/shard_map/ppermute | solution.py:700
  54.8 0.0 copy-done.10
  54.8 0.7 %copy.19 = f32[6,4]{0,1:T(4,128)} copy(f32[6,4]{1,0:T(8,128)S(1)} %copy-done.10) | data formatting | bytes 192
  55.5 0.0 copy-done.9
  55.5 0.0 copy-start.4
  55.5 0.0 copy-start.7
  55.5 1.7 %join_pieces.1 = f32[2,8,4096]{2,1,0:T(8,128)} custom-call(f32[32,2,8,128]{3,2,1,0:T(8,128)} %copy-done.9), custom_call_target="tpu_custom_call" | custom-call | tf_op jit(solution)/shard_map/join_pieces/pallas_call | solution.py:652
  57.2 0.8 %collective-permute-done.outer = f32[3,1024]{1,0:T(4,128)S(1)} collective-permute-done((f32[3,1024]{1,0:T(4,128)S(1)}, f32[3,1024]{1,0:T(4,128)S(1)}, u32[]{:S(2)}, u32[]{:S(2)}) %collective-permute-start) | collective-permute-done | bytes 12320 | tf_op jit(solution)/shard_map/ppermute | solution.py:700
  58.0 0.0 all-to-all-done.1.inner
  58.0 0.0 copy-done.4
  58.0 0.0 copy-done.7
  58.0 1.5 %assemble.1 = f32[3,9216]{1,0:T(4,128)} custom-call(s32[1]{0:T(128)} %bitcast.core_index, s32[1]{0:T(128)} %bitcast.1.pool_index, f32[144,256]{1,0:T(8,128)S(1)} %get-tuple-element.27.own, s32[1,4,1024]{2,1,0:T(4,128)S(1)} %copy-done.6, f32[8,3,1024]{2,1,0:T(4,128)S(1)} %all-to-all-done.1.inner, f32[3,1024]{1,0:T(4,128)S(1)} %collective-permute-done.outer, ...), custom_call_target="tpu_custom_call" | custom-call | tf_op jit(solution)/shard_map/assemble/pallas_call | solution.py:606
Async XLA Ops:
  1.3 15.7 %copy-start.2 = (f32[3,9216]{1,0:T(4,128)S(1)}, f32[3,9216]{1,0:T(4,128)}, u32[]{:S(2)}) copy-start(f32[3,9216]{1,0:T(4,128)} %disp.3) | copy-start | bytes 331780
  6.7 10.2 %copy-start = (f32[3,8,8192]{2,1,0:T(8,128)S(1)}, f32[3,8,8192]{2,1,0:T(8,128)}, u32[]{:S(2)}) copy-start(f32[3,8,8192]{2,1,0:T(8,128)} %grads.5) | copy-start | bytes 2359300
  6.7 10.3 %copy-start.1 = (s32[8,8192]{1,0:T(8,128)S(1)}, s32[8,8192]{1,0:T(8,128)}, u32[]{:S(2)}) copy-start(s32[8,8192]{1,0:T(8,128)} %nm.5) | copy-start | bytes 786436
  6.7 10.3 %copy-start.3 = (f32[2,8192]{1,0:T(2,128)S(1)}, f32[2,8192]{1,0:T(2,128)}, u32[]{:S(2)}) copy-start(f32[2,8192]{1,0:T(2,128)} %moduli.3) | copy-start | bytes 196612
  6.7 10.3 %copy-start.5 = (f32[8192]{0:T(1024)S(1)}, f32[8192]{0:T(1024)}, u32[]{:S(2)}) copy-start(f32[8192]{0:T(1024)} %param.17) | copy-start | bytes 98308
  6.7 10.3 %copy-start.8 = (f32[8,4]{1,0:T(8,128)S(1)}, f32[8,4]{1,0:T(8,128)}, u32[]{:S(2)}) copy-start(f32[8,4]{1,0:T(8,128)} %get-tuple-element.19.replace) | copy-start | bytes 388
  6.7 23.0 %all-to-all-start = ((f32[128,1,1152]{2,1,0:T(1,128)}), f32[128,1,1152]{2,1,0:T(1,128)S(1)}, u32[]{:S(2)}, u32[]{:S(2)}) async-start(f32[128,1,1152]{2,1,0:T(1,128)} %bitcast.10), calls=%async_computation | async-start | bytes 1179648 | tf_op jit(solution)/shard_map/all_to_all | solution.py:688
  31.1 14.4 %all-to-all-start.2 = ((f32[32,2,8,128]{3,2,1,0:T(8,128)}), f32[32,2,8,128]{3,2,1,0:T(8,128)S(1)}, u32[]{:S(2)}, u32[]{:S(2)}) async-start(f32[32,2,8,128]{3,2,1,0:T(8,128)} %sort_pieces.1), calls=%async_computation.2 | async-start | bytes 524288 | tf_op jit(solution)/shard_map/all_to_all | solution.py:696
  38.0 0.7 %copy-start.6 = (s32[1,4,1024]{2,1,0:T(4,128)S(1)}, s32[1,4,1024]{2,1,0:T(4,128)}, u32[]{:S(2)}) copy-start(s32[1,4,1024]{2,1,0:T(4,128)} %shared.3) | copy-start | bytes 49156
  45.5 10.0 %copy-start.9 = (f32[32,2,8,128]{3,2,1,0:T(8,128)}, f32[32,2,8,128]{3,2,1,0:T(8,128)S(1)}, u32[]{:S(2)}) copy-start(f32[32,2,8,128]{3,2,1,0:T(8,128)S(1)} %all-to-all-done.2.pieces) | copy-start | bytes 786436
  45.5 9.3 %copy-start.10 = (f32[6,4]{1,0:T(8,128)S(1)}, f32[6,4]{1,0:T(8,128)}, u32[]{:S(2)}) copy-start(f32[6,4]{1,0:T(8,128)} %get-tuple-element.39) | copy-start | bytes 292
  45.5 12.5 %all-to-all-start.1 = ((f32[8,3,1024]{2,1,0:T(4,128)}), f32[8,3,1024]{2,1,0:T(4,128)S(1)}, u32[]{:S(2)}, u32[]{:S(2)}) async-start(f32[8,3,1024]{2,1,0:T(4,128)} %get-tuple-element.28), calls=%async_computation.1 | async-start | bytes 262144 | tf_op jit(solution)/shard_map/all_to_all | solution.py:698
  50.9 7.2 %collective-permute-start = (f32[3,1024]{1,0:T(4,128)S(1)}, f32[3,1024]{1,0:T(4,128)S(1)}, u32[]{:S(2)}, u32[]{:S(2)}) collective-permute-start(f32[3,1024]{1,0:T(4,128)S(1)} %get-tuple-element.29), channel_id=1, source_target_pairs={{4,8},{12,16},{20,24},{28,32},{36,40},{44,48},{52,56},{60,64},{68,... | collective-permute-start | bytes 36872 | tf_op jit(solution)/shard_map/ppermute | solution.py:700
  55.5 2.5 %copy-start.4 = (f32[3,9216]{1,0:T(4,128)S(1)}, f32[3,9216]{1,0:T(4,128)}, u32[]{:S(2)}) copy-start(f32[3,9216]{1,0:T(4,128)} %external.1) | copy-start | bytes 331780
  55.5 2.5 %copy-start.7 = (f32[9216]{0:T(1024)S(1)}, f32[9216]{0:T(1024)}, u32[]{:S(2)}) copy-start(f32[9216]{0:T(1024)} %param.20) | copy-start | bytes 110596

commit v7 on v6

--- a/solution.py
+++ b/solution.py
@@ -463,10 +463,20 @@
     add(lax.fori_loop(1, (end - begin) // unroll, body, group(0)))
 
 
-def macro_first_kernel(unroll, replace, disp, nm, grads, volumes, moduli, sums, table, step):
+def macro_first_kernel(
+    unroll, replace, disp, nm, grads, volumes, moduli, shared, sums, table, step, face_nodes
+):
+    for i in range(4):
+        for half in range(2):
+            cols = slice((2 * i + half) * LANES, (2 * i + half + 1) * LANES)
+            face_nodes[i, 4 * half : 4 * half + 4, :] = shared[0, :, cols]
     pack_table(disp, table, step)
     sums[...] = jnp.zeros_like(sums)
     macro_tiles(0, SPLIT, unroll, replace, table, step, nm, grads, volumes, moduli, sums)
+
+
+def face_lists(core, pool):
+    return 1 - core, core, 3 - (pool & 1), 2 + (pool & 1)
 
 
 def macro_last_kernel(
@@ -481,10 +491,12 @@
     volumes,
     moduli,
     so_far,
-    shared,
+    face_nodes,
     own,
-    inner,
-    outer,
+    to_core,
+    to_brick,
+    to_even,
+    to_odd,
     sums,
     faces,
 ):
@@ -497,13 +509,7 @@
 
     for pair in range(4):
         first, second = 2 * pair, 2 * pair + 1
-        node = jnp.concatenate(
-            [
-                shared[0, :, first * LANES : (first + 1) * LANES],
-                shared[0, :, second * LANES : (second + 1) * LANES],
-            ],
-            axis=0,
-        )
+        node = face_nodes[pair]
         hi, lo = node >> 7, node & 127
         picked = [jnp.zeros((8, LANES), f32) for _ in range(3)]
         for r in range(72):
@@ -520,19 +526,9 @@
                 faces[face, c : c + 1, second * LANES : (second + 1) * LANES] = picked[c][
                     4 + face : 5 + face
                 ]
-    core, pool = core_index[0], pool_index[0]
-    pools = inner.shape[0] // 2
-    inner[...] = jnp.zeros_like(inner)
-    inner[(1 - core) * pools + pool] = faces[1 - core]
-    outer[...] = faces[core]
-
-    @pl.when(pool > 0)
-    def _():
-        inner[core * pools + pool - 1] = faces[2]
-
-    @pl.when(pool < pools - 1)
-    def _():
-        inner[core * pools + pool + 1] = faces[3]
+    lists = face_lists(core_index[0], pool_index[0])
+    for face, out in zip(lists, (to_core, to_brick, to_even, to_odd)):
+        out[...] = faces[face]
 
 
 def macro_first(*arguments):
@@ -543,51 +539,39 @@
             jax.ShapeDtypeStruct((6 * HI, LO), f32),
             jax.ShapeDtypeStruct((2, 72 * LANES), jnp.int32),
             jax.ShapeDtypeStruct((1, LANES), f32),
+            jax.ShapeDtypeStruct((4, 8, LANES), jnp.int32),
         ),
-        in_specs=[pl.BlockSpec(memory_space=SMEM)] + [vmem] * 5,
-        out_specs=(vmem,) * 3,
+        in_specs=[pl.BlockSpec(memory_space=SMEM)] + [vmem] * 6,
+        out_specs=(vmem,) * 4,
         compiler_params=pltpu.CompilerParams(vmem_limit_bytes=32 << 20),
         name="macro_first",
     )(*arguments)
 
 
-def macro_last(pools, *arguments):
+def macro_last(*arguments):
     vmem = pl.BlockSpec(memory_space=VMEM)
     return pl.pallas_call(
         functools.partial(macro_last_kernel, UNROLL),
         out_shape=(
             jax.ShapeDtypeStruct((3 * HI, LO), f32),
-            jax.ShapeDtypeStruct((2 * pools, 3, 1024), f32),
-            jax.ShapeDtypeStruct((3, 1024), f32),
-        ),
+        )
+        + (jax.ShapeDtypeStruct((3, 1024), f32),) * 4,
         in_specs=[pl.BlockSpec(memory_space=SMEM)] * 3 + [vmem] * 8,
-        out_specs=(vmem,) * 3,
+        out_specs=(vmem,) * 5,
         scratch_shapes=[VMEM((6 * HI, LO), f32), VMEM((4, 3, 1024), f32)],
         compiler_params=pltpu.CompilerParams(vmem_limit_bytes=32 << 20),
         name="macro_last",
     )(*arguments)
 
 
-def assemble_kernel(core_index, pool_index, own, shared, inner, outer, external, mass, out):
-    core, pool = core_index[0], pool_index[0]
-    pools = inner.shape[0] // 2
-    below, above = jnp.maximum(pool - 1, 0), jnp.minimum(pool + 1, pools - 1)
-    arrivals = (
-        (1 - core, True, lambda c, cols: inner[(1 - core) * pools + pool, c : c + 1, cols]),
-        (core, True, lambda c, cols: outer[c : c + 1, cols]),
-        (2, pool > 0, lambda c, cols: inner[core * pools + below, c : c + 1, cols]),
-        (3, pool < pools - 1, lambda c, cols: inner[core * pools + above, c : c + 1, cols]),
-    )
+def assemble_kernel(core_index, pool_index, own, shared, r0, r1, r2, r3, external, mass, out):
     total = None
-    for face, there, arrived in arrivals:
+    for face, arrived in zip(face_lists(core_index[0], pool_index[0]), (r0, r1, r2, r3)):
         for part in range(4):
             cols = slice(part * LO, (part + 1) * LO)
             values = []
             for c in range(3):
-                value = arrived(c, cols)
-                if there is not True:
-                    value = jnp.where(there, value, 0.0)
-                values += list(halves(value))
+                values += list(halves(arrived[c : c + 1, cols]))
             left, right = one_hot_sum(shared[0, pl.ds(face, 1), cols], values, LO)
             product = lax.dot_general(
                 left, right, (((1,), (1,)), ((), ())), preferred_element_type=f32
@@ -601,16 +585,16 @@
     out[...] = (external[...] - out[...]) / mass[...]
 
 
-def assemble(place, own, shared, inner, outer, external, mass):
+def assemble(place, own, shared, arrived, external, mass):
     vmem = pl.BlockSpec(memory_space=VMEM)
     return pl.pallas_call(
         assemble_kernel,
         out_shape=jax.ShapeDtypeStruct(external.shape, f32),
-        in_specs=[pl.BlockSpec(memory_space=SMEM)] * 2 + [vmem] * 6,
+        in_specs=[pl.BlockSpec(memory_space=SMEM)] * 2 + [vmem] * 8,
         out_specs=vmem,
         compiler_params=pltpu.CompilerParams(vmem_limit_bytes=32 << 20),
         name="assemble",
-    )(*place, own, shared, inner, outer, external, mass)
+    )(*place, own, shared, *arrived, external, mass)
 
 
 def sort_kernel(pieces, out, order, places, sem):
@@ -689,19 +673,27 @@
         send.reshape(bricks * pools, 1, 9 * LANES), BOTH, split_axis=0, concat_axis=0, tiled=True
     )
     dense = (node_map, shape_grads, volumes.reshape(64, LANES), elastic_moduli)
-    so_far, table, step = macro_first(replace, displacement, *dense)
+    so_far, table, step, face_nodes = macro_first(replace, displacement, *dense, shared_nodes)
     pieces, so_far = lax.optimization_barrier((pieces, so_far))
     sorted_pieces = sort_pieces(pieces.reshape(9 * bricks * pools, LANES), bricks)
     sorted_pieces, so_far = lax.optimization_barrier((sorted_pieces, so_far))
     mine = lax.all_to_all(sorted_pieces, BRICK, split_axis=0, concat_axis=0, tiled=True)
-    own, inner, outer = macro_last(pools, replace, *place, table, step, *dense, so_far, shared_nodes)
-    inner = lax.all_to_all(inner, ("core", "pool"), split_axis=0, concat_axis=0, tiled=True)
-    steps = [(i, i + 1) for i in range(1, bricks - 1, 2)]
-    outer = lax.ppermute(outer, BRICK, steps + [(j, i) for i, j in steps])
+    own, *faces = macro_last(replace, *place, table, step, *dense, so_far, face_nodes)
+
+    def swap(array, axis, size, first):
+        steps = [(i, i + 1) for i in range(first, size - 1, 2)]
+        return lax.ppermute(array, axis, steps + [(j, i) for i, j in steps])
+
+    arrived = (
+        swap(faces[0], "core", 2, 0),
+        swap(faces[1], BRICK, bricks, 1),
+        swap(faces[2], "pool", pools, 0),
+        swap(faces[3], "pool", pools, 1),
+    )
     owned_fields = join_pieces(mine)
-    inner, outer, owned_fields = lax.optimization_barrier((inner, outer, owned_fields))
+    *arrived, owned_fields = lax.optimization_barrier((*arrived, owned_fields))
     acceleration = assemble(
-        place, own, shared_nodes, inner, outer, external_force, nodal_mass.reshape(1, -1)
+        place, own, shared_nodes, arrived, external_force, nodal_mass.reshape(1, -1)
     )
     return (acceleration, band_stress, owned_fields)
 

time: 60.5 us -> 59 us (0.975)
  waiting for transfers between devices: 1.51 us -> 0.53 us
  starting transfers between devices: 26.4 us -> 27.1 us
  Pallas kernels: 28.8 us -> 28.1 us
    ppermute x1 -> x4, starting transfers between devices: 3.95 us -> 9.92 us  [swap(): return lax.ppermute(array, axis, steps + [(j, i) for i, j in steps])]
    all_to_all x1 -> x0, starting transfers between devices: 5.38 us -> none  [shards(): lax.all_to_all(inner, ('core', 'pool'), split_axis=0, concat_axis=0, tile...]
    ppermute x1 -> x4, waiting for transfers between devices: 0.81 us -> 0.01 us  [swap(): return lax.ppermute(array, axis, steps + [(j, i) for i, j in steps])]
    pallas_call x1, Pallas kernels: 6.59 us -> 5.97 us  [macro_last(): pl.pallas_call(functools.partial(macro_last_kernel, UNROLL), out_shape=(j...]
  transfers between devices with their start and end apart: 4 -> 6, of which waited for: 3 -> 1; matrix products, arithmetic and copies ran while one was open for 1% -> 1% of each run, Pallas kernels for 34% -> 34%
where the time goes in v7:
time: 59 us; the launch traced here: 58.6 us
  Pallas kernels  28.1 us (48%)
  starting transfers between devices  27.1 us (46%)
  between operations  1.49 us (3%)
  local copies, waits for them, and re-layouts  1.41 us (2%)
    pallas_call x1, Pallas kernels, macro_first(): pl.pallas_call(functools.partial(macro_first_kernel, UNROLL), out_shape=(...  12.2 us
    all_to_all x1, starting transfers between devices, shards(): lax.all_to_all(send.reshape(bricks * pools, 1, 9 * LANES), BOTH, split_ax...  10.2 us
    ppermute x4, starting transfers between devices, swap(): return lax.ppermute(array, axis, steps + [(j, i) for i, j in steps])  9.92 us
    all_to_all x1, starting transfers between devices, shards(): lax.all_to_all(sorted_pieces, BRICK, split_axis=0, concat_axis=0, tiled=T...  6.95 us
    pallas_call x1, Pallas kernels, macro_last(): pl.pallas_call(functools.partial(macro_last_kernel, UNROLL), out_shape=(j...  5.97 us
    pallas_call x1, Pallas kernels, solve_cells(): pl.pallas_call(cells_kernel, out_shape=(jax.ShapeDtypeStruct((36 * TILES,...  5.4 us
    pallas_call x1, Pallas kernels, join_pieces(): pl.pallas_call(join_kernel, out_shape=jax.ShapeDtypeStruct((2, 8, NV), f3...  1.67 us
    pallas_call x1, Pallas kernels, assemble(): pl.pallas_call(assemble_kernel, out_shape=jax.ShapeDtypeStruct(external.s...  1.52 us
  transfers between devices with their start and end apart: 6, of which 1 were waited for; matrix products, arithmetic and copies ran while one was open for 1% of the time, Pallas kernels for 34%

profile of v7, /device:TPU:40, one launch (start us, length us, event | category | flops | bytes accessed | tf_op | source)
XLA Modules:
  0.0 58.6 jit_solution(14302360032030977899)
XLA Ops:
  1.3 0.0 copy-start.2
  1.3 5.4 %cells.1 = (f32[1152,128]{1,0:T(8,128)}, f32[6,4]{1,0:T(8,128)}, f32[8,4]{1,0:T(8,128)}) custom-call(s32[1]{0:T(128)S(6)} %copy.20.count, s32[1,4]{1,0:T(1,128)} %owner.1, s32[1,4]{1,0:T(1,128)} %element.1, f32[3,9216]{1,0:T(4,128)} %disp.3, s32[8,8192]{1,0:T(8,128)} %nm.5, f32[3,8,8192]{2,1,0:T(8,128)} %grads.5, f32[4,8,4096]{2,1,0:T(8,128)} %micro.1, ...), custom_call_target="tpu_custom_call" | custom-call | tf_op jit(solution)/shard_map/cells/pallas_call | solution.py:321
  6.7 0.0 copy-start
  6.7 0.0 copy-start.1
  6.7 0.0 copy-start.3
  6.7 0.0 copy-start.5
  6.7 0.0 copy-start.6
  6.7 0.0 copy-start.8
  6.7 10.2 %all-to-all-start = ((f32[128,1,1152]{2,1,0:T(1,128)}), f32[128,1,1152]{2,1,0:T(1,128)S(1)}, u32[]{:S(2)}, u32[]{:S(2)}) async-start(f32[128,1,1152]{2,1,0:T(1,128)} %bitcast.10), calls=%async_computation | async-start | bytes 1179648 | tf_op jit(solution)/shard_map/all_to_all | solution.py:672
  16.9 0.0 copy-done.2
  16.9 0.0 copy-done
  17.0 0.0 copy-done.1
  17.0 0.0 copy-done.3
  17.0 0.0 copy-done.5
  17.0 0.0 copy-done.6
  17.0 0.0 copy-done.8
  17.0 12.2 %macro_first.1 = (f32[288,256]{1,0:T(8,128)S(1)}, s32[2,9216]{1,0:T(2,128)S(1)}, f32[1,128]{1,0:T(1,128)S(1)}, s32[4,8,128]{2,1,0:T(8,128)S(1)}) custom-call(f32[8,4]{1,0:T(8,128)S(1)} %copy-done.8, f32[3,9216]{1,0:T(4,128)S(1)} %copy-done.2, s32[8,8192]{1,0:T(8,128)S(1)} %copy-done.1, f32[3,8,8192]{2,1,0:T(8,128)S(1)} %copy-done, f32[64,128]{1,0:T(8,128)S(1)} %bitcast.7, ...), custom_call_target="tpu_custom_call" | custom-call | tf_op jit(solution)/shard_map/macro_first/pallas_call | solution.py:536
  29.2 0.5 all-to-all-done
  29.7 1.4 %sort_pieces.1 = f32[32,2,8,128]{3,2,1,0:T(8,128)} custom-call(f32[1152,128]{1,0:T(8,128)S(1)} %bitcast.6), custom_call_target="tpu_custom_call" | custom-call | tf_op jit(solution)/shard_map/sort_pieces/pallas_call | solution.py:617
  31.1 7.0 %all-to-all-start.1 = ((f32[32,2,8,128]{3,2,1,0:T(8,128)}), f32[32,2,8,128]{3,2,1,0:T(8,128)S(1)}, u32[]{:S(2)}, u32[]{:S(2)}) async-start(f32[32,2,8,128]{3,2,1,0:T(8,128)} %sort_pieces.1), calls=%async_computation.1 | async-start | bytes 524288 | tf_op jit(solution)/shard_map/all_to_all | solution.py:680
  38.1 6.0 %macro_last.1 = (f32[144,256]{1,0:T(8,128)S(1)}, f32[3,1024]{1,0:T(4,128)S(1)}, f32[3,1024]{1,0:T(4,128)S(1)}, f32[3,1024]{1,0:T(4,128)S(1)}, f32[3,1024]{1,0:T(4,128)S(1)}) custom-call(f32[8,4]{1,0:T(8,128)S(1)} %copy-done.8, s32[1]{0:T(128)} %bitcast.core_index, s32[1]{0:T(128)} %bitcast.1.pool_index, s32[2,9216]{1,0:T(2,128)S(1)} %get-tuple-element.25.table, ...), custom_call_target="tpu_custom_call" | custom-call | tf_op jit(solution)/shard_map/macro_last/pallas_call | solution.py:553
  44.0 0.0 copy-start.10
  44.1 0.2 collective-permute-start
  44.3 4.5 %collective-permute-start.1 = (f32[3,1024]{1,0:T(4,128)S(1)}, f32[3,1024]{1,0:T(4,128)S(1)}, u32[]{:S(2)}, u32[]{:S(2)}) collective-permute-start(f32[3,1024]{1,0:T(4,128)S(1)} %get-tuple-element.35), channel_id=1, source_target_pairs={{4,8},{12,16},{20,24},{28,32},{36,40},{44,48},{52,56},{60,64},{68,... | collective-permute-start | bytes 36872 | tf_op jit(solution)/shard_map/ppermute | solution.py:685
  48.8 0.4 collective-permute-start.2
  49.2 4.8 %collective-permute-start.3 = (f32[3,1024]{1,0:T(4,128)S(1)}, f32[3,1024]{1,0:T(4,128)S(1)}, u32[]{:S(2)}, u32[]{:S(2)}) collective-permute-start(f32[3,1024]{1,0:T(4,128)S(1)} %get-tuple-element.37), channel_id=1, source_target_pairs={{1,2},{2,1},{5,6},{6,5},{9,10},{10,9},{13,14},{14,13},{17,18},{18,... | collective-permute-start | bytes 36872 | tf_op jit(solution)/shard_map/ppermute | solution.py:685
  54.0 0.0 copy-done.10
  54.0 0.7 %copy.19 = f32[6,4]{0,1:T(4,128)} copy(f32[6,4]{1,0:T(8,128)S(1)} %copy-done.10) | data formatting | bytes 192
  54.7 0.0 copy-start.4
  54.7 0.0 copy-start.7
  54.7 0.0 all-to-all-done.1.pieces
  54.7 0.0 copy-start.9
  54.7 0.7 %copy-done.9 = f32[32,2,8,128]{3,2,1,0:T(8,128)} copy-done((f32[32,2,8,128]{3,2,1,0:T(8,128)}, f32[32,2,8,128]{3,2,1,0:T(8,128)S(1)}, u32[]{:S(2)}) %copy-start.9) | copy-done | bytes 262168
  55.4 1.7 %join_pieces.1 = f32[2,8,4096]{2,1,0:T(8,128)} custom-call(f32[32,2,8,128]{3,2,1,0:T(8,128)} %copy-done.9), custom_call_target="tpu_custom_call" | custom-call | tf_op jit(solution)/shard_map/join_pieces/pallas_call | solution.py:636
  57.0 0.0 collective-permute-done.r0
  57.1 0.0 collective-permute-done.1.r1
  57.1 0.0 collective-permute-done.2.r2
  57.1 0.0 collective-permute-done.3.r3
  57.1 0.0 copy-done.4
  57.1 0.0 copy-done.7
  57.1 1.5 %assemble.1 = f32[3,9216]{1,0:T(4,128)} custom-call(s32[1]{0:T(128)} %bitcast.core_index, s32[1]{0:T(128)} %bitcast.1.pool_index, f32[144,256]{1,0:T(8,128)S(1)} %get-tuple-element.33.own, s32[1,4,1024]{2,1,0:T(4,128)S(1)} %copy-done.6, f32[3,1024]{1,0:T(4,128)S(1)} %collective-permute-done.r0, f32[3,1024]{1,0:T(4,128)S(1)} %collective-permute-done.1.r1, ...), custom_call_target="tpu_custom_call" | custom-call | tf_op jit(solution)/shard_map/assemble/pallas_call | solution.py:590
Async XLA Ops:
  1.3 15.7 %copy-start.2 = (f32[3,9216]{1,0:T(4,128)S(1)}, f32[3,9216]{1,0:T(4,128)}, u32[]{:S(2)}) copy-start(f32[3,9216]{1,0:T(4,128)} %disp.3) | copy-start | bytes 331780
  6.7 10.3 %copy-start = (f32[3,8,8192]{2,1,0:T(8,128)S(1)}, f32[3,8,8192]{2,1,0:T(8,128)}, u32[]{:S(2)}) copy-start(f32[3,8,8192]{2,1,0:T(8,128)} %grads.5) | copy-start | bytes 2359300
  6.7 10.3 %copy-start.1 = (s32[8,8192]{1,0:T(8,128)S(1)}, s32[8,8192]{1,0:T(8,128)}, u32[]{:S(2)}) copy-start(s32[8,8192]{1,0:T(8,128)} %nm.5) | copy-start | bytes 786436
  6.7 10.3 %copy-start.3 = (f32[2,8192]{1,0:T(2,128)S(1)}, f32[2,8192]{1,0:T(2,128)}, u32[]{:S(2)}) copy-start(f32[2,8192]{1,0:T(2,128)} %moduli.3) | copy-start | bytes 196612
  6.7 10.3 %copy-start.5 = (f32[8192]{0:T(1024)S(1)}, f32[8192]{0:T(1024)}, u32[]{:S(2)}) copy-start(f32[8192]{0:T(1024)} %param.17) | copy-start | bytes 98308
  6.7 10.3 %copy-start.6 = (s32[1,4,1024]{2,1,0:T(4,128)S(1)}, s32[1,4,1024]{2,1,0:T(4,128)}, u32[]{:S(2)}) copy-start(s32[1,4,1024]{2,1,0:T(4,128)} %shared.3) | copy-start | bytes 49156
  6.7 10.3 %copy-start.8 = (f32[8,4]{1,0:T(8,128)S(1)}, f32[8,4]{1,0:T(8,128)}, u32[]{:S(2)}) copy-start(f32[8,4]{1,0:T(8,128)} %get-tuple-element.24.replace) | copy-start | bytes 388
  6.7 23.0 %all-to-all-start = ((f32[128,1,1152]{2,1,0:T(1,128)}), f32[128,1,1152]{2,1,0:T(1,128)S(1)}, u32[]{:S(2)}, u32[]{:S(2)}) async-start(f32[128,1,1152]{2,1,0:T(1,128)} %bitcast.10), calls=%async_computation | async-start | bytes 1179648 | tf_op jit(solution)/shard_map/all_to_all | solution.py:672
  31.1 23.6 %all-to-all-start.1 = ((f32[32,2,8,128]{3,2,1,0:T(8,128)}), f32[32,2,8,128]{3,2,1,0:T(8,128)S(1)}, u32[]{:S(2)}, u32[]{:S(2)}) async-start(f32[32,2,8,128]{3,2,1,0:T(8,128)} %sort_pieces.1), calls=%async_computation.1 | async-start | bytes 524288 | tf_op jit(solution)/shard_map/all_to_all | solution.py:680
  44.0 10.0 %copy-start.10 = (f32[6,4]{1,0:T(8,128)S(1)}, f32[6,4]{1,0:T(8,128)}, u32[]{:S(2)}) copy-start(f32[6,4]{1,0:T(8,128)} %get-tuple-element.49) | copy-start | bytes 292
  44.1 13.0 %collective-permute-start = (f32[3,1024]{1,0:T(4,128)S(1)}, f32[3,1024]{1,0:T(4,128)S(1)}, u32[]{:S(2)}, u32[]{:S(2)}) collective-permute-start(f32[3,1024]{1,0:T(4,128)S(1)} %get-tuple-element.34), channel_id=1, source_target_pairs={{0,4},{4,0},{1,5},{5,1},{2,6},{6,2},{3,7},{7,3},{8,12},{12,8},{9,1... | collective-permute-start | bytes 36872 | tf_op jit(solution)/shard_map/ppermute | solution.py:685
  44.3 12.8 %collective-permute-start.1 = (f32[3,1024]{1,0:T(4,128)S(1)}, f32[3,1024]{1,0:T(4,128)S(1)}, u32[]{:S(2)}, u32[]{:S(2)}) collective-permute-start(f32[3,1024]{1,0:T(4,128)S(1)} %get-tuple-element.35), channel_id=1, source_target_pairs={{4,8},{12,16},{20,24},{28,32},{36,40},{44,48},{52,56},{60,64},{68,... | collective-permute-start | bytes 36872 | tf_op jit(solution)/shard_map/ppermute | solution.py:685
  48.8 8.2 %collective-permute-start.2 = (f32[3,1024]{1,0:T(4,128)S(1)}, f32[3,1024]{1,0:T(4,128)S(1)}, u32[]{:S(2)}, u32[]{:S(2)}) collective-permute-start(f32[3,1024]{1,0:T(4,128)S(1)} %get-tuple-element.36), channel_id=1, source_target_pairs={{0,1},{2,3},{1,0},{3,2},{4,5},{6,7},{5,4},{7,6},{8,9},{10,11},{9,8... | collective-permute-start | bytes 36872 | tf_op jit(solution)/shard_map/ppermute | solution.py:685
  49.2 7.8 %collective-permute-start.3 = (f32[3,1024]{1,0:T(4,128)S(1)}, f32[3,1024]{1,0:T(4,128)S(1)}, u32[]{:S(2)}, u32[]{:S(2)}) collective-permute-start(f32[3,1024]{1,0:T(4,128)S(1)} %get-tuple-element.37), channel_id=1, source_target_pairs={{1,2},{2,1},{5,6},{6,5},{9,10},{10,9},{13,14},{14,13},{17,18},{18,... | collective-permute-start | bytes 36872 | tf_op jit(solution)/shard_map/ppermute | solution.py:685
  54.7 2.4 %copy-start.4 = (f32[3,9216]{1,0:T(4,128)S(1)}, f32[3,9216]{1,0:T(4,128)}, u32[]{:S(2)}) copy-start(f32[3,9216]{1,0:T(4,128)} %external.1) | copy-start | bytes 331780
  54.7 2.4 %copy-start.7 = (f32[9216]{0:T(1024)S(1)}, f32[9216]{0:T(1024)}, u32[]{:S(2)}) copy-start(f32[9216]{0:T(1024)} %param.20) | copy-start | bytes 110596
  54.7 0.7 %copy-start.9 = (f32[32,2,8,128]{3,2,1,0:T(8,128)}, f32[32,2,8,128]{3,2,1,0:T(8,128)S(1)}, u32[]{:S(2)}) copy-start(f32[32,2,8,128]{3,2,1,0:T(8,128)S(1)} %all-to-all-done.1.pieces) | copy-start | bytes 786436

commit v8 on v7

--- a/solution.py
+++ b/solution.py
@@ -296,8 +296,11 @@
         total = jnp.zeros((8, 2 * LANES), f32)
         for x in range(G):
             total = total + slab_stress(st[k, 8 * x : 8 * x + 8, :], first_rows)
-        mean = jnp.sum(total, axis=1, keepdims=True) * (1.0 / NV)
-        result = jnp.where((lane == k) & live, jnp.broadcast_to(mean, (8, LANES)), result)
+        mean = jnp.where(live, jnp.sum(total, axis=1, keepdims=True) * (1.0 / NV), 0.0)
+        mean = jnp.broadcast_to(mean, (8, LANES))
+        result = jnp.where(lane == k, mean, result)
+        across = jnp.sum(jnp.where(lane == row, mean, 0.0), axis=0, keepdims=True)
+        band_stress[k : k + 1, :] = across[:, 0:6]
         pool = owner[0, k] & 3
 
         @pl.when(live)
@@ -310,7 +313,6 @@
             brick = (owner[0, k] >> 2).astype(f32)
             send[pl.ds(9 * pool + 8, TILES, stride=36), :] = jnp.full((TILES, LANES), brick, f32)
 
-    band_stress[...] = result[0:6, 0:4]
     for k in range(4):
         live_element = jnp.where(k < count[0], element[0, k], -1).astype(f32)
         result = jnp.where((lane == k) & (row == 6), live_element, result)
@@ -322,7 +324,7 @@
         cells_kernel,
         out_shape=(
             jax.ShapeDtypeStruct((36 * TILES, LANES), f32),
-            jax.ShapeDtypeStruct((6, 4), f32),
+            jax.ShapeDtypeStruct((4, 6), f32),
             jax.ShapeDtypeStruct((8, 4), f32),
         ),
         in_specs=[pl.BlockSpec(memory_space=SMEM)] * 3 + [pl.BlockSpec(memory_space=VMEM)] * 6,
@@ -564,7 +566,14 @@
     )(*arguments)
 
 
-def assemble_kernel(core_index, pool_index, own, shared, r0, r1, r2, r3, external, mass, out):
+def assemble_kernel(
+    core_index, pool_index, own, shared, r0, r1, r2, r3, external, mass, pieces, out, fields, joined, sem
+):
+    for i in range(TILES):
+        for s in range(2):
+            joined[s, :, i * LANES : (i + 1) * LANES] = pieces[i, s]
+    copy = pltpu.make_async_copy(joined, fields, sem)
+    copy.start()
     total = None
     for face, arrived in zip(face_lists(core_index[0], pool_index[0]), (r0, r1, r2, r3)):
         for part in range(4):
@@ -583,18 +592,23 @@
         for r in range(36):
             out[c : c + 1, r * LO : (r + 1) * LO] = whole[r : r + 1]
     out[...] = (external[...] - out[...]) / mass[...]
-
-
-def assemble(place, own, shared, arrived, external, mass):
+    copy.wait()
+
+
+def assemble(place, own, shared, arrived, external, mass, pieces):
     vmem = pl.BlockSpec(memory_space=VMEM)
     return pl.pallas_call(
         assemble_kernel,
-        out_shape=jax.ShapeDtypeStruct(external.shape, f32),
-        in_specs=[pl.BlockSpec(memory_space=SMEM)] * 2 + [vmem] * 8,
-        out_specs=vmem,
+        out_shape=(
+            jax.ShapeDtypeStruct(external.shape, f32),
+            jax.ShapeDtypeStruct((2, 8, NV), f32),
+        ),
+        in_specs=[pl.BlockSpec(memory_space=SMEM)] * 2 + [vmem] * 9,
+        out_specs=(vmem, pl.BlockSpec(memory_space=pl.ANY)),
+        scratch_shapes=[VMEM((2, 8, NV), f32), pltpu.SemaphoreType.DMA],
         compiler_params=pltpu.CompilerParams(vmem_limit_bytes=32 << 20),
         name="assemble",
-    )(*place, own, shared, *arrived, external, mass)
+    )(*place, own, shared, *arrived, external, mass, pieces)
 
 
 def sort_kernel(pieces, out, order, places, sem):
@@ -622,23 +636,6 @@
         scratch_shapes=[VMEM((8, LANES), jnp.int32), SMEM((8, LANES), jnp.int32), pltpu.SemaphoreType.DMA],
         compiler_params=pltpu.CompilerParams(vmem_limit_bytes=32 << 20),
         name="sort_pieces",
-    )(pieces)
-
-
-def join_kernel(pieces, out):
-    for i in range(TILES):
-        for s in range(2):
-            out[s, :, i * LANES : (i + 1) * LANES] = pieces[i, s]
-
-
-def join_pieces(pieces):
-    vmem = pl.BlockSpec(memory_space=VMEM)
-    return pl.pallas_call(
-        join_kernel,
-        out_shape=jax.ShapeDtypeStruct((2, 8, NV), f32),
-        in_specs=[vmem],
-        out_specs=vmem,
-        name="join_pieces",
     )(pieces)
 
 
@@ -690,12 +687,10 @@
         swap(faces[2], "pool", pools, 0),
         swap(faces[3], "pool", pools, 1),
     )
-    owned_fields = join_pieces(mine)
-    *arrived, owned_fields = lax.optimization_barrier((*arrived, owned_fields))
-    acceleration = assemble(
-        place, own, shared_nodes, arrived, external_force, nodal_mass.reshape(1, -1)
-    )
-    return (acceleration, band_stress, owned_fields)
+    acceleration, owned_fields = assemble(
+        place, own, shared_nodes, arrived, external_force, nodal_mass.reshape(1, -1), mine
+    )
+    return (acceleration, band_stress.T, owned_fields)
 
 
 def solution(mesh):

time: 59 us -> 58.4 us (0.990)
  waiting for transfers between devices: 0.53 us -> 2.21 us
  local copies, waits for them, and re-layouts: 1.41 us -> 0.05 us
  Pallas kernels: 28.1 us -> 27.1 us
    ppermute x4, waiting for transfers between devices: 0.01 us -> 1.68 us  [swap(): return lax.ppermute(array, axis, steps + [(j, i) for i, j in steps])]
    unnamed x23 -> x18, local copies, waits for them, and re-layouts: 1.41 us -> 0.05 us
    pallas_call x2 -> x1, Pallas kernels: 3.19 us -> 2.17 us  [assemble(): pl.pallas_call(assemble_kernel, out_shape=(jax.ShapeDtypeStruct(external....]
  transfers between devices with their start and end apart: 6 -> 6, of which waited for: 1 -> 2; matrix products, arithmetic and copies ran while one was open for 1% -> 0% of each run, Pallas kernels for 34% -> 31%
where the time goes in v8:
time: 58.4 us; the launch traced here: 57.9 us
  Pallas kernels  27.1 us (46%)
  starting transfers between devices  27 us (46%)
  waiting for transfers between devices  2.21 us (4%)
  between operations  1.48 us (3%)
    pallas_call x1, Pallas kernels, macro_first(): pl.pallas_call(functools.partial(macro_first_kernel, UNROLL), out_shape=(...  12.2 us
    all_to_all x1, starting transfers between devices, shards(): lax.all_to_all(send.reshape(bricks * pools, 1, 9 * LANES), BOTH, split_ax...  10.2 us
    ppermute x4, starting transfers between devices, swap(): return lax.ppermute(array, axis, steps + [(j, i) for i, j in steps])  9.9 us
    all_to_all x1, starting transfers between devices, shards(): lax.all_to_all(sorted_pieces, BRICK, split_axis=0, concat_axis=0, tiled=T...  6.96 us
    pallas_call x1, Pallas kernels, macro_last(): pl.pallas_call(functools.partial(macro_last_kernel, UNROLL), out_shape=(j...  5.95 us
    pallas_call x1, Pallas kernels, solve_cells(): pl.pallas_call(cells_kernel, out_shape=(jax.ShapeDtypeStruct((36 * TILES,...  5.43 us
    pallas_call x1, Pallas kernels, assemble(): pl.pallas_call(assemble_kernel, out_shape=(jax.ShapeDtypeStruct(external....  2.17 us
    ppermute x4, waiting for transfers between devices, swap(): return lax.ppermute(array, axis, steps + [(j, i) for i, j in steps])  1.68 us
  transfers between devices with their start and end apart: 6, of which 2 were waited for; matrix products, arithmetic and copies ran while one was open for 0% of the time, Pallas kernels for 31%

profile of v8, /device:TPU:40, one launch (start us, length us, event | category | flops | bytes accessed | tf_op | source)
XLA Modules:
  0.0 57.9 jit_solution(8822526326936117886)
XLA Ops:
  1.3 0.0 copy-start.2
  1.3 5.4 %cells.1 = (f32[1152,128]{1,0:T(8,128)}, f32[4,6]{1,0:T(4,128)}, f32[8,4]{1,0:T(8,128)}) custom-call(s32[1]{0:T(128)S(6)} %copy.18.count, s32[1,4]{1,0:T(1,128)} %owner.1, s32[1,4]{1,0:T(1,128)} %element.1, f32[3,9216]{1,0:T(4,128)} %disp.3, s32[8,8192]{1,0:T(8,128)} %nm.5, f32[3,8,8192]{2,1,0:T(8,128)} %grads.5, f32[4,8,4096]{2,1,0:T(8,128)} %micro.1, ...), custom_call_target="tpu_custom_call" | custom-call | tf_op jit(solution)/shard_map/cells/pallas_call | solution.py:323
  6.7 0.0 copy-start
  6.7 0.0 copy-start.1
  6.7 0.0 copy-start.3
  6.7 0.0 copy-start.5
  6.7 0.0 copy-start.6
  6.8 0.0 copy-start.8
  6.8 10.2 %all-to-all-start = ((f32[128,1,1152]{2,1,0:T(1,128)}), f32[128,1,1152]{2,1,0:T(1,128)S(1)}, u32[]{:S(2)}, u32[]{:S(2)}) async-start(f32[128,1,1152]{2,1,0:T(1,128)} %bitcast.11), calls=%async_computation | async-start | bytes 1179648 | tf_op jit(solution)/shard_map/all_to_all | solution.py:669
  17.0 0.0 copy-done.2
  17.0 0.0 copy-done
  17.0 0.0 copy-done.1
  17.0 0.0 copy-done.3
  17.0 0.0 copy-done.5
  17.0 0.0 copy-done.6
  17.0 0.0 copy-done.8
  17.0 12.2 %macro_first.1 = (f32[288,256]{1,0:T(8,128)S(1)}, s32[2,9216]{1,0:T(2,128)S(1)}, f32[1,128]{1,0:T(1,128)S(1)}, s32[4,8,128]{2,1,0:T(8,128)S(1)}) custom-call(f32[8,4]{1,0:T(8,128)S(1)} %copy-done.8, f32[3,9216]{1,0:T(4,128)S(1)} %copy-done.2, s32[8,8192]{1,0:T(8,128)S(1)} %copy-done.1, f32[3,8,8192]{2,1,0:T(8,128)S(1)} %copy-done, f32[64,128]{1,0:T(8,128)S(1)} %bitcast.8, ...), custom_call_target="tpu_custom_call" | custom-call | tf_op jit(solution)/shard_map/macro_first/pallas_call | solution.py:538
  29.2 0.5 all-to-all-done
  29.7 1.4 %sort_pieces.1 = f32[32,2,8,128]{3,2,1,0:T(8,128)} custom-call(f32[1152,128]{1,0:T(8,128)S(1)} %bitcast.7), custom_call_target="tpu_custom_call" | custom-call | tf_op jit(solution)/shard_map/sort_pieces/pallas_call | solution.py:631
  31.1 7.0 %all-to-all-start.1 = ((f32[32,2,8,128]{3,2,1,0:T(8,128)}), f32[32,2,8,128]{3,2,1,0:T(8,128)S(1)}, u32[]{:S(2)}, u32[]{:S(2)}) async-start(f32[32,2,8,128]{3,2,1,0:T(8,128)} %sort_pieces.1), calls=%async_computation.1 | async-start | bytes 524288 | tf_op jit(solution)/shard_map/all_to_all | solution.py:677
  38.1 0.0 copy-start.4
  38.1 0.0 copy-start.7
  38.1 6.0 %macro_last.1 = (f32[144,256]{1,0:T(8,128)S(1)}, f32[3,1024]{1,0:T(4,128)S(1)}, f32[3,1024]{1,0:T(4,128)S(1)}, f32[3,1024]{1,0:T(4,128)S(1)}, f32[3,1024]{1,0:T(4,128)S(1)}) custom-call(f32[8,4]{1,0:T(8,128)S(1)} %copy-done.8, s32[1]{0:T(128)} %bitcast.core_index, s32[1]{0:T(128)} %bitcast.1.pool_index, s32[2,9216]{1,0:T(2,128)S(1)} %get-tuple-element.22.table, ...), custom_call_target="tpu_custom_call" | custom-call | tf_op jit(solution)/shard_map/macro_last/pallas_call | solution.py:555
  44.1 0.2 collective-permute-start
  44.3 4.5 %collective-permute-start.1 = (f32[3,1024]{1,0:T(4,128)S(1)}, f32[3,1024]{1,0:T(4,128)S(1)}, u32[]{:S(2)}, u32[]{:S(2)}) collective-permute-start(f32[3,1024]{1,0:T(4,128)S(1)} %get-tuple-element.32), channel_id=1, source_target_pairs={{4,8},{12,16},{20,24},{28,32},{36,40},{44,48},{52,56},{60,64},{68,... | collective-permute-start | bytes 36872 | tf_op jit(solution)/shard_map/ppermute | solution.py:682
  48.8 0.4 collective-permute-start.2
  49.2 4.8 %collective-permute-start.3 = (f32[3,1024]{1,0:T(4,128)S(1)}, f32[3,1024]{1,0:T(4,128)S(1)}, u32[]{:S(2)}, u32[]{:S(2)}) collective-permute-start(f32[3,1024]{1,0:T(4,128)S(1)} %get-tuple-element.34), channel_id=1, source_target_pairs={{1,2},{2,1},{5,6},{6,5},{9,10},{10,9},{13,14},{14,13},{17,18},{18,... | collective-permute-start | bytes 36872 | tf_op jit(solution)/shard_map/ppermute | solution.py:682
  54.0 0.0 collective-permute-done.r0
  54.0 0.0 collective-permute-done.1.r1
  54.0 0.0 collective-permute-done.2.r2
  54.0 1.7 %collective-permute-done.3.r3 = f32[3,1024]{1,0:T(4,128)S(1)} collective-permute-done((f32[3,1024]{1,0:T(4,128)S(1)}, f32[3,1024]{1,0:T(4,128)S(1)}, u32[]{:S(2)}, u32[]{:S(2)}) %collective-permute-start.3) | collective-permute-done | bytes 12320 | tf_op jit(solution)/shard_map/ppermute | solution.py:682
  55.7 0.0 all-to-all-done.1.pieces
  55.7 0.0 copy-done.4
  55.7 0.0 copy-done.7
  55.7 2.2 %assemble.1 = (f32[3,9216]{1,0:T(4,128)}, f32[2,8,4096]{2,1,0:T(8,128)}) custom-call(s32[1]{0:T(128)} %bitcast.core_index, s32[1]{0:T(128)} %bitcast.1.pool_index, f32[144,256]{1,0:T(8,128)S(1)} %get-tuple-element.30.own, s32[1,4,1024]{2,1,0:T(4,128)S(1)} %copy-done.6, f32[3,1024]{1,0:T(4,128)S(1)} %collective-permute-done.r0, ...), custom_call_target="tpu_custom_call" | custom-call | tf_op jit(solution)/shard_map/assemble/pallas_call | solution.py:600
Async XLA Ops:
  1.3 15.7 %copy-start.2 = (f32[3,9216]{1,0:T(4,128)S(1)}, f32[3,9216]{1,0:T(4,128)}, u32[]{:S(2)}) copy-start(f32[3,9216]{1,0:T(4,128)} %disp.3) | copy-start | bytes 331780
  6.7 10.3 %copy-start = (f32[3,8,8192]{2,1,0:T(8,128)S(1)}, f32[3,8,8192]{2,1,0:T(8,128)}, u32[]{:S(2)}) copy-start(f32[3,8,8192]{2,1,0:T(8,128)} %grads.5) | copy-start | bytes 2359300
  6.7 10.3 %copy-start.1 = (s32[8,8192]{1,0:T(8,128)S(1)}, s32[8,8192]{1,0:T(8,128)}, u32[]{:S(2)}) copy-start(s32[8,8192]{1,0:T(8,128)} %nm.5) | copy-start | bytes 786436
  6.7 10.3 %copy-start.3 = (f32[2,8192]{1,0:T(2,128)S(1)}, f32[2,8192]{1,0:T(2,128)}, u32[]{:S(2)}) copy-start(f32[2,8192]{1,0:T(2,128)} %moduli.3) | copy-start | bytes 196612
  6.7 10.3 %copy-start.5 = (f32[8192]{0:T(1024)S(1)}, f32[8192]{0:T(1024)}, u32[]{:S(2)}) copy-start(f32[8192]{0:T(1024)} %param.17) | copy-start | bytes 98308
  6.7 10.3 %copy-start.6 = (s32[1,4,1024]{2,1,0:T(4,128)S(1)}, s32[1,4,1024]{2,1,0:T(4,128)}, u32[]{:S(2)}) copy-start(s32[1,4,1024]{2,1,0:T(4,128)} %shared.3) | copy-start | bytes 49156
  6.8 10.3 %copy-start.8 = (f32[8,4]{1,0:T(8,128)S(1)}, f32[8,4]{1,0:T(8,128)}, u32[]{:S(2)}) copy-start(f32[8,4]{1,0:T(8,128)} %get-tuple-element.21.replace) | copy-start | bytes 388
  6.8 23.0 %all-to-all-start = ((f32[128,1,1152]{2,1,0:T(1,128)}), f32[128,1,1152]{2,1,0:T(1,128)S(1)}, u32[]{:S(2)}, u32[]{:S(2)}) async-start(f32[128,1,1152]{2,1,0:T(1,128)} %bitcast.11), calls=%async_computation | async-start | bytes 1179648 | tf_op jit(solution)/shard_map/all_to_all | solution.py:669
  31.1 24.6 %all-to-all-start.1 = ((f32[32,2,8,128]{3,2,1,0:T(8,128)}), f32[32,2,8,128]{3,2,1,0:T(8,128)S(1)}, u32[]{:S(2)}, u32[]{:S(2)}) async-start(f32[32,2,8,128]{3,2,1,0:T(8,128)} %sort_pieces.1), calls=%async_computation.1 | async-start | bytes 524288 | tf_op jit(solution)/shard_map/all_to_all | solution.py:677
  38.1 17.6 %copy-start.4 = (f32[3,9216]{1,0:T(4,128)S(1)}, f32[3,9216]{1,0:T(4,128)}, u32[]{:S(2)}) copy-start(f32[3,9216]{1,0:T(4,128)} %external.1) | copy-start | bytes 331780
  38.1 17.6 %copy-start.7 = (f32[9216]{0:T(1024)S(1)}, f32[9216]{0:T(1024)}, u32[]{:S(2)}) copy-start(f32[9216]{0:T(1024)} %param.20) | copy-start | bytes 110596
  44.1 9.9 %collective-permute-start = (f32[3,1024]{1,0:T(4,128)S(1)}, f32[3,1024]{1,0:T(4,128)S(1)}, u32[]{:S(2)}, u32[]{:S(2)}) collective-permute-start(f32[3,1024]{1,0:T(4,128)S(1)} %get-tuple-element.31), channel_id=1, source_target_pairs={{0,4},{4,0},{1,5},{5,1},{2,6},{6,2},{3,7},{7,3},{8,12},{12,8},{9,1... | collective-permute-start | bytes 36872 | tf_op jit(solution)/shard_map/ppermute | solution.py:682
  44.3 9.7 %collective-permute-start.1 = (f32[3,1024]{1,0:T(4,128)S(1)}, f32[3,1024]{1,0:T(4,128)S(1)}, u32[]{:S(2)}, u32[]{:S(2)}) collective-permute-start(f32[3,1024]{1,0:T(4,128)S(1)} %get-tuple-element.32), channel_id=1, source_target_pairs={{4,8},{12,16},{20,24},{28,32},{36,40},{44,48},{52,56},{60,64},{68,... | collective-permute-start | bytes 36872 | tf_op jit(solution)/shard_map/ppermute | solution.py:682
  48.8 5.2 %collective-permute-start.2 = (f32[3,1024]{1,0:T(4,128)S(1)}, f32[3,1024]{1,0:T(4,128)S(1)}, u32[]{:S(2)}, u32[]{:S(2)}) collective-permute-start(f32[3,1024]{1,0:T(4,128)S(1)} %get-tuple-element.33), channel_id=1, source_target_pairs={{0,1},{2,3},{1,0},{3,2},{4,5},{6,7},{5,4},{7,6},{8,9},{10,11},{9,8... | collective-permute-start | bytes 36872 | tf_op jit(solution)/shard_map/ppermute | solution.py:682
  49.2 6.5 %collective-permute-start.3 = (f32[3,1024]{1,0:T(4,128)S(1)}, f32[3,1024]{1,0:T(4,128)S(1)}, u32[]{:S(2)}, u32[]{:S(2)}) collective-permute-start(f32[3,1024]{1,0:T(4,128)S(1)} %get-tuple-element.34), channel_id=1, source_target_pairs={{1,2},{2,1},{5,6},{6,5},{9,10},{10,9},{13,14},{14,13},{17,18},{18,... | collective-permute-start | bytes 36872 | tf_op jit(solution)/shard_map/ppermute | solution.py:682

commit v9 on v8

--- a/solution.py
+++ b/solution.py
@@ -478,7 +478,7 @@
 
 
 def face_lists(core, pool):
-    return 1 - core, core, 3 - (pool & 1), 2 + (pool & 1)
+    return core, 2 + (pool & 1), 3 - (pool & 1), 1 - core
 
 
 def macro_last_kernel(
@@ -495,10 +495,10 @@
     so_far,
     face_nodes,
     own,
+    to_brick,
+    to_odd,
+    to_even,
     to_core,
-    to_brick,
-    to_even,
-    to_odd,
     sums,
     faces,
 ):
@@ -529,7 +529,7 @@
                     4 + face : 5 + face
                 ]
     lists = face_lists(core_index[0], pool_index[0])
-    for face, out in zip(lists, (to_core, to_brick, to_even, to_odd)):
+    for face, out in zip(lists, (to_brick, to_odd, to_even, to_core)):
         out[...] = faces[face]
 
 
@@ -682,10 +682,10 @@
         return lax.ppermute(array, axis, steps + [(j, i) for i, j in steps])
 
     arrived = (
-        swap(faces[0], "core", 2, 0),
-        swap(faces[1], BRICK, bricks, 1),
+        swap(faces[0], BRICK, bricks, 1),
+        swap(faces[1], "pool", pools, 1),
         swap(faces[2], "pool", pools, 0),
-        swap(faces[3], "pool", pools, 1),
+        swap(faces[3], "core", 2, 0),
     )
     acceleration, owned_fields = assemble(
         place, own, shared_nodes, arrived, external_force, nodal_mass.reshape(1, -1), mine

time: 58.4 us -> 58.5 us (level)
  waiting for transfers between devices: 2.21 us -> 4.14 us
  starting transfers between devices: 27 us -> 25.3 us
    ppermute x4, waiting for transfers between devices: 1.68 us -> 3.63 us  [swap(): return lax.ppermute(array, axis, steps + [(j, i) for i, j in steps])]
    ppermute x4, starting transfers between devices: 9.9 us -> 8.16 us  [swap(): return lax.ppermute(array, axis, steps + [(j, i) for i, j in steps])]
  transfers between devices with their start and end apart: 6 -> 6, of which waited for: 2 -> 3; matrix products, arithmetic and copies ran while one was open for 0% -> 0% of each run, Pallas kernels for 31% -> 31%
where the time goes in v9:
time: 58.5 us; the launch traced here: 58.1 us
  Pallas kernels  27.1 us (46%)
  starting transfers between devices  25.3 us (43%)
  waiting for transfers between devices  4.14 us (7%)
  between operations  1.49 us (3%)
    pallas_call x1, Pallas kernels, macro_first(): pl.pallas_call(functools.partial(macro_first_kernel, UNROLL), out_shape=(...  12.2 us
    all_to_all x1, starting transfers between devices, shards(): lax.all_to_all(send.reshape(bricks * pools, 1, 9 * LANES), BOTH, split_ax...  10.2 us
    ppermute x4, starting transfers between devices, swap(): return lax.ppermute(array, axis, steps + [(j, i) for i, j in steps])  8.16 us
    all_to_all x1, starting transfers between devices, shards(): lax.all_to_all(sorted_pieces, BRICK, split_axis=0, concat_axis=0, tiled=T...  6.95 us
    pallas_call x1, Pallas kernels, macro_last(): pl.pallas_call(functools.partial(macro_last_kernel, UNROLL), out_shape=(j...  5.96 us
    pallas_call x1, Pallas kernels, solve_cells(): pl.pallas_call(cells_kernel, out_shape=(jax.ShapeDtypeStruct((36 * TILES,...  5.43 us
    ppermute x4, waiting for transfers between devices, swap(): return lax.ppermute(array, axis, steps + [(j, i) for i, j in steps])  3.63 us
    pallas_call x1, Pallas kernels, assemble(): pl.pallas_call(assemble_kernel, out_shape=(jax.ShapeDtypeStruct(external....  2.18 us
  transfers between devices with their start and end apart: 6, of which 3 were waited for; matrix products, arithmetic and copies ran while one was open for 0% of the time, Pallas kernels for 31%

profile of v9, /device:TPU:40, one launch (start us, length us, event | category | flops | bytes accessed | tf_op | source)
XLA Modules:
  0.0 58.1 jit_solution(732016532534673438)
XLA Ops:
  1.3 0.0 copy-start.2
  1.3 5.4 %cells.1 = (f32[1152,128]{1,0:T(8,128)}, f32[4,6]{1,0:T(4,128)}, f32[8,4]{1,0:T(8,128)}) custom-call(s32[1]{0:T(128)S(6)} %copy.18.count, s32[1,4]{1,0:T(1,128)} %owner.1, s32[1,4]{1,0:T(1,128)} %element.1, f32[3,9216]{1,0:T(4,128)} %disp.3, s32[8,8192]{1,0:T(8,128)} %nm.5, f32[3,8,8192]{2,1,0:T(8,128)} %grads.5, f32[4,8,4096]{2,1,0:T(8,128)} %micro.1, ...), custom_call_target="tpu_custom_call" | custom-call | tf_op jit(solution)/shard_map/cells/pallas_call | solution.py:323
  6.7 0.0 copy-start
  6.7 0.0 copy-start.1
  6.7 0.0 copy-start.3
  6.7 0.0 copy-start.5
  6.7 0.0 copy-start.6
  6.8 0.0 copy-start.8
  6.8 10.2 %all-to-all-start = ((f32[128,1,1152]{2,1,0:T(1,128)}), f32[128,1,1152]{2,1,0:T(1,128)S(1)}, u32[]{:S(2)}, u32[]{:S(2)}) async-start(f32[128,1,1152]{2,1,0:T(1,128)} %bitcast.11), calls=%async_computation | async-start | bytes 1179648 | tf_op jit(solution)/shard_map/all_to_all | solution.py:669
  17.0 0.0 copy-done.2
  17.0 0.0 copy-done
  17.0 0.0 copy-done.1
  17.0 0.0 copy-done.3
  17.0 0.0 copy-done.5
  17.0 0.0 copy-done.6
  17.0 0.0 copy-done.8
  17.0 12.2 %macro_first.1 = (f32[288,256]{1,0:T(8,128)S(1)}, s32[2,9216]{1,0:T(2,128)S(1)}, f32[1,128]{1,0:T(1,128)S(1)}, s32[4,8,128]{2,1,0:T(8,128)S(1)}) custom-call(f32[8,4]{1,0:T(8,128)S(1)} %copy-done.8, f32[3,9216]{1,0:T(4,128)S(1)} %copy-done.2, s32[8,8192]{1,0:T(8,128)S(1)} %copy-done.1, f32[3,8,8192]{2,1,0:T(8,128)S(1)} %copy-done, f32[64,128]{1,0:T(8,128)S(1)} %bitcast.8, ...), custom_call_target="tpu_custom_call" | custom-call | tf_op jit(solution)/shard_map/macro_first/pallas_call | solution.py:538
  29.2 0.5 all-to-all-done
  29.7 1.4 %sort_pieces.1 = f32[32,2,8,128]{3,2,1,0:T(8,128)} custom-call(f32[1152,128]{1,0:T(8,128)S(1)} %bitcast.7), custom_call_target="tpu_custom_call" | custom-call | tf_op jit(solution)/shard_map/sort_pieces/pallas_call | solution.py:631
  31.1 7.0 %all-to-all-start.1 = ((f32[32,2,8,128]{3,2,1,0:T(8,128)}), f32[32,2,8,128]{3,2,1,0:T(8,128)S(1)}, u32[]{:S(2)}, u32[]{:S(2)}) async-start(f32[32,2,8,128]{3,2,1,0:T(8,128)} %sort_pieces.1), calls=%async_computation.1 | async-start | bytes 524288 | tf_op jit(solution)/shard_map/all_to_all | solution.py:677
  38.1 0.0 copy-start.4
  38.1 0.0 copy-start.7
  38.1 6.0 %macro_last.1 = (f32[144,256]{1,0:T(8,128)S(1)}, f32[3,1024]{1,0:T(4,128)S(1)}, f32[3,1024]{1,0:T(4,128)S(1)}, f32[3,1024]{1,0:T(4,128)S(1)}, f32[3,1024]{1,0:T(4,128)S(1)}) custom-call(f32[8,4]{1,0:T(8,128)S(1)} %copy-done.8, s32[1]{0:T(128)} %bitcast.core_index, s32[1]{0:T(128)} %bitcast.1.pool_index, s32[2,9216]{1,0:T(2,128)S(1)} %get-tuple-element.22.table, ...), custom_call_target="tpu_custom_call" | custom-call | tf_op jit(solution)/shard_map/macro_last/pallas_call | solution.py:555
  44.1 4.3 %collective-permute-start = (f32[3,1024]{1,0:T(4,128)S(1)}, f32[3,1024]{1,0:T(4,128)S(1)}, u32[]{:S(2)}, u32[]{:S(2)}) collective-permute-start(f32[3,1024]{1,0:T(4,128)S(1)} %get-tuple-element.31), channel_id=1, source_target_pairs={{4,8},{12,16},{20,24},{28,32},{36,40},{44,48},{52,56},{60,64},{68,... | collective-permute-start | bytes 36872 | tf_op jit(solution)/shard_map/ppermute | solution.py:682
  48.4 3.7 %collective-permute-start.1 = (f32[3,1024]{1,0:T(4,128)S(1)}, f32[3,1024]{1,0:T(4,128)S(1)}, u32[]{:S(2)}, u32[]{:S(2)}) collective-permute-start(f32[3,1024]{1,0:T(4,128)S(1)} %get-tuple-element.32), channel_id=1, source_target_pairs={{1,2},{2,1},{5,6},{6,5},{9,10},{10,9},{13,14},{14,13},{17,18},{18,... | collective-permute-start | bytes 36872 | tf_op jit(solution)/shard_map/ppermute | solution.py:682
  52.1 0.1 collective-permute-start.2
  52.2 0.1 collective-permute-start.3
  52.3 0.0 collective-permute-done.r0
  52.3 1.8 %collective-permute-done.1.r1 = f32[3,1024]{1,0:T(4,128)S(1)} collective-permute-done((f32[3,1024]{1,0:T(4,128)S(1)}, f32[3,1024]{1,0:T(4,128)S(1)}, u32[]{:S(2)}, u32[]{:S(2)}) %collective-permute-start.1) | collective-permute-done | bytes 12320 | tf_op jit(solution)/shard_map/ppermute | solution.py:682
  54.0 1.9 %collective-permute-done.2.r2 = f32[3,1024]{1,0:T(4,128)S(1)} collective-permute-done((f32[3,1024]{1,0:T(4,128)S(1)}, f32[3,1024]{1,0:T(4,128)S(1)}, u32[]{:S(2)}, u32[]{:S(2)}) %collective-permute-start.2) | collective-permute-done | bytes 12320 | tf_op jit(solution)/shard_map/ppermute | solution.py:682
  55.9 0.0 collective-permute-done.3.r3
  55.9 0.0 all-to-all-done.1.pieces
  55.9 0.0 copy-done.4
  55.9 0.0 copy-done.7
  55.9 2.2 %assemble.1 = (f32[3,9216]{1,0:T(4,128)}, f32[2,8,4096]{2,1,0:T(8,128)}) custom-call(s32[1]{0:T(128)} %bitcast.core_index, s32[1]{0:T(128)} %bitcast.1.pool_index, f32[144,256]{1,0:T(8,128)S(1)} %get-tuple-element.30.own, s32[1,4,1024]{2,1,0:T(4,128)S(1)} %copy-done.6, f32[3,1024]{1,0:T(4,128)S(1)} %collective-permute-done.r0, ...), custom_call_target="tpu_custom_call" | custom-call | tf_op jit(solution)/shard_map/assemble/pallas_call | solution.py:600
Async XLA Ops:
  1.3 15.7 %copy-start.2 = (f32[3,9216]{1,0:T(4,128)S(1)}, f32[3,9216]{1,0:T(4,128)}, u32[]{:S(2)}) copy-start(f32[3,9216]{1,0:T(4,128)} %disp.3) | copy-start | bytes 331780
  6.7 10.3 %copy-start = (f32[3,8,8192]{2,1,0:T(8,128)S(1)}, f32[3,8,8192]{2,1,0:T(8,128)}, u32[]{:S(2)}) copy-start(f32[3,8,8192]{2,1,0:T(8,128)} %grads.5) | copy-start | bytes 2359300
  6.7 10.3 %copy-start.1 = (s32[8,8192]{1,0:T(8,128)S(1)}, s32[8,8192]{1,0:T(8,128)}, u32[]{:S(2)}) copy-start(s32[8,8192]{1,0:T(8,128)} %nm.5) | copy-start | bytes 786436
  6.7 10.3 %copy-start.3 = (f32[2,8192]{1,0:T(2,128)S(1)}, f32[2,8192]{1,0:T(2,128)}, u32[]{:S(2)}) copy-start(f32[2,8192]{1,0:T(2,128)} %moduli.3) | copy-start | bytes 196612
  6.7 10.3 %copy-start.5 = (f32[8192]{0:T(1024)S(1)}, f32[8192]{0:T(1024)}, u32[]{:S(2)}) copy-start(f32[8192]{0:T(1024)} %param.17) | copy-start | bytes 98308
  6.7 10.3 %copy-start.6 = (s32[1,4,1024]{2,1,0:T(4,128)S(1)}, s32[1,4,1024]{2,1,0:T(4,128)}, u32[]{:S(2)}) copy-start(s32[1,4,1024]{2,1,0:T(4,128)} %shared.3) | copy-start | bytes 49156
  6.8 10.3 %copy-start.8 = (f32[8,4]{1,0:T(8,128)S(1)}, f32[8,4]{1,0:T(8,128)}, u32[]{:S(2)}) copy-start(f32[8,4]{1,0:T(8,128)} %get-tuple-element.21.replace) | copy-start | bytes 388
  6.8 23.0 %all-to-all-start = ((f32[128,1,1152]{2,1,0:T(1,128)}), f32[128,1,1152]{2,1,0:T(1,128)S(1)}, u32[]{:S(2)}, u32[]{:S(2)}) async-start(f32[128,1,1152]{2,1,0:T(1,128)} %bitcast.11), calls=%async_computation | async-start | bytes 1179648 | tf_op jit(solution)/shard_map/all_to_all | solution.py:669
  31.1 24.8 %all-to-all-start.1 = ((f32[32,2,8,128]{3,2,1,0:T(8,128)}), f32[32,2,8,128]{3,2,1,0:T(8,128)S(1)}, u32[]{:S(2)}, u32[]{:S(2)}) async-start(f32[32,2,8,128]{3,2,1,0:T(8,128)} %sort_pieces.1), calls=%async_computation.1 | async-start | bytes 524288 | tf_op jit(solution)/shard_map/all_to_all | solution.py:677
  38.1 17.8 %copy-start.4 = (f32[3,9216]{1,0:T(4,128)S(1)}, f32[3,9216]{1,0:T(4,128)}, u32[]{:S(2)}) copy-start(f32[3,9216]{1,0:T(4,128)} %external.1) | copy-start | bytes 331780
  38.1 17.8 %copy-start.7 = (f32[9216]{0:T(1024)S(1)}, f32[9216]{0:T(1024)}, u32[]{:S(2)}) copy-start(f32[9216]{0:T(1024)} %param.20) | copy-start | bytes 110596
  44.1 8.2 %collective-permute-start = (f32[3,1024]{1,0:T(4,128)S(1)}, f32[3,1024]{1,0:T(4,128)S(1)}, u32[]{:S(2)}, u32[]{:S(2)}) collective-permute-start(f32[3,1024]{1,0:T(4,128)S(1)} %get-tuple-element.31), channel_id=1, source_target_pairs={{4,8},{12,16},{20,24},{28,32},{36,40},{44,48},{52,56},{60,64},{68,... | collective-permute-start | bytes 36872 | tf_op jit(solution)/shard_map/ppermute | solution.py:682
  48.4 5.6 %collective-permute-start.1 = (f32[3,1024]{1,0:T(4,128)S(1)}, f32[3,1024]{1,0:T(4,128)S(1)}, u32[]{:S(2)}, u32[]{:S(2)}) collective-permute-start(f32[3,1024]{1,0:T(4,128)S(1)} %get-tuple-element.32), channel_id=1, source_target_pairs={{1,2},{2,1},{5,6},{6,5},{9,10},{10,9},{13,14},{14,13},{17,18},{18,... | collective-permute-start | bytes 36872 | tf_op jit(solution)/shard_map/ppermute | solution.py:682
  52.1 3.8 %collective-permute-start.2 = (f32[3,1024]{1,0:T(4,128)S(1)}, f32[3,1024]{1,0:T(4,128)S(1)}, u32[]{:S(2)}, u32[]{:S(2)}) collective-permute-start(f32[3,1024]{1,0:T(4,128)S(1)} %get-tuple-element.33), channel_id=1, source_target_pairs={{0,1},{2,3},{1,0},{3,2},{4,5},{6,7},{5,4},{7,6},{8,9},{10,11},{9,8... | collective-permute-start | bytes 36872 | tf_op jit(solution)/shard_map/ppermute | solution.py:682
  52.2 3.7 %collective-permute-start.3 = (f32[3,1024]{1,0:T(4,128)S(1)}, f32[3,1024]{1,0:T(4,128)S(1)}, u32[]{:S(2)}, u32[]{:S(2)}) collective-permute-start(f32[3,1024]{1,0:T(4,128)S(1)} %get-tuple-element.34), channel_id=1, source_target_pairs={{0,4},{4,0},{1,5},{5,1},{2,6},{6,2},{3,7},{7,3},{8,12},{12,8},{9,1... | collective-permute-start | bytes 36872 | tf_op jit(solution)/shard_map/ppermute | solution.py:682

commit v10 on v7

--- a/solution.py
+++ b/solution.py
@@ -296,8 +296,11 @@
         total = jnp.zeros((8, 2 * LANES), f32)
         for x in range(G):
             total = total + slab_stress(st[k, 8 * x : 8 * x + 8, :], first_rows)
-        mean = jnp.sum(total, axis=1, keepdims=True) * (1.0 / NV)
-        result = jnp.where((lane == k) & live, jnp.broadcast_to(mean, (8, LANES)), result)
+        mean = jnp.where(live, jnp.sum(total, axis=1, keepdims=True) * (1.0 / NV), 0.0)
+        mean = jnp.broadcast_to(mean, (8, LANES))
+        result = jnp.where(lane == k, mean, result)
+        across = jnp.sum(jnp.where(lane == row, mean, 0.0), axis=0, keepdims=True)
+        band_stress[k : k + 1, :] = across[:, 0:6]
         pool = owner[0, k] & 3
 
         @pl.when(live)
@@ -310,7 +313,6 @@
             brick = (owner[0, k] >> 2).astype(f32)
             send[pl.ds(9 * pool + 8, TILES, stride=36), :] = jnp.full((TILES, LANES), brick, f32)
 
-    band_stress[...] = result[0:6, 0:4]
     for k in range(4):
         live_element = jnp.where(k < count[0], element[0, k], -1).astype(f32)
         result = jnp.where((lane == k) & (row == 6), live_element, result)
@@ -322,7 +324,7 @@
         cells_kernel,
         out_shape=(
             jax.ShapeDtypeStruct((36 * TILES, LANES), f32),
-            jax.ShapeDtypeStruct((6, 4), f32),
+            jax.ShapeDtypeStruct((4, 6), f32),
             jax.ShapeDtypeStruct((8, 4), f32),
         ),
         in_specs=[pl.BlockSpec(memory_space=SMEM)] * 3 + [pl.BlockSpec(memory_space=VMEM)] * 6,
@@ -476,7 +478,7 @@
 
 
 def face_lists(core, pool):
-    return 1 - core, core, 3 - (pool & 1), 2 + (pool & 1)
+    return core, 2 + (pool & 1), 3 - (pool & 1), 1 - core
 
 
 def macro_last_kernel(
@@ -493,10 +495,10 @@
     so_far,
     face_nodes,
     own,
+    to_brick,
+    to_odd,
+    to_even,
     to_core,
-    to_brick,
-    to_even,
-    to_odd,
     sums,
     faces,
 ):
@@ -527,7 +529,7 @@
                     4 + face : 5 + face
                 ]
     lists = face_lists(core_index[0], pool_index[0])
-    for face, out in zip(lists, (to_core, to_brick, to_even, to_odd)):
+    for face, out in zip(lists, (to_brick, to_odd, to_even, to_core)):
         out[...] = faces[face]
 
 
@@ -685,17 +687,17 @@
         return lax.ppermute(array, axis, steps + [(j, i) for i, j in steps])
 
     arrived = (
-        swap(faces[0], "core", 2, 0),
-        swap(faces[1], BRICK, bricks, 1),
+        swap(faces[0], BRICK, bricks, 1),
+        swap(faces[1], "pool", pools, 1),
         swap(faces[2], "pool", pools, 0),
-        swap(faces[3], "pool", pools, 1),
+        swap(faces[3], "core", 2, 0),
     )
     owned_fields = join_pieces(mine)
     *arrived, owned_fields = lax.optimization_barrier((*arrived, owned_fields))
     acceleration = assemble(
         place, own, shared_nodes, arrived, external_force, nodal_mass.reshape(1, -1)
     )
-    return (acceleration, band_stress, owned_fields)
+    return (acceleration, band_stress.T, owned_fields)
 
 
 def solution(mesh):

time: 59 us -> 59.1 us (level)
  the two profiles are of different devices: /device:TPU:40 before, /device:TPU:25 now
where the time goes in v10:
time: 59.1 us; the launch traced here: 58.8 us
  Pallas kernels  28.2 us (48%)
  starting transfers between devices  27.9 us (47%)
  between operations  1.47 us (2%)
  local copies, waits for them, and re-layouts  0.74 us (1%)
    pallas_call x1, Pallas kernels, macro_first(): pl.pallas_call(functools.partial(macro_first_kernel, UNROLL), out_shape=(...  12.2 us
    all_to_all x1, starting transfers between devices, shards(): lax.all_to_all(send.reshape(bricks * pools, 1, 9 * LANES), BOTH, split_ax...  10.6 us
    ppermute x4, starting transfers between devices, swap(): return lax.ppermute(array, axis, steps + [(j, i) for i, j in steps])  10.4 us
    all_to_all x1, starting transfers between devices, shards(): lax.all_to_all(sorted_pieces, BRICK, split_axis=0, concat_axis=0, tiled=T...  6.89 us
    pallas_call x1, Pallas kernels, macro_last(): pl.pallas_call(functools.partial(macro_last_kernel, UNROLL), out_shape=(j...  5.96 us
    pallas_call x1, Pallas kernels, solve_cells(): pl.pallas_call(cells_kernel, out_shape=(jax.ShapeDtypeStruct((36 * TILES,...  5.43 us
    pallas_call x1, Pallas kernels, join_pieces(): pl.pallas_call(join_kernel, out_shape=jax.ShapeDtypeStruct((2, 8, NV), f3...  1.67 us
    pallas_call x1, Pallas kernels, assemble(): pl.pallas_call(assemble_kernel, out_shape=jax.ShapeDtypeStruct(external.s...  1.53 us
  transfers between devices with their start and end apart: 6, of which 1 were waited for; matrix products, arithmetic and copies ran while one was open for 0% of the time, Pallas kernels for 34%

profile of v10, /device:TPU:25, one launch (start us, length us, event | category | flops | bytes accessed | tf_op | source)
XLA Modules:
  0.0 58.8 jit_solution(17201541026659216562)
XLA Ops:
  1.3 0.0 copy-start.2
  1.3 5.4 %cells.1 = (f32[1152,128]{1,0:T(8,128)}, f32[4,6]{1,0:T(4,128)}, f32[8,4]{1,0:T(8,128)}) custom-call(s32[1]{0:T(128)S(6)} %copy.18.count, s32[1,4]{1,0:T(1,128)} %owner.1, s32[1,4]{1,0:T(1,128)} %element.1, f32[3,9216]{1,0:T(4,128)} %disp.3, s32[8,8192]{1,0:T(8,128)} %nm.5, f32[3,8,8192]{2,1,0:T(8,128)} %grads.5, f32[4,8,4096]{2,1,0:T(8,128)} %micro.1, ...), custom_call_target="tpu_custom_call" | custom-call | tf_op jit(solution)/shard_map/cells/pallas_call | solution.py:323
  6.7 0.0 copy-start
  6.7 0.0 copy-start.1
  6.7 0.0 copy-start.3
  6.7 0.0 copy-start.5
  6.7 0.0 copy-start.6
  6.8 0.0 copy-start.8
  6.8 10.6 %all-to-all-start = ((f32[128,1,1152]{2,1,0:T(1,128)}), f32[128,1,1152]{2,1,0:T(1,128)S(1)}, u32[]{:S(2)}, u32[]{:S(2)}) async-start(f32[128,1,1152]{2,1,0:T(1,128)} %bitcast.11), calls=%async_computation | async-start | bytes 1179648 | tf_op jit(solution)/shard_map/all_to_all | solution.py:674
  17.4 0.0 copy-done.2
  17.4 0.0 copy-done
  17.4 0.0 copy-done.1
  17.4 0.0 copy-done.3
  17.4 0.0 copy-done.5
  17.4 0.0 copy-done.6
  17.4 0.0 copy-done.8
  17.4 12.2 %macro_first.1 = (f32[288,256]{1,0:T(8,128)S(1)}, s32[2,9216]{1,0:T(2,128)S(1)}, f32[1,128]{1,0:T(1,128)S(1)}, s32[4,8,128]{2,1,0:T(8,128)S(1)}) custom-call(f32[8,4]{1,0:T(8,128)S(1)} %copy-done.8, f32[3,9216]{1,0:T(4,128)S(1)} %copy-done.2, s32[8,8192]{1,0:T(8,128)S(1)} %copy-done.1, f32[3,8,8192]{2,1,0:T(8,128)S(1)} %copy-done, f32[64,128]{1,0:T(8,128)S(1)} %bitcast.8, ...), custom_call_target="tpu_custom_call" | custom-call | tf_op jit(solution)/shard_map/macro_first/pallas_call | solution.py:538
  29.6 0.5 all-to-all-done
  30.1 1.4 %sort_pieces.1 = f32[32,2,8,128]{3,2,1,0:T(8,128)} custom-call(f32[1152,128]{1,0:T(8,128)S(1)} %bitcast.7), custom_call_target="tpu_custom_call" | custom-call | tf_op jit(solution)/shard_map/sort_pieces/pallas_call | solution.py:619
  31.5 6.9 %all-to-all-start.1 = ((f32[32,2,8,128]{3,2,1,0:T(8,128)}), f32[32,2,8,128]{3,2,1,0:T(8,128)S(1)}, u32[]{:S(2)}, u32[]{:S(2)}) async-start(f32[32,2,8,128]{3,2,1,0:T(8,128)} %sort_pieces.1), calls=%async_computation.1 | async-start | bytes 524288 | tf_op jit(solution)/shard_map/all_to_all | solution.py:682
  38.4 6.0 %macro_last.1 = (f32[144,256]{1,0:T(8,128)S(1)}, f32[3,1024]{1,0:T(4,128)S(1)}, f32[3,1024]{1,0:T(4,128)S(1)}, f32[3,1024]{1,0:T(4,128)S(1)}, f32[3,1024]{1,0:T(4,128)S(1)}) custom-call(f32[8,4]{1,0:T(8,128)S(1)} %copy-done.8, s32[1]{0:T(128)} %bitcast.core_index, s32[1]{0:T(128)} %bitcast.1.pool_index, s32[2,9216]{1,0:T(2,128)S(1)} %get-tuple-element.25.table, ...), custom_call_target="tpu_custom_call" | custom-call | tf_op jit(solution)/shard_map/macro_last/pallas_call | solution.py:555
  44.4 3.3 %collective-permute-start = (f32[3,1024]{1,0:T(4,128)S(1)}, f32[3,1024]{1,0:T(4,128)S(1)}, u32[]{:S(2)}, u32[]{:S(2)}) collective-permute-start(f32[3,1024]{1,0:T(4,128)S(1)} %get-tuple-element.34), channel_id=1, source_target_pairs={{4,8},{12,16},{20,24},{28,32},{36,40},{44,48},{52,56},{60,64},{68,... | collective-permute-start | bytes 36872 | tf_op jit(solution)/shard_map/ppermute | solution.py:687
  47.7 0.7 %collective-permute-start.1 = (f32[3,1024]{1,0:T(4,128)S(1)}, f32[3,1024]{1,0:T(4,128)S(1)}, u32[]{:S(2)}, u32[]{:S(2)}) collective-permute-start(f32[3,1024]{1,0:T(4,128)S(1)} %get-tuple-element.35), channel_id=1, source_target_pairs={{1,2},{2,1},{5,6},{6,5},{9,10},{10,9},{13,14},{14,13},{17,18},{18,... | collective-permute-start | bytes 36872 | tf_op jit(solution)/shard_map/ppermute | solution.py:687
  48.4 4.2 %collective-permute-start.2 = (f32[3,1024]{1,0:T(4,128)S(1)}, f32[3,1024]{1,0:T(4,128)S(1)}, u32[]{:S(2)}, u32[]{:S(2)}) collective-permute-start(f32[3,1024]{1,0:T(4,128)S(1)} %get-tuple-element.36), channel_id=1, source_target_pairs={{0,1},{2,3},{1,0},{3,2},{4,5},{6,7},{5,4},{7,6},{8,9},{10,11},{9,8... | collective-permute-start | bytes 36872 | tf_op jit(solution)/shard_map/ppermute | solution.py:687
  52.6 0.0 copy-start.4
  52.6 0.0 copy-start.7
  52.6 2.2 %collective-permute-start.3 = (f32[3,1024]{1,0:T(4,128)S(1)}, f32[3,1024]{1,0:T(4,128)S(1)}, u32[]{:S(2)}, u32[]{:S(2)}) collective-permute-start(f32[3,1024]{1,0:T(4,128)S(1)} %get-tuple-element.37), channel_id=1, source_target_pairs={{0,4},{4,0},{1,5},{5,1},{2,6},{6,2},{3,7},{7,3},{8,12},{12,8},{9,1... | collective-permute-start | bytes 36872 | tf_op jit(solution)/shard_map/ppermute | solution.py:687
  54.8 0.0 all-to-all-done.1.pieces
  54.8 0.0 copy-start.9
  54.8 0.7 %copy-done.9 = f32[32,2,8,128]{3,2,1,0:T(8,128)} copy-done((f32[32,2,8,128]{3,2,1,0:T(8,128)}, f32[32,2,8,128]{3,2,1,0:T(8,128)S(1)}, u32[]{:S(2)}) %copy-start.9) | copy-done | bytes 262168
  55.5 1.7 %join_pieces.1 = f32[2,8,4096]{2,1,0:T(8,128)} custom-call(f32[32,2,8,128]{3,2,1,0:T(8,128)} %copy-done.9), custom_call_target="tpu_custom_call" | custom-call | tf_op jit(solution)/shard_map/join_pieces/pallas_call | solution.py:638
  57.2 0.0 collective-permute-done.r0
  57.2 0.0 collective-permute-done.1.r1
  57.2 0.0 collective-permute-done.2.r2
  57.2 0.0 collective-permute-done.3.r3
  57.2 0.0 copy-done.4
  57.2 0.0 copy-done.7
  57.2 1.5 %assemble.1 = f32[3,9216]{1,0:T(4,128)} custom-call(s32[1]{0:T(128)} %bitcast.core_index, s32[1]{0:T(128)} %bitcast.1.pool_index, f32[144,256]{1,0:T(8,128)S(1)} %get-tuple-element.33.own, s32[1,4,1024]{2,1,0:T(4,128)S(1)} %copy-done.6, f32[3,1024]{1,0:T(4,128)S(1)} %collective-permute-done.r0, f32[3,1024]{1,0:T(4,128)S(1)} %collective-permute-done.1.r1, ...), custom_call_target="tpu_custom_call" | custom-call | tf_op jit(solution)/shard_map/assemble/pallas_call | solution.py:592
Async XLA Ops:
  1.3 16.1 %copy-start.2 = (f32[3,9216]{1,0:T(4,128)S(1)}, f32[3,9216]{1,0:T(4,128)}, u32[]{:S(2)}) copy-start(f32[3,9216]{1,0:T(4,128)} %disp.3) | copy-start | bytes 331780
  6.7 10.7 %copy-start = (f32[3,8,8192]{2,1,0:T(8,128)S(1)}, f32[3,8,8192]{2,1,0:T(8,128)}, u32[]{:S(2)}) copy-start(f32[3,8,8192]{2,1,0:T(8,128)} %grads.5) | copy-start | bytes 2359300
  6.7 10.7 %copy-start.1 = (s32[8,8192]{1,0:T(8,128)S(1)}, s32[8,8192]{1,0:T(8,128)}, u32[]{:S(2)}) copy-start(s32[8,8192]{1,0:T(8,128)} %nm.5) | copy-start | bytes 786436
  6.7 10.7 %copy-start.3 = (f32[2,8192]{1,0:T(2,128)S(1)}, f32[2,8192]{1,0:T(2,128)}, u32[]{:S(2)}) copy-start(f32[2,8192]{1,0:T(2,128)} %moduli.3) | copy-start | bytes 196612
  6.7 10.7 %copy-start.5 = (f32[8192]{0:T(1024)S(1)}, f32[8192]{0:T(1024)}, u32[]{:S(2)}) copy-start(f32[8192]{0:T(1024)} %param.17) | copy-start | bytes 98308
  6.7 10.7 %copy-start.6 = (s32[1,4,1024]{2,1,0:T(4,128)S(1)}, s32[1,4,1024]{2,1,0:T(4,128)}, u32[]{:S(2)}) copy-start(s32[1,4,1024]{2,1,0:T(4,128)} %shared.3) | copy-start | bytes 49156
  6.8 10.7 %copy-start.8 = (f32[8,4]{1,0:T(8,128)S(1)}, f32[8,4]{1,0:T(8,128)}, u32[]{:S(2)}) copy-start(f32[8,4]{1,0:T(8,128)} %get-tuple-element.24.replace) | copy-start | bytes 388
  6.8 23.3 %all-to-all-start = ((f32[128,1,1152]{2,1,0:T(1,128)}), f32[128,1,1152]{2,1,0:T(1,128)S(1)}, u32[]{:S(2)}, u32[]{:S(2)}) async-start(f32[128,1,1152]{2,1,0:T(1,128)} %bitcast.11), calls=%async_computation | async-start | bytes 1179648 | tf_op jit(solution)/shard_map/all_to_all | solution.py:674
  31.5 23.3 %all-to-all-start.1 = ((f32[32,2,8,128]{3,2,1,0:T(8,128)}), f32[32,2,8,128]{3,2,1,0:T(8,128)S(1)}, u32[]{:S(2)}, u32[]{:S(2)}) async-start(f32[32,2,8,128]{3,2,1,0:T(8,128)} %sort_pieces.1), calls=%async_computation.1 | async-start | bytes 524288 | tf_op jit(solution)/shard_map/all_to_all | solution.py:682
  44.4 12.8 %collective-permute-start = (f32[3,1024]{1,0:T(4,128)S(1)}, f32[3,1024]{1,0:T(4,128)S(1)}, u32[]{:S(2)}, u32[]{:S(2)}) collective-permute-start(f32[3,1024]{1,0:T(4,128)S(1)} %get-tuple-element.34), channel_id=1, source_target_pairs={{4,8},{12,16},{20,24},{28,32},{36,40},{44,48},{52,56},{60,64},{68,... | collective-permute-start | bytes 36872 | tf_op jit(solution)/shard_map/ppermute | solution.py:687
  47.7 9.4 %collective-permute-start.1 = (f32[3,1024]{1,0:T(4,128)S(1)}, f32[3,1024]{1,0:T(4,128)S(1)}, u32[]{:S(2)}, u32[]{:S(2)}) collective-permute-start(f32[3,1024]{1,0:T(4,128)S(1)} %get-tuple-element.35), channel_id=1, source_target_pairs={{1,2},{2,1},{5,6},{6,5},{9,10},{10,9},{13,14},{14,13},{17,18},{18,... | collective-permute-start | bytes 36872 | tf_op jit(solution)/shard_map/ppermute | solution.py:687
  48.4 8.8 %collective-permute-start.2 = (f32[3,1024]{1,0:T(4,128)S(1)}, f32[3,1024]{1,0:T(4,128)S(1)}, u32[]{:S(2)}, u32[]{:S(2)}) collective-permute-start(f32[3,1024]{1,0:T(4,128)S(1)} %get-tuple-element.36), channel_id=1, source_target_pairs={{0,1},{2,3},{1,0},{3,2},{4,5},{6,7},{5,4},{7,6},{8,9},{10,11},{9,8... | collective-permute-start | bytes 36872 | tf_op jit(solution)/shard_map/ppermute | solution.py:687
  52.6 4.6 %copy-start.4 = (f32[3,9216]{1,0:T(4,128)S(1)}, f32[3,9216]{1,0:T(4,128)}, u32[]{:S(2)}) copy-start(f32[3,9216]{1,0:T(4,128)} %external.1) | copy-start | bytes 331780
  52.6 4.6 %copy-start.7 = (f32[9216]{0:T(1024)S(1)}, f32[9216]{0:T(1024)}, u32[]{:S(2)}) copy-start(f32[9216]{0:T(1024)} %param.20) | copy-start | bytes 110596
  52.6 4.6 %collective-permute-start.3 = (f32[3,1024]{1,0:T(4,128)S(1)}, f32[3,1024]{1,0:T(4,128)S(1)}, u32[]{:S(2)}, u32[]{:S(2)}) collective-permute-start(f32[3,1024]{1,0:T(4,128)S(1)} %get-tuple-element.37), channel_id=1, source_target_pairs={{0,4},{4,0},{1,5},{5,1},{2,6},{6,2},{3,7},{7,3},{8,12},{12,8},{9,1... | collective-permute-start | bytes 36872 | tf_op jit(solution)/shard_map/ppermute | solution.py:687
  54.8 0.7 %copy-start.9 = (f32[32,2,8,128]{3,2,1,0:T(8,128)}, f32[32,2,8,128]{3,2,1,0:T(8,128)S(1)}, u32[]{:S(2)}) copy-start(f32[32,2,8,128]{3,2,1,0:T(8,128)S(1)} %all-to-all-done.1.pieces) | copy-start | bytes 786436

commit v11 on v9

--- a/solution.py
+++ b/solution.py
@@ -19,7 +19,7 @@
 STEPS = float((1 << 20) - 2)
 OFFSET = 1 << 20
 UNROLL = 4
-SPLIT = 48
+SPLIT = 56
 BRICK = ("row", "pair", "core")
 BOTH = BRICK + ("pool",)
 VMEM = pltpu.VMEM

time: 58.5 us -> 58.2 us (level)
    pallas_call x1, Pallas kernels: 5.96 us -> 3.87 us  [macro_last(): pl.pallas_call(functools.partial(macro_last_kernel, UNROLL), out_shape=(j...]
    pallas_call x1, Pallas kernels: 12.2 us -> 14 us  [macro_first(): pl.pallas_call(functools.partial(macro_first_kernel, UNROLL), out_shape=(...]
  transfers between devices with their start and end apart: 6 -> 6, of which waited for: 3 -> 2; matrix products, arithmetic and copies ran while one was open for 0% -> 0% of each run, Pallas kernels for 31% -> 31%
where the time goes in v11:
time: 58.2 us; the launch traced here: 57.8 us
  Pallas kernels  26.9 us (46%)
  starting transfers between devices  25.8 us (44%)
  waiting for transfers between devices  3.63 us (6%)
  between operations  1.49 us (3%)
    pallas_call x1, Pallas kernels, macro_first(): pl.pallas_call(functools.partial(macro_first_kernel, UNROLL), out_shape=(...  14 us
    all_to_all x1, starting transfers between devices, shards(): lax.all_to_all(send.reshape(bricks * pools, 1, 9 * LANES), BOTH, split_ax...  10.2 us
    ppermute x4, starting transfers between devices, swap(): return lax.ppermute(array, axis, steps + [(j, i) for i, j in steps])  8.18 us
    all_to_all x1, starting transfers between devices, shards(): lax.all_to_all(sorted_pieces, BRICK, split_axis=0, concat_axis=0, tiled=T...  7.44 us
    pallas_call x1, Pallas kernels, solve_cells(): pl.pallas_call(cells_kernel, out_shape=(jax.ShapeDtypeStruct((36 * TILES,...  5.43 us
    pallas_call x1, Pallas kernels, macro_last(): pl.pallas_call(functools.partial(macro_last_kernel, UNROLL), out_shape=(j...  3.87 us
    ppermute x4, waiting for transfers between devices, swap(): return lax.ppermute(array, axis, steps + [(j, i) for i, j in steps])  3.63 us
    pallas_call x1, Pallas kernels, assemble(): pl.pallas_call(assemble_kernel, out_shape=(jax.ShapeDtypeStruct(external....  2.18 us
  transfers between devices with their start and end apart: 6, of which 2 were waited for; matrix products, arithmetic and copies ran while one was open for 0% of the time, Pallas kernels for 31%

profile of v11, /device:TPU:40, one launch (start us, length us, event | category | flops | bytes accessed | tf_op | source)
XLA Modules:
  0.0 57.8 jit_solution(15656516816312213169)
XLA Ops:
  1.3 0.0 copy-start.2
  1.3 5.4 %cells.1 = (f32[1152,128]{1,0:T(8,128)}, f32[4,6]{1,0:T(4,128)}, f32[8,4]{1,0:T(8,128)}) custom-call(s32[1]{0:T(128)S(6)} %copy.18.count, s32[1,4]{1,0:T(1,128)} %owner.1, s32[1,4]{1,0:T(1,128)} %element.1, f32[3,9216]{1,0:T(4,128)} %disp.3, s32[8,8192]{1,0:T(8,128)} %nm.5, f32[3,8,8192]{2,1,0:T(8,128)} %grads.5, f32[4,8,4096]{2,1,0:T(8,128)} %micro.1, ...), custom_call_target="tpu_custom_call" | custom-call | tf_op jit(solution)/shard_map/cells/pallas_call | solution.py:323
  6.7 0.0 copy-start
  6.7 0.0 copy-start.1
  6.7 0.0 copy-start.3
  6.7 0.0 copy-start.5
  6.8 0.0 copy-start.6
  6.8 0.0 copy-start.8
  6.8 10.2 %all-to-all-start = ((f32[128,1,1152]{2,1,0:T(1,128)}), f32[128,1,1152]{2,1,0:T(1,128)S(1)}, u32[]{:S(2)}, u32[]{:S(2)}) async-start(f32[128,1,1152]{2,1,0:T(1,128)} %bitcast.11), calls=%async_computation | async-start | bytes 1179648 | tf_op jit(solution)/shard_map/all_to_all | solution.py:669
  17.0 0.0 copy-done.2
  17.0 0.0 copy-done
  17.0 0.0 copy-done.1
  17.0 0.0 copy-done.3
  17.0 0.0 copy-done.5
  17.0 0.0 copy-done.6
  17.0 0.0 copy-done.8
  17.0 14.0 %macro_first.1 = (f32[288,256]{1,0:T(8,128)S(1)}, s32[2,9216]{1,0:T(2,128)S(1)}, f32[1,128]{1,0:T(1,128)S(1)}, s32[4,8,128]{2,1,0:T(8,128)S(1)}) custom-call(f32[8,4]{1,0:T(8,128)S(1)} %copy-done.8, f32[3,9216]{1,0:T(4,128)S(1)} %copy-done.2, s32[8,8192]{1,0:T(8,128)S(1)} %copy-done.1, f32[3,8,8192]{2,1,0:T(8,128)S(1)} %copy-done, f32[64,128]{1,0:T(8,128)S(1)} %bitcast.8, ...), custom_call_target="tpu_custom_call" | custom-call | tf_op jit(solution)/shard_map/macro_first/pallas_call | solution.py:538
  31.0 0.0 all-to-all-done
  31.1 1.4 %sort_pieces.1 = f32[32,2,8,128]{3,2,1,0:T(8,128)} custom-call(f32[1152,128]{1,0:T(8,128)S(1)} %bitcast.7), custom_call_target="tpu_custom_call" | custom-call | tf_op jit(solution)/shard_map/sort_pieces/pallas_call | solution.py:631
  32.5 7.4 %all-to-all-start.1 = ((f32[32,2,8,128]{3,2,1,0:T(8,128)}), f32[32,2,8,128]{3,2,1,0:T(8,128)S(1)}, u32[]{:S(2)}, u32[]{:S(2)}) async-start(f32[32,2,8,128]{3,2,1,0:T(8,128)} %sort_pieces.1), calls=%async_computation.1 | async-start | bytes 524288 | tf_op jit(solution)/shard_map/all_to_all | solution.py:677
  39.9 0.0 copy-start.4
  39.9 0.0 copy-start.7
  39.9 3.9 %macro_last.1 = (f32[144,256]{1,0:T(8,128)S(1)}, f32[3,1024]{1,0:T(4,128)S(1)}, f32[3,1024]{1,0:T(4,128)S(1)}, f32[3,1024]{1,0:T(4,128)S(1)}, f32[3,1024]{1,0:T(4,128)S(1)}) custom-call(f32[8,4]{1,0:T(8,128)S(1)} %copy-done.8, s32[1]{0:T(128)} %bitcast.core_index, s32[1]{0:T(128)} %bitcast.1.pool_index, s32[2,9216]{1,0:T(2,128)S(1)} %get-tuple-element.22.table, ...), custom_call_target="tpu_custom_call" | custom-call | tf_op jit(solution)/shard_map/macro_last/pallas_call | solution.py:555
  43.8 4.3 %collective-permute-start = (f32[3,1024]{1,0:T(4,128)S(1)}, f32[3,1024]{1,0:T(4,128)S(1)}, u32[]{:S(2)}, u32[]{:S(2)}) collective-permute-start(f32[3,1024]{1,0:T(4,128)S(1)} %get-tuple-element.31), channel_id=1, source_target_pairs={{4,8},{12,16},{20,24},{28,32},{36,40},{44,48},{52,56},{60,64},{68,... | collective-permute-start | bytes 36872 | tf_op jit(solution)/shard_map/ppermute | solution.py:682
  48.1 3.7 %collective-permute-start.1 = (f32[3,1024]{1,0:T(4,128)S(1)}, f32[3,1024]{1,0:T(4,128)S(1)}, u32[]{:S(2)}, u32[]{:S(2)}) collective-permute-start(f32[3,1024]{1,0:T(4,128)S(1)} %get-tuple-element.32), channel_id=1, source_target_pairs={{1,2},{2,1},{5,6},{6,5},{9,10},{10,9},{13,14},{14,13},{17,18},{18,... | collective-permute-start | bytes 36872 | tf_op jit(solution)/shard_map/ppermute | solution.py:682
  51.8 0.1 collective-permute-start.2
  51.9 0.1 collective-permute-start.3
  52.0 0.0 collective-permute-done.r0
  52.0 1.8 %collective-permute-done.1.r1 = f32[3,1024]{1,0:T(4,128)S(1)} collective-permute-done((f32[3,1024]{1,0:T(4,128)S(1)}, f32[3,1024]{1,0:T(4,128)S(1)}, u32[]{:S(2)}, u32[]{:S(2)}) %collective-permute-start.1) | collective-permute-done | bytes 12320 | tf_op jit(solution)/shard_map/ppermute | solution.py:682
  53.8 1.9 %collective-permute-done.2.r2 = f32[3,1024]{1,0:T(4,128)S(1)} collective-permute-done((f32[3,1024]{1,0:T(4,128)S(1)}, f32[3,1024]{1,0:T(4,128)S(1)}, u32[]{:S(2)}, u32[]{:S(2)}) %collective-permute-start.2) | collective-permute-done | bytes 12320 | tf_op jit(solution)/shard_map/ppermute | solution.py:682
  55.6 0.0 collective-permute-done.3.r3
  55.6 0.0 all-to-all-done.1.pieces
  55.6 0.0 copy-done.4
  55.7 0.0 copy-done.7
  55.7 2.2 %assemble.1 = (f32[3,9216]{1,0:T(4,128)}, f32[2,8,4096]{2,1,0:T(8,128)}) custom-call(s32[1]{0:T(128)} %bitcast.core_index, s32[1]{0:T(128)} %bitcast.1.pool_index, f32[144,256]{1,0:T(8,128)S(1)} %get-tuple-element.30.own, s32[1,4,1024]{2,1,0:T(4,128)S(1)} %copy-done.6, f32[3,1024]{1,0:T(4,128)S(1)} %collective-permute-done.r0, ...), custom_call_target="tpu_custom_call" | custom-call | tf_op jit(solution)/shard_map/assemble/pallas_call | solution.py:600
Async XLA Ops:
  1.3 15.7 %copy-start.2 = (f32[3,9216]{1,0:T(4,128)S(1)}, f32[3,9216]{1,0:T(4,128)}, u32[]{:S(2)}) copy-start(f32[3,9216]{1,0:T(4,128)} %disp.3) | copy-start | bytes 331780
  6.7 10.3 %copy-start = (f32[3,8,8192]{2,1,0:T(8,128)S(1)}, f32[3,8,8192]{2,1,0:T(8,128)}, u32[]{:S(2)}) copy-start(f32[3,8,8192]{2,1,0:T(8,128)} %grads.5) | copy-start | bytes 2359300
  6.7 10.3 %copy-start.1 = (s32[8,8192]{1,0:T(8,128)S(1)}, s32[8,8192]{1,0:T(8,128)}, u32[]{:S(2)}) copy-start(s32[8,8192]{1,0:T(8,128)} %nm.5) | copy-start | bytes 786436
  6.7 10.3 %copy-start.3 = (f32[2,8192]{1,0:T(2,128)S(1)}, f32[2,8192]{1,0:T(2,128)}, u32[]{:S(2)}) copy-start(f32[2,8192]{1,0:T(2,128)} %moduli.3) | copy-start | bytes 196612
  6.7 10.3 %copy-start.5 = (f32[8192]{0:T(1024)S(1)}, f32[8192]{0:T(1024)}, u32[]{:S(2)}) copy-start(f32[8192]{0:T(1024)} %param.17) | copy-start | bytes 98308
  6.8 10.3 %copy-start.6 = (s32[1,4,1024]{2,1,0:T(4,128)S(1)}, s32[1,4,1024]{2,1,0:T(4,128)}, u32[]{:S(2)}) copy-start(s32[1,4,1024]{2,1,0:T(4,128)} %shared.3) | copy-start | bytes 49156
  6.8 10.3 %copy-start.8 = (f32[8,4]{1,0:T(8,128)S(1)}, f32[8,4]{1,0:T(8,128)}, u32[]{:S(2)}) copy-start(f32[8,4]{1,0:T(8,128)} %get-tuple-element.21.replace) | copy-start | bytes 388
  6.8 24.3 %all-to-all-start = ((f32[128,1,1152]{2,1,0:T(1,128)}), f32[128,1,1152]{2,1,0:T(1,128)S(1)}, u32[]{:S(2)}, u32[]{:S(2)}) async-start(f32[128,1,1152]{2,1,0:T(1,128)} %bitcast.11), calls=%async_computation | async-start | bytes 1179648 | tf_op jit(solution)/shard_map/all_to_all | solution.py:669
  32.5 23.2 %all-to-all-start.1 = ((f32[32,2,8,128]{3,2,1,0:T(8,128)}), f32[32,2,8,128]{3,2,1,0:T(8,128)S(1)}, u32[]{:S(2)}, u32[]{:S(2)}) async-start(f32[32,2,8,128]{3,2,1,0:T(8,128)} %sort_pieces.1), calls=%async_computation.1 | async-start | bytes 524288 | tf_op jit(solution)/shard_map/all_to_all | solution.py:677
  39.9 15.7 %copy-start.4 = (f32[3,9216]{1,0:T(4,128)S(1)}, f32[3,9216]{1,0:T(4,128)}, u32[]{:S(2)}) copy-start(f32[3,9216]{1,0:T(4,128)} %external.1) | copy-start | bytes 331780
  39.9 15.7 %copy-start.7 = (f32[9216]{0:T(1024)S(1)}, f32[9216]{0:T(1024)}, u32[]{:S(2)}) copy-start(f32[9216]{0:T(1024)} %param.20) | copy-start | bytes 110596
  43.8 8.2 %collective-permute-start = (f32[3,1024]{1,0:T(4,128)S(1)}, f32[3,1024]{1,0:T(4,128)S(1)}, u32[]{:S(2)}, u32[]{:S(2)}) collective-permute-start(f32[3,1024]{1,0:T(4,128)S(1)} %get-tuple-element.31), channel_id=1, source_target_pairs={{4,8},{12,16},{20,24},{28,32},{36,40},{44,48},{52,56},{60,64},{68,... | collective-permute-start | bytes 36872 | tf_op jit(solution)/shard_map/ppermute | solution.py:682
  48.1 5.6 %collective-permute-start.1 = (f32[3,1024]{1,0:T(4,128)S(1)}, f32[3,1024]{1,0:T(4,128)S(1)}, u32[]{:S(2)}, u32[]{:S(2)}) collective-permute-start(f32[3,1024]{1,0:T(4,128)S(1)} %get-tuple-element.32), channel_id=1, source_target_pairs={{1,2},{2,1},{5,6},{6,5},{9,10},{10,9},{13,14},{14,13},{17,18},{18,... | collective-permute-start | bytes 36872 | tf_op jit(solution)/shard_map/ppermute | solution.py:682
  51.8 3.8 %collective-permute-start.2 = (f32[3,1024]{1,0:T(4,128)S(1)}, f32[3,1024]{1,0:T(4,128)S(1)}, u32[]{:S(2)}, u32[]{:S(2)}) collective-permute-start(f32[3,1024]{1,0:T(4,128)S(1)} %get-tuple-element.33), channel_id=1, source_target_pairs={{0,1},{2,3},{1,0},{3,2},{4,5},{6,7},{5,4},{7,6},{8,9},{10,11},{9,8... | collective-permute-start | bytes 36872 | tf_op jit(solution)/shard_map/ppermute | solution.py:682
  51.9 3.7 %collective-permute-start.3 = (f32[3,1024]{1,0:T(4,128)S(1)}, f32[3,1024]{1,0:T(4,128)S(1)}, u32[]{:S(2)}, u32[]{:S(2)}) collective-permute-start(f32[3,1024]{1,0:T(4,128)S(1)} %get-tuple-element.34), channel_id=1, source_target_pairs={{0,4},{4,0},{1,5},{5,1},{2,6},{6,2},{3,7},{7,3},{8,12},{12,8},{9,1... | collective-permute-start | bytes 36872 | tf_op jit(solution)/shard_map/ppermute | solution.py:682

commit v12 on v11

--- a/solution.py
+++ b/solution.py
@@ -478,7 +478,7 @@
 
 
 def face_lists(core, pool):
-    return core, 2 + (pool & 1), 3 - (pool & 1), 1 - core
+    return 3 - (pool & 1), 2 + (pool & 1), core, 1 - core
 
 
 def macro_last_kernel(
@@ -495,9 +495,9 @@
     so_far,
     face_nodes,
     own,
+    to_even,
+    to_odd,
     to_brick,
-    to_odd,
-    to_even,
     to_core,
     sums,
     faces,
@@ -529,7 +529,7 @@
                     4 + face : 5 + face
                 ]
     lists = face_lists(core_index[0], pool_index[0])
-    for face, out in zip(lists, (to_brick, to_odd, to_even, to_core)):
+    for face, out in zip(lists, (to_even, to_odd, to_brick, to_core)):
         out[...] = faces[face]
 
 
@@ -682,9 +682,9 @@
         return lax.ppermute(array, axis, steps + [(j, i) for i, j in steps])
 
     arrived = (
-        swap(faces[0], BRICK, bricks, 1),
+        swap(faces[0], "pool", pools, 0),
         swap(faces[1], "pool", pools, 1),
-        swap(faces[2], "pool", pools, 0),
+        swap(faces[2], BRICK, bricks, 1),
         swap(faces[3], "core", 2, 0),
     )
     acceleration, owned_fields = assemble(

time: 58.2 us -> 58.6 us (level)
  starting transfers between devices: 25.8 us -> 26.7 us
    ppermute x4, starting transfers between devices: 8.18 us -> 8.97 us  [swap(): return lax.ppermute(array, axis, steps + [(j, i) for i, j in steps])]
  transfers between devices with their start and end apart: 6 -> 6, of which waited for: 2 -> 1; matrix products, arithmetic and copies ran while one was open for 0% -> 0% of each run, Pallas kernels for 31% -> 31%
where the time goes in v12:
time: 58.6 us; the launch traced here: 58.3 us
  Pallas kernels  26.8 us (46%)
  starting transfers between devices  26.7 us (46%)
  waiting for transfers between devices  3.29 us (6%)
  between operations  1.49 us (3%)
    pallas_call x1, Pallas kernels, macro_first(): pl.pallas_call(functools.partial(macro_first_kernel, UNROLL), out_shape=(...  14 us
    all_to_all x1, starting transfers between devices, shards(): lax.all_to_all(send.reshape(bricks * pools, 1, 9 * LANES), BOTH, split_ax...  10.2 us
    ppermute x4, starting transfers between devices, swap(): return lax.ppermute(array, axis, steps + [(j, i) for i, j in steps])  8.97 us
    all_to_all x1, starting transfers between devices, shards(): lax.all_to_all(sorted_pieces, BRICK, split_axis=0, concat_axis=0, tiled=T...  7.51 us
    pallas_call x1, Pallas kernels, solve_cells(): pl.pallas_call(cells_kernel, out_shape=(jax.ShapeDtypeStruct((36 * TILES,...  5.43 us
    pallas_call x1, Pallas kernels, macro_last(): pl.pallas_call(functools.partial(macro_last_kernel, UNROLL), out_shape=(j...  3.87 us
    ppermute x4, waiting for transfers between devices, swap(): return lax.ppermute(array, axis, steps + [(j, i) for i, j in steps])  3.28 us
    pallas_call x1, Pallas kernels, assemble(): pl.pallas_call(assemble_kernel, out_shape=(jax.ShapeDtypeStruct(external....  2.18 us
  transfers between devices with their start and end apart: 6, of which 1 were waited for; matrix products, arithmetic and copies ran while one was open for 0% of the time, Pallas kernels for 31%

profile of v12, /device:TPU:40, one launch (start us, length us, event | category | flops | bytes accessed | tf_op | source)
XLA Modules:
  0.0 58.3 jit_solution(6930822553240896886)
XLA Ops:
  1.3 0.0 copy-start.2
  1.3 5.4 %cells.1 = (f32[1152,128]{1,0:T(8,128)}, f32[4,6]{1,0:T(4,128)}, f32[8,4]{1,0:T(8,128)}) custom-call(s32[1]{0:T(128)S(6)} %copy.18.count, s32[1,4]{1,0:T(1,128)} %owner.1, s32[1,4]{1,0:T(1,128)} %element.1, f32[3,9216]{1,0:T(4,128)} %disp.3, s32[8,8192]{1,0:T(8,128)} %nm.5, f32[3,8,8192]{2,1,0:T(8,128)} %grads.5, f32[4,8,4096]{2,1,0:T(8,128)} %micro.1, ...), custom_call_target="tpu_custom_call" | custom-call | tf_op jit(solution)/shard_map/cells/pallas_call | solution.py:323
  6.7 0.0 copy-start
  6.7 0.0 copy-start.1
  6.7 0.0 copy-start.3
  6.7 0.0 copy-start.5
  6.7 0.0 copy-start.6
  6.8 0.0 copy-start.8
  6.8 10.2 %all-to-all-start = ((f32[128,1,1152]{2,1,0:T(1,128)}), f32[128,1,1152]{2,1,0:T(1,128)S(1)}, u32[]{:S(2)}, u32[]{:S(2)}) async-start(f32[128,1,1152]{2,1,0:T(1,128)} %bitcast.11), calls=%async_computation | async-start | bytes 1179648 | tf_op jit(solution)/shard_map/all_to_all | solution.py:669
  17.0 0.0 copy-done.2
  17.0 0.0 copy-done
  17.0 0.0 copy-done.1
  17.0 0.0 copy-done.3
  17.0 0.0 copy-done.5
  17.0 0.0 copy-done.6
  17.0 0.0 copy-done.8
  17.0 14.0 %macro_first.1 = (f32[288,256]{1,0:T(8,128)S(1)}, s32[2,9216]{1,0:T(2,128)S(1)}, f32[1,128]{1,0:T(1,128)S(1)}, s32[4,8,128]{2,1,0:T(8,128)S(1)}) custom-call(f32[8,4]{1,0:T(8,128)S(1)} %copy-done.8, f32[3,9216]{1,0:T(4,128)S(1)} %copy-done.2, s32[8,8192]{1,0:T(8,128)S(1)} %copy-done.1, f32[3,8,8192]{2,1,0:T(8,128)S(1)} %copy-done, f32[64,128]{1,0:T(8,128)S(1)} %bitcast.8, ...), custom_call_target="tpu_custom_call" | custom-call | tf_op jit(solution)/shard_map/macro_first/pallas_call | solution.py:538
  31.0 0.0 all-to-all-done
  31.0 1.4 %sort_pieces.1 = f32[32,2,8,128]{3,2,1,0:T(8,128)} custom-call(f32[1152,128]{1,0:T(8,128)S(1)} %bitcast.7), custom_call_target="tpu_custom_call" | custom-call | tf_op jit(solution)/shard_map/sort_pieces/pallas_call | solution.py:631
  32.4 7.5 %all-to-all-start.1 = ((f32[32,2,8,128]{3,2,1,0:T(8,128)}), f32[32,2,8,128]{3,2,1,0:T(8,128)S(1)}, u32[]{:S(2)}, u32[]{:S(2)}) async-start(f32[32,2,8,128]{3,2,1,0:T(8,128)} %sort_pieces.1), calls=%async_computation.1 | async-start | bytes 524288 | tf_op jit(solution)/shard_map/all_to_all | solution.py:677
  39.9 0.0 copy-start.4
  40.0 0.0 copy-start.7
  40.0 3.9 %macro_last.1 = (f32[144,256]{1,0:T(8,128)S(1)}, f32[3,1024]{1,0:T(4,128)S(1)}, f32[3,1024]{1,0:T(4,128)S(1)}, f32[3,1024]{1,0:T(4,128)S(1)}, f32[3,1024]{1,0:T(4,128)S(1)}) custom-call(f32[8,4]{1,0:T(8,128)S(1)} %copy-done.8, s32[1]{0:T(128)} %bitcast.core_index, s32[1]{0:T(128)} %bitcast.1.pool_index, s32[2,9216]{1,0:T(2,128)S(1)} %get-tuple-element.22.table, ...), custom_call_target="tpu_custom_call" | custom-call | tf_op jit(solution)/shard_map/macro_last/pallas_call | solution.py:555
  43.8 0.4 collective-permute-start
  44.2 4.7 %collective-permute-start.1 = (f32[3,1024]{1,0:T(4,128)S(1)}, f32[3,1024]{1,0:T(4,128)S(1)}, u32[]{:S(2)}, u32[]{:S(2)}) collective-permute-start(f32[3,1024]{1,0:T(4,128)S(1)} %get-tuple-element.32), channel_id=1, source_target_pairs={{1,2},{2,1},{5,6},{6,5},{9,10},{10,9},{13,14},{14,13},{17,18},{18,... | collective-permute-start | bytes 36872 | tf_op jit(solution)/shard_map/ppermute | solution.py:682
  49.0 3.8 %collective-permute-start.2 = (f32[3,1024]{1,0:T(4,128)S(1)}, f32[3,1024]{1,0:T(4,128)S(1)}, u32[]{:S(2)}, u32[]{:S(2)}) collective-permute-start(f32[3,1024]{1,0:T(4,128)S(1)} %get-tuple-element.33), channel_id=1, source_target_pairs={{4,8},{12,16},{20,24},{28,32},{36,40},{44,48},{52,56},{60,64},{68,... | collective-permute-start | bytes 36872 | tf_op jit(solution)/shard_map/ppermute | solution.py:682
  52.7 0.1 collective-permute-start.3
  52.8 0.0 collective-permute-done.r0
  52.8 0.0 collective-permute-done.1.r1
  52.8 3.3 %collective-permute-done.2.r2 = f32[3,1024]{1,0:T(4,128)S(1)} collective-permute-done((f32[3,1024]{1,0:T(4,128)S(1)}, f32[3,1024]{1,0:T(4,128)S(1)}, u32[]{:S(2)}, u32[]{:S(2)}) %collective-permute-start.2) | collective-permute-done | bytes 12320 | tf_op jit(solution)/shard_map/ppermute | solution.py:682
  56.1 0.0 collective-permute-done.3.r3
  56.1 0.0 all-to-all-done.1.pieces
  56.1 0.0 copy-done.4
  56.1 0.0 copy-done.7
  56.1 2.2 %assemble.1 = (f32[3,9216]{1,0:T(4,128)}, f32[2,8,4096]{2,1,0:T(8,128)}) custom-call(s32[1]{0:T(128)} %bitcast.core_index, s32[1]{0:T(128)} %bitcast.1.pool_index, f32[144,256]{1,0:T(8,128)S(1)} %get-tuple-element.30.own, s32[1,4,1024]{2,1,0:T(4,128)S(1)} %copy-done.6, f32[3,1024]{1,0:T(4,128)S(1)} %collective-permute-done.r0, ...), custom_call_target="tpu_custom_call" | custom-call | tf_op jit(solution)/shard_map/assemble/pallas_call | solution.py:600
Async XLA Ops:
  1.3 15.7 %copy-start.2 = (f32[3,9216]{1,0:T(4,128)S(1)}, f32[3,9216]{1,0:T(4,128)}, u32[]{:S(2)}) copy-start(f32[3,9216]{1,0:T(4,128)} %disp.3) | copy-start | bytes 331780
  6.7 10.3 %copy-start = (f32[3,8,8192]{2,1,0:T(8,128)S(1)}, f32[3,8,8192]{2,1,0:T(8,128)}, u32[]{:S(2)}) copy-start(f32[3,8,8192]{2,1,0:T(8,128)} %grads.5) | copy-start | bytes 2359300
  6.7 10.3 %copy-start.1 = (s32[8,8192]{1,0:T(8,128)S(1)}, s32[8,8192]{1,0:T(8,128)}, u32[]{:S(2)}) copy-start(s32[8,8192]{1,0:T(8,128)} %nm.5) | copy-start | bytes 786436
  6.7 10.3 %copy-start.3 = (f32[2,8192]{1,0:T(2,128)S(1)}, f32[2,8192]{1,0:T(2,128)}, u32[]{:S(2)}) copy-start(f32[2,8192]{1,0:T(2,128)} %moduli.3) | copy-start | bytes 196612
  6.7 10.3 %copy-start.5 = (f32[8192]{0:T(1024)S(1)}, f32[8192]{0:T(1024)}, u32[]{:S(2)}) copy-start(f32[8192]{0:T(1024)} %param.17) | copy-start | bytes 98308
  6.7 10.3 %copy-start.6 = (s32[1,4,1024]{2,1,0:T(4,128)S(1)}, s32[1,4,1024]{2,1,0:T(4,128)}, u32[]{:S(2)}) copy-start(s32[1,4,1024]{2,1,0:T(4,128)} %shared.3) | copy-start | bytes 49156
  6.8 10.3 %copy-start.8 = (f32[8,4]{1,0:T(8,128)S(1)}, f32[8,4]{1,0:T(8,128)}, u32[]{:S(2)}) copy-start(f32[8,4]{1,0:T(8,128)} %get-tuple-element.21.replace) | copy-start | bytes 388
  6.8 24.2 %all-to-all-start = ((f32[128,1,1152]{2,1,0:T(1,128)}), f32[128,1,1152]{2,1,0:T(1,128)S(1)}, u32[]{:S(2)}, u32[]{:S(2)}) async-start(f32[128,1,1152]{2,1,0:T(1,128)} %bitcast.11), calls=%async_computation | async-start | bytes 1179648 | tf_op jit(solution)/shard_map/all_to_all | solution.py:669
  32.4 23.7 %all-to-all-start.1 = ((f32[32,2,8,128]{3,2,1,0:T(8,128)}), f32[32,2,8,128]{3,2,1,0:T(8,128)S(1)}, u32[]{:S(2)}, u32[]{:S(2)}) async-start(f32[32,2,8,128]{3,2,1,0:T(8,128)} %sort_pieces.1), calls=%async_computation.1 | async-start | bytes 524288 | tf_op jit(solution)/shard_map/all_to_all | solution.py:677
  39.9 16.2 %copy-start.4 = (f32[3,9216]{1,0:T(4,128)S(1)}, f32[3,9216]{1,0:T(4,128)}, u32[]{:S(2)}) copy-start(f32[3,9216]{1,0:T(4,128)} %external.1) | copy-start | bytes 331780
  40.0 16.2 %copy-start.7 = (f32[9216]{0:T(1024)S(1)}, f32[9216]{0:T(1024)}, u32[]{:S(2)}) copy-start(f32[9216]{0:T(1024)} %param.20) | copy-start | bytes 110596
  43.8 9.0 %collective-permute-start = (f32[3,1024]{1,0:T(4,128)S(1)}, f32[3,1024]{1,0:T(4,128)S(1)}, u32[]{:S(2)}, u32[]{:S(2)}) collective-permute-start(f32[3,1024]{1,0:T(4,128)S(1)} %get-tuple-element.31), channel_id=1, source_target_pairs={{0,1},{2,3},{1,0},{3,2},{4,5},{6,7},{5,4},{7,6},{8,9},{10,11},{9,8... | collective-permute-start | bytes 36872 | tf_op jit(solution)/shard_map/ppermute | solution.py:682
  44.2 8.6 %collective-permute-start.1 = (f32[3,1024]{1,0:T(4,128)S(1)}, f32[3,1024]{1,0:T(4,128)S(1)}, u32[]{:S(2)}, u32[]{:S(2)}) collective-permute-start(f32[3,1024]{1,0:T(4,128)S(1)} %get-tuple-element.32), channel_id=1, source_target_pairs={{1,2},{2,1},{5,6},{6,5},{9,10},{10,9},{13,14},{14,13},{17,18},{18,... | collective-permute-start | bytes 36872 | tf_op jit(solution)/shard_map/ppermute | solution.py:682
  49.0 7.2 %collective-permute-start.2 = (f32[3,1024]{1,0:T(4,128)S(1)}, f32[3,1024]{1,0:T(4,128)S(1)}, u32[]{:S(2)}, u32[]{:S(2)}) collective-permute-start(f32[3,1024]{1,0:T(4,128)S(1)} %get-tuple-element.33), channel_id=1, source_target_pairs={{4,8},{12,16},{20,24},{28,32},{36,40},{44,48},{52,56},{60,64},{68,... | collective-permute-start | bytes 36872 | tf_op jit(solution)/shard_map/ppermute | solution.py:682
  52.7 3.4 %collective-permute-start.3 = (f32[3,1024]{1,0:T(4,128)S(1)}, f32[3,1024]{1,0:T(4,128)S(1)}, u32[]{:S(2)}, u32[]{:S(2)}) collective-permute-start(f32[3,1024]{1,0:T(4,128)S(1)} %get-tuple-element.34), channel_id=1, source_target_pairs={{0,4},{4,0},{1,5},{5,1},{2,6},{6,2},{3,7},{7,3},{8,12},{12,8},{9,1... | collective-permute-start | bytes 36872 | tf_op jit(solution)/shard_map/ppermute | solution.py:682
